TPU v7x, 32 devices: a whole 2x2x4 slice. The times are simulated.
32 devices in a mesh: dp: 4 (over y, x), fsdp: 8 (over z, core).
Axes of the slice: x: 2, y: 2, z: 4, core: 2. Of those that a mesh axis runs over, the one named last changes fastest.
Arguments:
- byte_ids: int32 [2, 32, 1152], P(None, ('dp', 'fsdp')), may hold values from 0 to 255
- layouts: int32 [2, 32], P(None, ('dp', 'fsdp')), may hold values from 0 to 1
- weights: float32 [9728, 512], P(('dp', 'fsdp'))
- vectors: float32 [6, 512], P(None, ('dp', 'fsdp'))
- m_weights: float32 [9728, 512], P(('dp', 'fsdp')), may hold values from -0.002 to 0.002
- v_weights: float32 [9728, 512], P(('dp', 'fsdp')), may hold values from 2e-08 to 4e-07
- m_vectors: float32 [6, 512], P(None, ('dp', 'fsdp')), may hold values from -0.002 to 0.002
- v_vectors: float32 [6, 512], P(None, ('dp', 'fsdp')), may hold values from 2e-08 to 4e-07
Outputs:
- loss: float32 [], replicated
- grad_norm: float32 [], replicated
- m_weights_new: float32 [9728, 512], P(('dp', 'fsdp'))
- v_weights_new: float32 [9728, 512], P(('dp', 'fsdp'))
- weights_update: float32 [9728, 512], P(('dp', 'fsdp'))
- m_vectors_new: float32 [6, 512], P(None, ('dp', 'fsdp'))
- v_vectors_new: float32 [6, 512], P(None, ('dp', 'fsdp'))
- vectors_update: float32 [6, 512], P(None, ('dp', 'fsdp'))
All inputs are finite; a program needn't handle non-finite values.
Results may differ from a plain program's by a relative error of at most 0.0052.
The roundings to bfloat16 on the way count: a program that leaves them out, or rounds other values in their place, can miss the bound.
Values may be sent and summed in bfloat16 or wider, within the bound.
No kernel may reach another device: no remote copies, remote signals or barrier semaphores. Data moves between devices by JAX's collectives and lax.ppermute only.
A program may use at most 192 MiB of HBM per device.

v0:
```python
from functools import partial

import jax
import jax.numpy as jnp
from jax import lax
from jax.sharding import PartitionSpec as P

D = 512
HEADS = 8
HEAD = 64
FF = 2048
VOCAB = 256
POOL = 3


EPS_NORM = 1e-05
EPS_ADAM = 1e-08
CLIP = 0.2
RATE = 0.03
DECAY = 0.1
BETA = 0.5
STEP = 3
NEGATIVE = -1000000000.0


def product(left, right):
    return jnp.dot(left, right, preferred_element_type=jnp.float32)


def product_tn(left, right):
    return lax.dot_general(
        left, right, (((0,), (0,)), ((), ())), preferred_element_type=jnp.float32
    )


def product_nt(left, right):
    return lax.dot_general(
        left, right, (((1,), (1,)), ((), ())), preferred_element_type=jnp.float32
    )


def layer_norm(values, gain, offset):
    center = values - jnp.mean(values, -1, keepdims=True)
    spread = jnp.mean(center * center, -1, keepdims=True)
    return center * lax.rsqrt(spread + EPS_NORM) * gain + offset


def blocks(stacked):
    widths = [VOCAB, POOL * D, 3 * D, D, FF, FF, POOL * D, VOCAB]
    pieces = []
    offset = 0
    for width in widths:
        pieces.append(stacked[offset : offset + width])
        offset = offset + width
    return pieces


def row_bounds(layout, length):
    places = jnp.arange(length, dtype=jnp.int32)
    half = length // 2
    split = layout == 1
    first = jnp.where(split & (places >= half), half, 0).astype(jnp.int32)
    last = jnp.where(split & (places < half), half, length).astype(jnp.int32)
    return (places, first, last)


def attention_bias(layout, short_len):
    places = jnp.arange(short_len, dtype=jnp.int32)
    segment = ((layout == 1) & (places >= short_len // 2)).astype(jnp.int32)
    allowed = (places[None, :] <= places[:, None]) & (segment[None, :] == segment[:, None])
    slopes = 2.0 ** (-8.0 * (jnp.arange(HEADS, dtype=jnp.float32) + 1.0) / HEADS)
    distance = (places[:, None] - places[None, :]).astype(jnp.float32)
    return jnp.where(allowed[None], -slopes[:, None, None] * distance[None], NEGATIVE)


def to_heads(matrix):
    return matrix.reshape(matrix.shape[0], HEADS, HEAD).transpose(1, 0, 2)


def from_heads(tensor):
    return tensor.transpose(1, 0, 2).reshape(tensor.shape[1], HEADS * HEAD)


def forward(gathered, byte_ids, layout, count):
    stacked, vec_low = gathered
    vecs = vec_low.astype(jnp.float32)
    embed_table, pool_w, qkv_w, out_w, ffn_in, ffn_out, up_w, head_w = blocks(stacked)
    length = byte_ids.shape[0]
    short_len = length // POOL
    places, first, last = row_bounds(layout, length)
    vocab_ids = jnp.arange(VOCAB, dtype=jnp.int32)
    one_hot = (byte_ids[:, None] == vocab_ids[None, :]).astype(jnp.bfloat16)
    embed = product(one_hot, embed_table)
    keep_shift = (places - 2 >= first)[:, None]
    shifted = jnp.concatenate([jnp.zeros((2, D), jnp.float32), embed[:-2]], 0)
    shifted = jnp.where(keep_shift, shifted, 0.0).astype(jnp.bfloat16).reshape(short_len, POOL * D)
    short = product(shifted, pool_w)
    normed = layer_norm(short, vecs[0], vecs[1]).astype(jnp.bfloat16)
    qkv = product_nt(normed, qkv_w).astype(jnp.bfloat16)
    queries = to_heads(qkv[:, :D])
    key_rows = to_heads(qkv[:, D : 2 * D])
    val_rows = to_heads(qkv[:, 2 * D :])
    bias = attention_bias(layout, short_len)
    scores = (
        jnp.einsum("hqd,hkd->hqk", queries, key_rows, preferred_element_type=jnp.float32) * 0.125
        + bias
    )
    top = jnp.max(scores, -1, keepdims=True)
    expo = jnp.exp(scores - top)
    summed = jnp.sum(expo, -1, keepdims=True)
    probs = expo / summed
    log_total = top + jnp.log(summed)
    mixed = jnp.einsum(
        "hqk,hkd->hqd", probs.astype(jnp.bfloat16), val_rows, preferred_element_type=jnp.float32
    )
    mixed = from_heads(mixed).astype(jnp.bfloat16)
    resid = short + product(mixed, out_w)
    normed2 = layer_norm(resid, vecs[2], vecs[3]).astype(jnp.bfloat16)
    hidden = product_nt(normed2, ffn_in)
    active = jax.nn.gelu(hidden, approximate=False).astype(jnp.bfloat16)
    deep = (resid + product(active, ffn_out)).astype(jnp.bfloat16)
    upward = product_nt(deep, up_w).reshape(length, D)
    joined = embed + upward
    final = layer_norm(joined, vecs[4], vecs[5]).astype(jnp.bfloat16)
    logits = product_nt(final, head_w)
    nexts = jnp.concatenate([byte_ids[1:], byte_ids[:1]])
    valid = (places + 1 < last).astype(jnp.float32)
    target = (nexts[:, None] == vocab_ids[None, :]).astype(jnp.float32)
    peak = jnp.max(logits, -1, keepdims=True)
    shifted_exp = jnp.exp(logits - peak)
    denom = jnp.sum(shifted_exp, -1, keepdims=True)
    lse_rows = peak[:, 0] + jnp.log(denom[:, 0])
    part_loss = jnp.sum(valid * (lse_rows - jnp.sum(logits * target, -1))) / count
    dlogits = (valid[:, None] * (shifted_exp / denom - target) / count).astype(jnp.bfloat16)
    kept = {
        "byte_ids": byte_ids,
        "keep_shift": keep_shift,
        "shifted": shifted,
        "short": short,
        "normed": normed,
        "queries": queries,
        "key_rows": key_rows,
        "val_rows": val_rows,
        "layout": layout,
        "log_total": log_total,
        "mixed": mixed,
        "resid": resid,
        "normed2": normed2,
        "hidden": hidden,
        "active": active,
        "deep": deep,
        "joined": joined,
        "final": final,
        "dlogits": dlogits,
    }
    return (part_loss, kept)


def backward(gathered, kept):
    stacked, vec_low = gathered
    vecs = vec_low.astype(jnp.float32)
    embed_table, pool_w, qkv_w, out_w, ffn_in, ffn_out, up_w, head_w = blocks(stacked)
    length = kept["byte_ids"].shape[0]
    short_len = length // POOL
    dlogits = kept["dlogits"]
    grad_head = product_tn(dlogits, kept["final"])
    dfinal = product(dlogits, head_w)
    _, pull_final = jax.vjp(layer_norm, kept["joined"], vecs[4], vecs[5])
    djoined, dgain_f, dbias_f = pull_final(dfinal)
    dupward = djoined.reshape(short_len, POOL * D).astype(jnp.bfloat16)
    grad_up = product_tn(dupward, kept["deep"])
    ddeep = product(dupward, up_w)
    dbranch2 = ddeep.astype(jnp.bfloat16)
    grad_fout = product_tn(kept["active"], dbranch2)
    dactive = product_nt(dbranch2, ffn_out)
    _, pull_gelu = jax.vjp(partial(jax.nn.gelu, approximate=False), kept["hidden"])
    dhidden = pull_gelu(dactive)[0].astype(jnp.bfloat16)
    grad_fin = product_tn(dhidden, kept["normed2"])
    dnormed2 = product(dhidden, ffn_in)
    _, pull_second = jax.vjp(layer_norm, kept["resid"], vecs[2], vecs[3])
    dresid_norm, dgain_2, dbias_2 = pull_second(dnormed2)
    dresid = ddeep + dresid_norm
    dbranch = dresid.astype(jnp.bfloat16)
    grad_out = product_tn(kept["mixed"], dbranch)
    dmixed = to_heads(product_nt(dbranch, out_w).astype(jnp.bfloat16))
    queries = kept["queries"]
    key_rows = kept["key_rows"]
    bias = attention_bias(kept["layout"], short_len)
    scores = (
        jnp.einsum("hqd,hkd->hqk", queries, key_rows, preferred_element_type=jnp.float32) * 0.125
        + bias
    )
    probs = jnp.exp(scores - kept["log_total"])
    dprobs = jnp.einsum(
        "hqd,hkd->hqk", dmixed, kept["val_rows"], preferred_element_type=jnp.float32
    )
    delta = jnp.sum(dprobs * probs, -1, keepdims=True)
    dscores = (probs * (dprobs - delta) * 0.125).astype(jnp.bfloat16)
    dqueries = jnp.einsum("hqk,hkd->hqd", dscores, key_rows, preferred_element_type=jnp.float32)
    dkeys = jnp.einsum("hqk,hqd->hkd", dscores, queries, preferred_element_type=jnp.float32)
    dvalues = jnp.einsum(
        "hqk,hqd->hkd", probs.astype(jnp.bfloat16), dmixed, preferred_element_type=jnp.float32
    )
    dqkv = jnp.concatenate(
        [from_heads(dqueries), from_heads(dkeys), from_heads(dvalues)], 1
    ).astype(jnp.bfloat16)
    grad_qkv = product_tn(dqkv, kept["normed"])
    dnormed = product(dqkv, qkv_w)
    _, pull_first = jax.vjp(layer_norm, kept["short"], vecs[0], vecs[1])
    dshort_norm, dgain_1, dbias_1 = pull_first(dnormed)
    dshort = (dresid + dshort_norm).astype(jnp.bfloat16)
    grad_pool = product_tn(kept["shifted"], dshort)
    dshifted = product_nt(dshort, pool_w).reshape(length, D)
    dshifted = jnp.where(kept["keep_shift"], dshifted, 0.0)
    dembed = djoined + jnp.concatenate([dshifted[2:], jnp.zeros((2, D), jnp.float32)], 0)
    vocab_ids = jnp.arange(VOCAB, dtype=jnp.int32)
    one_hot = (kept["byte_ids"][:, None] == vocab_ids[None, :]).astype(jnp.float32)
    grad_embed = lax.dot_general(
        one_hot,
        dembed,
        (((0,), (0,)), ((), ())),
        precision=lax.Precision.HIGHEST,
        preferred_element_type=jnp.float32,
    )
    grad_stack = jnp.concatenate(
        [grad_embed, grad_pool, grad_qkv, grad_out, grad_fin, grad_fout, grad_up, grad_head], 0
    )
    grad_vecs = jnp.stack([dgain_1, dbias_1, dgain_2, dbias_2, dgain_f, dbias_f], 0)
    return (grad_stack, grad_vecs)


def adam(param, first_m, second_m, grad, decay):
    first_new = BETA * first_m + (1.0 - BETA) * grad
    second_new = BETA * second_m + (1.0 - BETA) * grad * grad
    correct = 1.0 - BETA**STEP
    update = -RATE * (
        first_new / correct / (jnp.sqrt(second_new / correct) + EPS_ADAM) + decay * param
    )
    return (first_new, second_new, update)


def shards(byte_ids, layouts, weights, vectors, m_weights, v_weights, m_vectors, v_vectors):
    devices = lax.axis_size(("dp", "fsdp"))
    micro = byte_ids.shape[0]
    count = float(micro * layouts.shape[1] * devices * byte_ids.shape[2])
    weights_low = weights.astype(jnp.bfloat16)
    vectors_low = vectors.astype(jnp.bfloat16)
    grad_stack = jnp.zeros((weights.shape[0] * devices, D), jnp.float32)
    grad_vecs = jnp.zeros((6, vectors.shape[1] * devices), jnp.float32)
    loss_local = jnp.zeros((), jnp.float32)
    for index in range(micro):
        forward_set = (
            lax.all_gather(weights_low, ("dp", "fsdp"), axis=0, tiled=True),
            lax.all_gather(vectors_low, ("dp", "fsdp"), axis=1, tiled=True),
        )
        part_loss, kept = forward(forward_set, byte_ids[index, 0], layouts[index, 0], count)
        backward_set = (
            lax.all_gather(weights_low, ("dp", "fsdp"), axis=0, tiled=True),
            lax.all_gather(vectors_low, ("dp", "fsdp"), axis=1, tiled=True),
        )
        step_stack, step_vecs = backward(backward_set, kept)
        grad_stack = grad_stack + step_stack
        grad_vecs = grad_vecs + step_vecs
        loss_local = loss_local + part_loss
    owned_stack, owned_vecs = (
        lax.psum_scatter(grad_stack, ("dp", "fsdp"), scatter_dimension=0, tiled=True),
        lax.psum_scatter(grad_vecs, ("dp", "fsdp"), scatter_dimension=1, tiled=True),
    )
    squares = jnp.sum(owned_stack * owned_stack) + jnp.sum(owned_vecs * owned_vecs)
    total_squares, loss = lax.psum((squares, loss_local), ("dp", "fsdp"))
    grad_norm = jnp.sqrt(total_squares)
    factor = CLIP / jnp.maximum(grad_norm, CLIP)
    first_w, second_w, update_w = adam(weights, m_weights, v_weights, owned_stack * factor, DECAY)
    first_v, second_v, update_v = adam(vectors, m_vectors, v_vectors, owned_vecs * factor, 0.0)
    return (loss, grad_norm, first_w, second_w, update_w, first_v, second_v, update_v)


def solution(mesh):
    in_specs = (
        P(None, ("dp", "fsdp"), None),
        P(None, ("dp", "fsdp")),
        P(("dp", "fsdp"), None),
        P(None, ("dp", "fsdp")),
        P(("dp", "fsdp"), None),
        P(("dp", "fsdp"), None),
        P(None, ("dp", "fsdp")),
        P(None, ("dp", "fsdp")),
    )
    out_specs = (
        P(),
        P(),
        P(("dp", "fsdp"), None),
        P(("dp", "fsdp"), None),
        P(("dp", "fsdp"), None),
        P(None, ("dp", "fsdp")),
        P(None, ("dp", "fsdp")),
        P(None, ("dp", "fsdp")),
    )
    return jax.shard_map(shards, mesh=mesh, in_specs=in_specs, out_specs=out_specs, check_vma=False)
```

profile of v0, /device:TPU:0, one launch (start us, length us, event | category | flops | bytes accessed | tf_op | source)
XLA Modules:
  0.0 722.7 jit_solution(9651001540598982905)
XLA Ops:
  13.8 43.8 %all-gather = bf16[32,16,6]{1,2,0:T(8,128)(2,1)S(1)} all-gather(bf16[1,16,6]{1,2,0:T(8,128)(2,1)S(1)} %convert_bitcast_fusion), channel_id=1, replica_groups=mesh['dp'=4,'fsdp'=8] {'dp','fsdp'}, dimensions={0}, use_global_device_ids=true | all-gather | bytes 6336 | tf_op jit(solution)/shard_map/all_gather | solution.py:254
  67.4 31.1 %all-gather.3.cloned.1.call-done = bf16[9728,512]{1,0:T(8,128)(2,1)} async-done(((bf16[304,512]{1,0:T(8,128)(2,1)}), bf16[9728,512]{1,0:T(8,128)(2,1)}) %all-gather.3.cloned.1.call-update) | async-done | bytes 9961488 | tf_op jit(solution)/shard_map/all_gather | solution.py:253
  103.5 2.7 fusion.233
  116.4 2.7 fusion.236
  123.2 2.9 fusion.237
  138.4 9.8 %multiply_convert_fusion.2 = (bf16[384,2048]{1,0:T(8,128)(2,1)S(1)}, f32[384,2048]{1,0:T(8,128)}, f32[384,2048]{1,0:T(8,128)}) fusion(bf16[9728,512]{1,0:T(8,128)(2,1)S(1)} %bitcast.128, f32[384,512]{1,0:T(8,128)S(1)} %get-tuple-element.97, f32[384]{0:T(512)S(1)} %fusion.201, f32[384]{0:T(512)S(1)} %broadcast_multiply_fusion.2, f32[512]{0:T(512)S(1)} %bitcast.166, ...), kind=kOutput, calls=%fused_computation.40 | convolution fusion | flops 857407488 | bytes 10756096 | tf_op jit(solution)/shard_map/dot_general | solution.py:37
  152.4 3.3 reshape.489
  155.7 3.0 copy.107
  158.7 10.3 %multiply_convert_fusion.3 = (bf16[384,2048]{1,0:T(8,128)(2,1)S(1)}, f32[384,2048]{1,0:T(8,128)}, f32[384,2048]{1,0:T(8,128)}) fusion(bf16[9728,512]{1,0:T(8,128)(2,1)} %all-gather.3.cloned.1.call-done, f32[384,512]{1,0:T(8,128)S(1)} %get-tuple-element.104, f32[512]{0:T(512)S(1)} %bitcast.167, f32[512]{0:T(512)S(1)} %bitcast.158, f32[384]{0:T(512)S(1)} %copy-done.120, ...), kind=kOutput, calls=%fused_computation.53 | convolution fusion | flops 857407488 | bytes 10755072 | tf_op jit(solution)/shard_map/dot_general | solution.py:37
  169.1 3.1 fusion.101
  173.0 3.6 fusion.138
  181.2 4.3 fusion.224
  190.9 3.6 fusion.241
  194.5 3.1 copy.108
  200.5 3.6 fusion.242
  204.1 3.0 copy.115
  207.2 5.0 multiply_reduce_fusion.2
  220.1 3.0 convert_element_type.232
  226.7 3.2 convert_element_type.244
  229.9 2.7 fusion.134
  232.6 5.4 add_convert_fusion.1
  250.5 4.0 fusion.244
  254.4 4.1 fusion.121
  258.5 9.4 %fusion.104 = bf16[8,384,64]{1,2,0:T(8,128)(2,1)} fusion(bf16[8,384,64]{1,2,0:T(8,128)(2,1)} %bitcast.148, f32[8,384,384]{1,2,0:T(8,128)} %fusion.244, f32[8,384,384]{1,2,0:T(8,128)} %copy-done.8, f32[8,384]{1,0:T(8,128)} %log_add_fusion), kind=kOutput, calls=%fused_computation.136 | convolution fusion | flops 159452544 | bytes 10235904 | tf_op jit(solution)/shard_map/hqk,hkd->hqd/dot_general | solution.py:199
  267.9 9.7 %fusion.107 = bf16[8,384,64]{1,2,0:T(8,128)(2,1)} fusion(bf16[8,384,64]{1,2,0:T(8,128)(2,1)S(1)} %bitcast.151, f32[8,384,384]{1,2,0:T(8,128)} %fusion.244, f32[8,384,384]{1,2,0:T(8,128)} %copy-done.8, f32[8,384]{1,0:T(8,128)} %log_add_fusion), kind=kOutput, calls=%fused_computation.137 | convolution fusion | flops 159452544 | bytes 10235904 | tf_op jit(solution)/shard_map/hqk,hqd->hkd/dot_general | solution.py:200
  284.1 3.9 fusion.243
  288.1 4.1 fusion.118
  292.1 9.5 %fusion.110 = bf16[8,384,64]{1,2,0:T(8,128)(2,1)} fusion(bf16[8,384,64]{1,2,0:T(8,128)(2,1)} %bitcast.153, f32[8,384,384]{1,2,0:T(8,128)} %fusion.243, f32[8,384,384]{1,2,0:T(8,128)} %copy-done.7, f32[8,384]{1,0:T(8,128)} %log_add_fusion.1), kind=kOutput, calls=%fused_computation.138 | convolution fusion | flops 159452544 | bytes 10235904 | tf_op jit(solution)/shard_map/hqk,hkd->hqd/dot_general | solution.py:199
  301.6 9.5 %fusion.113 = bf16[8,384,64]{1,2,0:T(8,128)(2,1)} fusion(bf16[8,384,64]{1,2,0:T(8,128)(2,1)} %bitcast.155, f32[8,384,384]{1,2,0:T(8,128)} %fusion.243, f32[8,384,384]{1,2,0:T(8,128)} %copy-done.7, f32[8,384]{1,0:T(8,128)} %log_add_fusion.1), kind=kOutput, calls=%fused_computation.139 | convolution fusion | flops 159452544 | bytes 10235904 | tf_op jit(solution)/shard_map/hqk,hqd->hkd/dot_general | solution.py:200
  321.7 3.6 fusion.146
  325.3 3.3 reshape.499
  328.6 3.3 slice.207
  332.0 3.1 copy.135
  337.3 3.6 fusion.148
  340.9 3.3 reshape.494
  344.2 3.4 slice.205
  347.6 3.2 copy.134
  365.7 2.7 fusion.89
  368.5 2.7 convolution_dynamic-update-slice_fusion.4
  371.3 2.8 convolution_dynamic-update-slice_fusion.3
  375.5 3.7 convolution_dynamic-update-slice_fusion.2
  379.2 3.3 convolution_dynamic-update-slice_fusion.1
  382.5 2.7 convolution_dynamic-update-slice_fusion
  386.7 17.0 %add.310 = f32[9728,512]{1,0:T(8,128)} add(f32[9728,512]{1,0:T(8,128)S(1)} %convolution_dynamic-update-slice_fusion.13, f32[9728,512]{1,0:T(8,128)} %convolution_dynamic-update-slice_fusion.12) | non-fusion elementwise | flops 4980736 | bytes 59768832 | tf_op jit(solution)/shard_map/add | solution.py:262
  406.8 46.1 %reduce-scatter.7.cloned.1.call-done = f32[16,6]{1,0:T(8,128)} async-done(((f32[512,6]{1,0:T(8,128)}), f32[16,6]{1,0:T(8,128)}) %reduce-scatter.7.cloned.1.call-update) | async-done | bytes 400
  454.4 216.4 %reduce-scatter.5.cloned.1.call-done = f32[304,512]{1,0:T(8,128)} async-done(((f32[9728,512]{1,0:T(8,128)}), f32[304,512]{1,0:T(8,128)}) %reduce-scatter.5.cloned.1.call-update) | async-done | bytes 622608 | tf_op jit(solution)/shard_map/reduce_scatter | solution.py:266
  673.9 36.9 %all-reduce.4 = (f32[]{:T(128)}, f32[]{:T(128)}) all-reduce(f32[]{:T(128)S(6)} %multiply.147, f32[]{:T(128)S(6)} %add.312), channel_id=1, replica_groups=mesh['dp'=4,'fsdp'=8] {'dp','fsdp'}, use_global_device_ids=true, to_apply=%region_24.25 | all-reduce | flops 2 | bytes 16 | tf_op jit(solution)/shard_map/psum | solution.py:270
  712.2 2.7 add_multiply_fusion
  (480 shorter events, 129.9 us)
Async XLA Ops:
  7.2 91.3 %all-gather.3.cloned.1.call-start = ((), (), s32[]{:S(2)}) async-start(), calls=%async_computation.2 | async-start | bytes 10272768 | tf_op jit(solution)/shard_map/all_gather | solution.py:253
  9.1 443.9 %reduce-scatter.7.cloned.1.call-start = ((), (), s32[]{:S(2)}) async-start(), calls=%async_computation.4 | async-start | bytes 270336
  63.5 127.4 %copy-start.95 = (s32[1152]{0:T(1024)}, s32[1152]{0:T(1024)S(1)}, u32[]{:S(2)}) copy-start(s32[1152]{0:T(1024)S(1)} %get-tuple-element.118) | copy-start | bytes 13828
  64.3 35.8 %copy-start.76 = (s32[1152]{0:T(1024)}, s32[1152]{0:T(1024)S(1)}, u32[]{:S(2)}) copy-start(s32[1152]{0:T(1024)S(1)} %get-tuple-element.30) | copy-start | bytes 13828
  64.3 46.7 %copy-start.78 = (s32[1152]{0:T(1024)}, s32[1152]{0:T(1024)S(1)}, u32[]{:S(2)}) copy-start(s32[1152]{0:T(1024)S(1)} %get-tuple-element.31) | copy-start | bytes 13828
  65.8 40.7 %copy-start.127 = (f32[1,512]{1,0:T(1,128)}, f32[1,512]{1,0:T(1,128)S(1)}, u32[]{:S(2)}) copy-start(f32[1,512]{1,0:T(1,128)S(1)} %get-tuple-element.71) | copy-start | bytes 6148
  65.8 40.8 %copy-start.151 = (f32[1,512]{1,0:T(1,128)}, f32[1,512]{1,0:T(1,128)S(1)}, u32[]{:S(2)}) copy-start(f32[1,512]{1,0:T(1,128)S(1)} %get-tuple-element.70) | copy-start | bytes 6148
  65.8 92.9 %copy-start.102 = (f32[1,512]{1,0:T(1,128)}, f32[1,512]{1,0:T(1,128)S(1)}, u32[]{:S(2)}) copy-start(f32[1,512]{1,0:T(1,128)S(1)} %get-tuple-element.69) | copy-start | bytes 6148
  106.2 31.4 %copy-start.26 = (f32[384,512]{1,0:T(8,128)}, f32[384,512]{1,0:T(8,128)S(1)}, u32[]{:S(2)}) copy-start(f32[384,512]{1,0:T(8,128)S(1)} %get-tuple-element.93) | copy-start | bytes 2359300
  110.1 26.5 %copy-start.62 = (bf16[384,512]{0,1:T(8,128)(2,1)}, bf16[384,512]{0,1:T(8,128)(2,1)S(1)}, u32[]{:S(2)}) copy-start(bf16[384,512]{0,1:T(8,128)(2,1)S(1)} %copy.105) | copy-start | bytes 1179652
  119.0 9.5 %copy-start.29 = (f32[384,512]{1,0:T(8,128)}, f32[384,512]{1,0:T(8,128)S(1)}, u32[]{:S(2)}) copy-start(f32[384,512]{1,0:T(8,128)S(1)} %get-tuple-element.100) | copy-start | bytes 2359300
  127.3 4.4 slice-start.2
  128.5 6.3 copy-start.60
  128.5 4.7 copy-start.66
  128.5 4.7 copy-start.71
  128.5 4.7 copy-start.72
  128.5 4.7 copy-start.75
  128.5 4.7 copy-start.160
  132.3 36.8 %copy-start.15 = (f32[384,512]{1,0:T(8,128)}, f32[384,512]{1,0:T(8,128)S(1)}, u32[]{:S(2)}) copy-start(f32[384,512]{1,0:T(8,128)S(1)} %get-tuple-element.104) | copy-start | bytes 2359300
  132.3 26.4 %copy-start.99 = (f32[384]{0:T(512)}, f32[384]{0:T(512)S(1)}, u32[]{:S(2)}) copy-start(f32[384]{0:T(512)S(1)} %broadcast_multiply_fusion.4) | copy-start | bytes 4612
  138.1 107.8 %copy-start.13 = (f32[384,512]{1,0:T(8,128)}, f32[384,512]{1,0:T(8,128)S(1)}, u32[]{:S(2)}) copy-start(f32[384,512]{1,0:T(8,128)S(1)} %get-tuple-element.97) | copy-start | bytes 2359300
  138.1 107.8 %copy-start.97 = (f32[384]{0:T(512)}, f32[384]{0:T(512)S(1)}, u32[]{:S(2)}) copy-start(f32[384]{0:T(512)S(1)} %broadcast_multiply_fusion.2) | copy-start | bytes 4612
  138.4 107.6 %copy-start.118 = (f32[384]{0:T(512)}, f32[384]{0:T(512)S(1)}, u32[]{:S(2)}) copy-start(f32[384]{0:T(512)S(1)} %fusion.201) | copy-start | bytes 4612
  188.2 6.3 copy-start.37
  189.9 4.6 copy-start.34
  194.5 5.0 copy-start.93
  194.5 6.0 copy-start.139
  199.5 4.7 copy-start.32
  207.2 5.1 copy-start.1
  207.2 5.1 copy-start.5
  207.2 5.2 copy-start.6
  214.9 8.2 %copy-start.80 = (f32[1152]{0:T(1024)}, f32[1152]{0:T(1024)S(1)}, u32[]{:S(2)}) copy-start(f32[1152]{0:T(1024)S(1)} %negate_multiply_fusion.2) | copy-start | bytes 13828
  215.0 8.1 %copy-start.82 = (f32[1152]{0:T(1024)}, f32[1152]{0:T(1024)S(1)}, u32[]{:S(2)}) copy-start(f32[1152]{0:T(1024)S(1)} %negate_multiply_fusion.3) | copy-start | bytes 13828
  217.5 5.6 copy-start.2
  229.9 8.2 %slice-start.3 = ((s8[9961472]{0:T(1024)(128)(4,1)}), s8[4194304]{0:T(1024)(128)(4,1)S(1)}, s32[]{:S(2)}) async-start(s8[9961472]{0:T(1024)(128)(4,1)} %bitcast.129), calls=%async_computation.8 | async-start | bytes 8388608
  232.6 5.5 copy-start.51
  232.6 5.5 slice-start.4
  232.6 5.5 slice-start.5
  240.7 7.2 copy-start.49
  258.5 9.4 %copy-start.73 = (bf16[384,512]{0,1:T(8,128)(2,1)S(1)}, bf16[384,512]{0,1:T(8,128)(2,1)}, u32[]{:S(2)}) copy-start(bf16[384,512]{0,1:T(8,128)(2,1)} %copy.103) | copy-start | bytes 1179652
  301.6 9.6 %copy-start.69 = (bf16[8,384,64]{1,2,0:T(8,128)(2,1)S(1)}, bf16[8,384,64]{1,2,0:T(8,128)(2,1)}, u32[]{:S(2)}) copy-start(bf16[8,384,64]{1,2,0:T(8,128)(2,1)} %fusion.118) | copy-start | bytes 1179652
  320.4 350.4 %reduce-scatter.5.cloned.1.call-start = ((), (), s32[]{:S(2)}) async-start(), calls=%async_computation.3 | async-start | bytes 20545536 | tf_op jit(solution)/shard_map/reduce_scatter | solution.py:266
  403.6 307.9 %copy-start.124 = (f32[6,16]{1,0:T(8,128)S(1)}, f32[6,16]{1,0:T(8,128)}, u32[]{:S(2)}) copy-start(f32[6,16]{1,0:T(8,128)} %param.11) | copy-start | bytes 1156
  403.6 307.9 %copy-start.143 = (f32[6,16]{1,0:T(8,128)S(1)}, f32[6,16]{1,0:T(8,128)}, u32[]{:S(2)}) copy-start(f32[6,16]{1,0:T(8,128)} %param.15) | copy-start | bytes 1156
  403.6 307.9 %copy-start.144 = (f32[6,16]{1,0:T(8,128)S(1)}, f32[6,16]{1,0:T(8,128)}, u32[]{:S(2)}) copy-start(f32[6,16]{1,0:T(8,128)} %param.14) | copy-start | bytes 1156
  403.7 308.5 %copy-start.53 = (f32[304,512]{1,0:T(8,128)S(1)}, f32[304,512]{1,0:T(8,128)}, u32[]{:S(2)}) copy-start(f32[304,512]{1,0:T(8,128)} %param.10) | copy-start | bytes 1867780
  403.7 308.5 %copy-start.64 = (f32[304,512]{1,0:T(8,128)S(1)}, f32[304,512]{1,0:T(8,128)}, u32[]{:S(2)}) copy-start(f32[304,512]{1,0:T(8,128)} %param.13) | copy-start | bytes 1867780
  403.7 308.5 %copy-start.65 = (f32[304,512]{1,0:T(8,128)S(1)}, f32[304,512]{1,0:T(8,128)}, u32[]{:S(2)}) copy-start(f32[304,512]{1,0:T(8,128)} %param.12) | copy-start | bytes 1867780
  (124 other events, 281.9 us)
Sparse Core Ops, SparseCore 0:
  11.4 86.9 all-gather.2
  320.5 132.4 reduce-scatter.6
  455.4 215.2 reduce-scatter.4
where the time goes:
time: 732 us; the launch traced here: 723 us
  waiting for transfers between devices  294 us (40%)
  matrix products  174 us (24%)
  local copies, waits for them, and re-layouts  83.2 us (11%)
  blocking collectives  80.7 us (11%)
  other arithmetic  69.1 us (9%)
  between operations  21.7 us (3%)
    reduce_scatter x1, waiting for transfers between devices, shards(): lax.psum_scatter(grad_stack, ('dp', 'fsdp'), scatter_dimension=0, tiled=T...  216 us
    dot_general x14, matrix products, product_nt(): lax.dot_general(left, right, (((1,), (1,)), ((), ())), preferred_element_...  51.7 us
    unnamed x4, waiting for transfers between devices  46.2 us
    all_gather x1, blocking collectives, shards(): lax.all_gather(vectors_low, ('dp', 'fsdp'), axis=1, tiled=True)  43.8 us
    psum x1, blocking collectives, shards(): total_squares, loss = lax.psum((squares, loss_local), ('dp', 'fsdp'))  36.9 us
    dot_general x16, matrix products, product(): return jnp.dot(left, right, preferred_element_type=jnp.float32)  32.5 us
    all_gather x1, waiting for transfers between devices, shards(): lax.all_gather(weights_low, ('dp', 'fsdp'), axis=0, tiled=True)  31.1 us
    unnamed x342, local copies, waits for them, and re-layouts  26.4 us
  transfers between devices with their start and end apart: 3, of which 3 were waited for; matrix products, arithmetic and copies ran while one was open for 13% of the time, Pallas kernels for 0%

commit v1 on v0

v1 whole, which is shorter than its diff:
```python
from functools import partial

import jax
import jax.numpy as jnp
from jax import lax
from jax.experimental import pallas as pl
from jax.experimental.pallas import tpu as pltpu
from jax.sharding import PartitionSpec as P

D = 512
HEADS = 8
HEAD = 64
FF = 2048
VOCAB = 256
POOL = 3

EPS_NORM = 1e-05
EPS_ADAM = 1e-08
CLIP = 0.2
RATE = 0.03
DECAY = 0.1
BETA = 0.5
STEP = 3
NEGATIVE = -1000000000.0

F32 = jnp.float32
BF16 = jnp.bfloat16

ROW_E = 0
ROW_P = VOCAB
ROW_QKV = ROW_P + POOL * D
ROW_O = ROW_QKV + 3 * D
ROW_F1 = ROW_O + D
ROW_F2 = ROW_F1 + FF
ROW_U = ROW_F2 + FF
ROW_H = ROW_U + POOL * D
ROW_END = ROW_H + VOCAB

BLOCK = 256
AXES = ("dp", "fsdp")


def nn(left, right):
    return lax.dot_general(left, right, (((1,), (0,)), ((), ())), preferred_element_type=F32)


def nt(left, right):
    return lax.dot_general(left, right, (((1,), (1,)), ((), ())), preferred_element_type=F32)


def tn(left, right):
    return lax.dot_general(left, right, (((0,), (0,)), ((), ())), preferred_element_type=F32)


def norm_parts(values):
    center = values - jnp.mean(values, -1, keepdims=True)
    spread = jnp.mean(center * center, -1, keepdims=True)
    scale = lax.rsqrt(spread + EPS_NORM)
    return center * scale, scale


def norm_back(unit, scale, gain, grad):
    inner = grad * gain
    mean_inner = jnp.mean(inner, -1, keepdims=True)
    mean_cross = jnp.mean(inner * unit, -1, keepdims=True)
    return scale * (inner - mean_inner - unit * mean_cross)


def fold_rows(values):
    return jnp.sum(values.reshape(values.shape[0] // 8, 8, values.shape[1]), 0)


def one_hot_rows(ids):
    lanes = lax.broadcasted_iota(jnp.int32, (ids.shape[0], VOCAB), 1)
    return jnp.where(lanes == ids, 1.0, 0.0).astype(BF16)


def one_hot_cols(ids):
    lines = lax.broadcasted_iota(jnp.int32, (VOCAB, ids.shape[1]), 0)
    return jnp.where(lines == ids, 1.0, 0.0).astype(BF16)


def rows_of(index, size=BLOCK):
    return pl.ds(pl.multiple_of(index * size, size), size)


def attend_kernel(short_len, slots, lay_ref, slope_ref, cols_ref, vec_ref, w_hbm,
                  shifted_ref, short_ref, normed_ref, qkv_ref, lse_ref, mixed_ref, resid_ref,
                  w_ref, dist_ref, mask_ref, lse_cols, sems):
    rows = short_len * slots
    bounds = (ROW_E, ROW_QKV, ROW_O, ROW_F1)
    copies = [
        pltpu.make_async_copy(w_hbm.at[pl.ds(low, high - low)], w_ref.at[pl.ds(low, high - low)], sems.at[k])
        for k, (low, high) in enumerate(zip(bounds[:-1], bounds[1:]))
    ]
    for copy in copies:
        copy.start()
    copies[0].wait()
    gain, offset = vec_ref[0:1, :], vec_ref[1:2, :]

    def pool_step(block, carry):
        at = rows_of(block)
        for j in range(POOL):
            hot = one_hot_rows(cols_ref[at, POOL + j : POOL + j + 1])
            shifted_ref[at, j * D : (j + 1) * D] = nn(hot, w_ref[ROW_E:ROW_P, :]).astype(BF16)
        short = nn(shifted_ref[at, :], w_ref[ROW_P:ROW_QKV, :])
        short_ref[at, :] = short
        unit, _ = norm_parts(short)
        normed_ref[at, :] = (unit * gain + offset).astype(BF16)
        return carry

    lax.fori_loop(0, rows // BLOCK, pool_step, 0)
    copies[1].wait()

    def qkv_step(block, carry):
        at = rows_of(block)
        qkv_ref[at, :] = nt(normed_ref[at, :], w_ref[ROW_QKV:ROW_O, :]).astype(BF16)
        return carry

    lax.fori_loop(0, rows // BLOCK, qkv_step, 0)

    left_lanes = lax.broadcasted_iota(jnp.int32, (short_len, 2 * HEAD), 1) < HEAD
    tile = 128
    for slot in range(slots):
        at = pl.ds(slot * short_len, short_len)
        query = lax.broadcasted_iota(jnp.int32, (short_len, short_len), 0)
        key = lax.broadcasted_iota(jnp.int32, (short_len, short_len), 1)
        half = jnp.where(lay_ref[slot] == 1, short_len // 2, short_len)
        allowed = (key <= query) & ((key >= half) == (query >= half))
        dist_ref[...] = (key - query).astype(F32)
        mask_ref[...] = jnp.where(allowed, 0.0, NEGATIVE)

        def head_step(pair, carry):
            lanes = pl.ds(pl.multiple_of(pair * 2 * HEAD, 2 * HEAD), 2 * HEAD)
            lanes_k = pl.ds(pl.multiple_of(D + pair * 2 * HEAD, 2 * HEAD), 2 * HEAD)
            lanes_v = pl.ds(pl.multiple_of(2 * D + pair * 2 * HEAD, 2 * HEAD), 2 * HEAD)
            queries = qkv_ref[at, lanes] * jnp.asarray(0.125, BF16)
            keys = qkv_ref[at, lanes_k]
            values = qkv_ref[at, lanes_v]
            zero = jnp.zeros_like(values)
            vals = [jnp.where(left_lanes, values, zero), jnp.where(left_lanes, zero, values)]
            slots_q = [jnp.where(left_lanes, queries, zero), jnp.where(left_lanes, zero, queries)]
            for part in range(short_len // tile):
                low = part * tile
                mixed = jnp.zeros((tile, 2 * HEAD), F32)
                columns = lse_cols[low : low + tile, :]
                where = lax.broadcasted_iota(jnp.int32, (tile, 2 * HEAD), 1)
                for side in range(2):
                    head = pair * 2 + side
                    slope = slope_ref[head]
                    scores = nt(slots_q[side][low : low + tile], keys)
                    scores = scores + jnp.where(
                        mask_ref[low : low + tile, :] == 0.0, dist_ref[low : low + tile, :] * slope, NEGATIVE
                    )
                    top = jnp.max(scores, -1, keepdims=True)
                    expo = jnp.exp(scores - top)
                    total = jnp.sum(expo, -1, keepdims=True)
                    probs = (expo * (1.0 / total)).astype(BF16)
                    columns = jnp.where(where == head, top + jnp.log(total), columns)
                    mixed = mixed + nn(probs, vals[side])
                lse_cols[low : low + tile, :] = columns
                mixed_ref[pl.ds(slot * short_len + low, tile), lanes] = mixed.astype(BF16)
            return carry

        lse_cols[...] = jnp.zeros_like(lse_cols)
        lax.fori_loop(0, HEADS // 2, head_step, 0)
        turned = lse_cols[...].T
        for head in range(HEADS):
            lse_ref[slot, head] = turned[head : head + 1, :]

    copies[2].wait()

    def out_step(block, carry):
        at = rows_of(block)
        resid_ref[at, :] = short_ref[at, :] + nn(mixed_ref[at, :], w_ref[ROW_O:ROW_F1, :])
        return carry

    lax.fori_loop(0, rows // BLOCK, out_step, 0)


def gelu_parts(hidden):
    size = jnp.abs(hidden)
    near = 1.0 / (1.0 + (0.3275911 * 0.7071067811865476) * size)
    bell = jnp.exp(hidden * hidden * -0.5)
    tail = near * (0.127414796 + near * (-0.142248368 + near * (0.7107068705 + near * (-0.7265760135 + near * 0.5307027145))))
    tail = tail * bell
    cdf = jnp.where(hidden >= 0.0, 1.0 - tail, tail)
    return hidden * cdf, cdf + hidden * bell * 0.3989422804014327


def deep_kernel(count, cols_ref, lines_ref, vec_ref, resid_ref, w_hbm,
                grads_ref, table_ref, dresid_ref, small_ref,
                w_ref, normed_ref, act_ref, slope_ref, deep_ref, final_ref, dlog_ref, dup_ref, low_ref,
                ddeep_ref, dhid_ref, sems):
    rows = resid_ref.shape[0]
    blocks = rows // BLOCK
    base = ROW_F1 - VOCAB
    bounds = (ROW_F1, ROW_F2, ROW_U, ROW_END)
    copies = [
        pltpu.make_async_copy(w_hbm.at[pl.ds(low, high - low)], w_ref.at[pl.ds(low - base, high - low)], sems.at[k])
        for k, (low, high) in enumerate(zip(bounds[:-1], bounds[1:]))
    ]
    copies.append(pltpu.make_async_copy(w_hbm.at[pl.ds(0, VOCAB)], w_ref.at[pl.ds(0, VOCAB)], sems.at[3]))
    for copy in copies:
        copy.start()
    f1, f2, up, head = ROW_F1 - base, ROW_F2 - base, ROW_U - base, ROW_H - base
    gain2, offset2 = vec_ref[2:3, :], vec_ref[3:4, :]
    gain_f, offset_f = vec_ref[4:5, :], vec_ref[5:6, :]
    wide = 512

    def norm_step(block, carry):
        at = rows_of(block)
        unit, _ = norm_parts(resid_ref[at, :])
        normed_ref[at, :] = (unit * gain2 + offset2).astype(BF16)
        return carry

    lax.fori_loop(0, blocks, norm_step, 0)
    copies[0].wait()

    def hidden_step(index, carry):
        block, chunk = index // (FF // wide), index % (FF // wide)
        at = rows_of(block)
        lanes = rows_of(chunk, wide)
        hidden = nt(normed_ref[at, :], w_ref[pl.ds(pl.multiple_of(f1 + chunk * wide, VOCAB), wide), :])
        act, slope = gelu_parts(hidden)
        act_ref[at, lanes] = act.astype(BF16)
        slope_ref[at, lanes] = slope
        return carry

    lax.fori_loop(0, blocks * (FF // wide), hidden_step, 0)
    copies[1].wait()

    def deep_step(block, carry):
        at = rows_of(block)
        deep_ref[at, :] = (resid_ref[at, :] + nn(act_ref[at, :], w_ref[f2 : f2 + FF, :])).astype(BF16)
        return carry

    lax.fori_loop(0, blocks, deep_step, 0)
    copies[2].wait()
    copies[3].wait()

    small_ref[...] = jnp.zeros_like(small_ref)

    def head_step(index, carry):
        j, block = index // blocks, index % blocks
        at = rows_of(block)
        there = rows_of(index)
        up_rows = pl.ds(pl.multiple_of(up + j * D, VOCAB), D)
        columns = cols_ref[j, at, :]
        joined = nn(one_hot_rows(columns[:, 0:1]), w_ref[0:VOCAB, :]) + nt(deep_ref[at, :], w_ref[up_rows, :])
        unit, scale = norm_parts(joined)
        final = (unit * gain_f + offset_f).astype(BF16)
        final_ref[there, :] = final
        logits = nt(final, w_ref[head : head + VOCAB, :])
        nexts = columns[:, 2:3]
        lanes = lax.broadcasted_iota(jnp.int32, logits.shape, 1)
        target = jnp.where(lanes == nexts, 1.0, 0.0)
        valid = jnp.where(nexts >= 0, 1.0, 0.0)
        peak = jnp.max(logits, -1, keepdims=True)
        expo = jnp.exp(logits - peak)
        total = jnp.sum(expo, -1, keepdims=True)
        picked = jnp.sum(logits * target, -1, keepdims=True)
        losses = valid * (peak + jnp.log(total) - picked)
        dlogits = ((valid / count) * (expo * (1.0 / total) - target)).astype(BF16)
        dlog_ref[there, :] = dlogits
        dfinal = nn(dlogits, w_ref[head : head + VOCAB, :])
        djoined = norm_back(unit, scale, gain_f, dfinal)
        dup = djoined.astype(BF16)
        dup_ref[there, :] = dup
        low_ref[there, :] = (djoined - dup.astype(F32)).astype(BF16)
        back = nn(dup, w_ref[up_rows, :])

        @pl.when(j == 0)
        def _():
            ddeep_ref[at, :] = back

        @pl.when(j > 0)
        def _():
            ddeep_ref[at, :] += back

        small_ref[4, :, :] += fold_rows(dfinal * unit)
        small_ref[5, :, :] += fold_rows(dfinal)
        small_ref[6, :, :] += jnp.broadcast_to(fold_rows(losses), (8, D))
        return carry

    lax.fori_loop(0, POOL * blocks, head_step, 0)

    out_up, out_head = ROW_U - ROW_F1, ROW_H - ROW_F1
    grads_ref[out_head : out_head + VOCAB, :] = tn(dlog_ref[...], final_ref[...]).astype(BF16)
    for j in range(POOL):
        there = pl.ds(j * rows, rows)
        grads_ref[out_up + j * D : out_up + (j + 1) * D, :] = tn(dup_ref[there, :], deep_ref[...]).astype(BF16)
        hot = one_hot_cols(lines_ref[j : j + 1, :])
        part = nn(hot, dup_ref[there, :]) + nn(hot, low_ref[there, :])
        if j == 0:
            table_ref[...] = part
        else:
            table_ref[...] += part

    deep_ref[...] = ddeep_ref[...].astype(BF16)

    def dhid_step(index, carry):
        block, chunk = index // (FF // wide), index % (FF // wide)
        at = rows_of(block)
        lanes = rows_of(chunk, wide)
        dact = nt(deep_ref[at, :], w_ref[pl.ds(pl.multiple_of(f2 + chunk * wide, VOCAB), wide), :])
        dhid_ref[at, lanes] = (dact * slope_ref[at, lanes]).astype(BF16)
        return carry

    lax.fori_loop(0, blocks * (FF // wide), dhid_step, 0)

    def dff_step(chunk, carry):
        lanes = rows_of(chunk, wide)
        grads_ref[lanes, :] = tn(dhid_ref[:, lanes], normed_ref[...]).astype(BF16)
        grads_ref[pl.ds(pl.multiple_of(FF + chunk * wide, wide), wide), :] = tn(act_ref[:, lanes], deep_ref[...]).astype(BF16)
        return carry

    lax.fori_loop(0, FF // wide, dff_step, 0)

    def dnorm_step(block, carry):
        at = rows_of(block)
        dnormed = nn(dhid_ref[at, :], w_ref[f1 : f1 + FF, :])
        unit, scale = norm_parts(resid_ref[at, :])
        dresid_ref[at, :] = ddeep_ref[at, :] + norm_back(unit, scale, gain2, dnormed)
        small_ref[2, :, :] += fold_rows(dnormed * unit)
        small_ref[3, :, :] += fold_rows(dnormed)
        return carry

    lax.fori_loop(0, blocks, dnorm_step, 0)


def attend_back_kernel(short_len, slots, lay_ref, slope_ref, lines_ref, vec_ref, dresid_ref,
                       shifted_ref, short_ref, normed_ref, qkv_ref, lse_ref, mixed_ref, table_ref, w_hbm,
                       grads_ref, small_ref,
                       w_ref, dist_ref, mask_ref, dbranch_ref, dmix_ref, dqkv_ref, dshort_ref, sems):
    rows = short_len * slots
    blocks = rows // BLOCK
    base = ROW_P
    bounds = (ROW_O, ROW_QKV, ROW_P)
    ends = (ROW_F1, ROW_O, ROW_QKV)
    copies = [
        pltpu.make_async_copy(w_hbm.at[pl.ds(low, high - low)], w_ref.at[pl.ds(low - base, high - low)], sems.at[k])
        for k, (low, high) in enumerate(zip(bounds, ends))
    ]
    for copy in copies:
        copy.start()
    pool, proj, out = ROW_P - base, ROW_QKV - base, ROW_O - base
    small_ref[...] = jnp.zeros_like(small_ref)
    copies[0].wait()

    def dmix_step(block, carry):
        at = rows_of(block)
        dbranch = dresid_ref[at, :].astype(BF16)
        dbranch_ref[at, :] = dbranch
        dmix_ref[at, :] = nt(dbranch, w_ref[out : out + D, :]).astype(BF16)
        return carry

    lax.fori_loop(0, blocks, dmix_step, 0)
    grads_ref[ROW_O:ROW_F1, :] = tn(mixed_ref[...], dbranch_ref[...]).astype(BF16)

    left_lanes = lax.broadcasted_iota(jnp.int32, (short_len, 2 * HEAD), 1) < HEAD
    tile = 128
    for slot in range(slots):
        at = pl.ds(slot * short_len, short_len)
        key = lax.broadcasted_iota(jnp.int32, (short_len, short_len), 0)
        query = lax.broadcasted_iota(jnp.int32, (short_len, short_len), 1)
        half = jnp.where(lay_ref[slot] == 1, short_len // 2, short_len)
        allowed = (key <= query) & ((key >= half) == (query >= half))
        dist_ref[...] = (key - query).astype(F32)
        mask_ref[...] = jnp.where(allowed, 0.0, NEGATIVE)

        def head_step(pair, carry):
            lanes = pl.ds(pl.multiple_of(pair * 2 * HEAD, 2 * HEAD), 2 * HEAD)
            lanes_k = pl.ds(pl.multiple_of(D + pair * 2 * HEAD, 2 * HEAD), 2 * HEAD)
            lanes_v = pl.ds(pl.multiple_of(2 * D + pair * 2 * HEAD, 2 * HEAD), 2 * HEAD)
            queries = qkv_ref[at, lanes]
            keys = qkv_ref[at, lanes_k]
            values = qkv_ref[at, lanes_v]
            dmix = dmix_ref[at, lanes]
            zero = jnp.zeros_like(values)

            def one_side(side, array):
                return jnp.where(left_lanes, array, zero) if side == 0 else jnp.where(left_lanes, zero, array)

            scaled = queries * jnp.asarray(0.125, BF16)
            dkeys = jnp.zeros((short_len, 2 * HEAD), F32)
            dvalues = jnp.zeros((short_len, 2 * HEAD), F32)
            side_k = [one_side(side, keys) for side in range(2)]
            side_v = [one_side(side, values) for side in range(2)]
            side_q = [one_side(side, queries) for side in range(2)]
            side_m = [one_side(side, dmix) for side in range(2)]
            for part in range(short_len // tile):
                low = part * tile
                dqueries = jnp.zeros((tile, 2 * HEAD), F32)
                for side in range(2):
                    head = pair * 2 + side
                    slope = slope_ref[head]
                    scores = nt(side_k[side], scaled[low : low + tile])
                    scores = scores + jnp.where(
                        mask_ref[:, low : low + tile] == 0.0, dist_ref[:, low : low + tile] * slope, NEGATIVE
                    )
                    probs = jnp.exp(scores - lse_ref[slot, head, :, low : low + tile])
                    dprobs = nt(side_v[side], dmix[low : low + tile])
                    delta = jnp.sum(dprobs * probs, 0, keepdims=True)
                    dscores = (probs * (dprobs - delta) * 0.125).astype(BF16)
                    dvalues = dvalues + nn(probs.astype(BF16), side_m[side][low : low + tile])
                    dkeys = dkeys + nn(dscores, side_q[side][low : low + tile])
                    dqueries = dqueries + tn(dscores, side_k[side])
                dqkv_ref[pl.ds(slot * short_len + low, tile), lanes] = dqueries.astype(BF16)
            dqkv_ref[at, lanes_k] = dkeys.astype(BF16)
            dqkv_ref[at, lanes_v] = dvalues.astype(BF16)
            return carry

        lax.fori_loop(0, HEADS // 2, head_step, 0)

    copies[1].wait()
    gain = vec_ref[0:1, :]
    for part in range(3):
        grads_ref[ROW_QKV + part * D : ROW_QKV + (part + 1) * D, :] = tn(
            dqkv_ref[:, part * D : (part + 1) * D], normed_ref[...]
        ).astype(BF16)

    def dshort_step(block, carry):
        at = rows_of(block)
        dnormed = nn(dqkv_ref[at, :], w_ref[proj : proj + 3 * D, :])
        unit, scale = norm_parts(short_ref[at, :])
        dshort_ref[at, :] = (dresid_ref[at, :] + norm_back(unit, scale, gain, dnormed)).astype(BF16)
        small_ref[0, :, :] += fold_rows(dnormed * unit)
        small_ref[1, :, :] += fold_rows(dnormed)
        return carry

    lax.fori_loop(0, blocks, dshort_step, 0)
    copies[2].wait()
    table = table_ref[...]
    for j in range(POOL):
        cols = slice(j * D, (j + 1) * D)
        grads_ref[ROW_P + j * D : ROW_P + (j + 1) * D, :] = tn(shifted_ref[:, cols], dshort_ref[...]).astype(BF16)
        dshift = nt(dshort_ref[...], w_ref[pool + j * D : pool + (j + 1) * D, :])
        high = dshift.astype(BF16)
        low = (dshift - high.astype(F32)).astype(BF16)
        hot = one_hot_cols(lines_ref[POOL + j : POOL + j + 1, :])
        table = table + nn(hot, high) + nn(hot, low)
    grads_ref[ROW_E:ROW_P, :] = table.astype(BF16)


def step_inputs(byte_ids, layouts):
    slots, length = byte_ids.shape
    places = jnp.arange(length, dtype=jnp.int32)[None, :]
    half = length // 2
    split = (layouts == 1)[:, None]
    first = jnp.where(split & (places >= half), half, 0)
    last = jnp.where(split & (places < half), half, length)
    back = jnp.pad(byte_ids[:, :-2], ((0, 0), (2, 0)))
    back = jnp.where(places - 2 >= first, back, -1)
    ahead = jnp.pad(byte_ids[:, 1:], ((0, 0), (0, 1)))
    ahead = jnp.where(places + 1 < last, ahead, -1)
    kinds = jnp.stack([byte_ids, back, ahead], 0)
    kinds = kinds.reshape(3, slots, length // POOL, POOL).transpose(0, 3, 1, 2)
    kinds = kinds.reshape(3, POOL, slots * (length // POOL))
    lines = kinds.reshape(3 * POOL, -1)
    return lines


VMEM = pl.BlockSpec(memory_space=pltpu.VMEM)
SMEM = pl.BlockSpec(memory_space=pltpu.SMEM)
ANY = pl.BlockSpec(memory_space=pl.ANY)
LIMIT = 58 * 1024 * 1024


def device_grads(stacked, vecs, byte_ids, layouts, count):
    slots, length = byte_ids.shape
    short_len = length // POOL
    rows = slots * short_len
    lines = step_inputs(byte_ids, layouts)
    lines = jnp.pad(lines, ((0, 16 - lines.shape[0]), (0, 0)))
    cols = lines.T
    by_place = lines[: 3 * POOL].reshape(3, POOL, rows).transpose(1, 2, 0)
    slopes = 2.0 ** (-8.0 * (jnp.arange(HEADS, dtype=F32) + 1.0) / HEADS)
    vecs = jnp.pad(vecs.astype(F32), ((0, 2), (0, 0)))
    shape = jax.ShapeDtypeStruct
    params = pltpu.CompilerParams(vmem_limit_bytes=LIMIT)
    shifted, short, normed, qkv, lse, mixed, resid = pl.pallas_call(
        partial(attend_kernel, short_len, slots),
        out_shape=(
            shape((rows, POOL * D), BF16),
            shape((rows, D), F32),
            shape((rows, D), BF16),
            shape((rows, 3 * D), BF16),
            shape((slots, HEADS, 1, short_len), F32),
            shape((rows, D), BF16),
            shape((rows, D), F32),
        ),
        in_specs=[SMEM, SMEM, VMEM, VMEM, ANY],
        out_specs=(VMEM,) * 7,
        scratch_shapes=[
            pltpu.VMEM((ROW_F1, D), BF16),
            pltpu.VMEM((short_len, short_len), F32),
            pltpu.VMEM((short_len, short_len), F32),
            pltpu.VMEM((short_len, 2 * HEAD), F32),
            pltpu.SemaphoreType.DMA((3,)),
        ],
        compiler_params=params,
        name="attend",
    )(layouts, slopes, cols, vecs, stacked)
    grads_deep, table, dresid, small_deep = pl.pallas_call(
        partial(deep_kernel, count),
        out_shape=(
            shape((ROW_END - ROW_F1, D), BF16),
            shape((VOCAB, D), F32),
            shape((rows, D), F32),
            shape((8, 8, D), F32),
        ),
        in_specs=[VMEM, VMEM, VMEM, VMEM, ANY],
        out_specs=(VMEM,) * 4,
        scratch_shapes=[
            pltpu.VMEM((ROW_END - ROW_F1 + VOCAB, D), BF16),
            pltpu.VMEM((rows, D), BF16),
            pltpu.VMEM((rows, FF), BF16),
            pltpu.VMEM((rows, FF), F32),
            pltpu.VMEM((rows, D), BF16),
            pltpu.VMEM((POOL * rows, D), BF16),
            pltpu.VMEM((POOL * rows, VOCAB), BF16),
            pltpu.VMEM((POOL * rows, D), BF16),
            pltpu.VMEM((POOL * rows, D), BF16),
            pltpu.VMEM((rows, D), F32),
            pltpu.VMEM((rows, FF), BF16),
            pltpu.SemaphoreType.DMA((4,)),
        ],
        compiler_params=params,
        name="deep",
    )(by_place, lines, vecs, resid, stacked)
    grads_front, small_front = pl.pallas_call(
        partial(attend_back_kernel, short_len, slots),
        out_shape=(shape((ROW_F1, D), BF16), shape((8, 8, D), F32)),
        in_specs=[SMEM, SMEM] + [VMEM] * 10 + [ANY],
        out_specs=(VMEM,) * 2,
        scratch_shapes=[
            pltpu.VMEM((ROW_F1 - ROW_P, D), BF16),
            pltpu.VMEM((short_len, short_len), F32),
            pltpu.VMEM((short_len, short_len), F32),
            pltpu.VMEM((rows, D), BF16),
            pltpu.VMEM((rows, D), BF16),
            pltpu.VMEM((rows, 3 * D), BF16),
            pltpu.VMEM((rows, D), BF16),
            pltpu.SemaphoreType.DMA((3,)),
        ],
        compiler_params=params,
        name="attend_back",
    )(layouts, slopes, lines, vecs, dresid, shifted, short, normed, qkv, lse, mixed, table, stacked)
    small = jnp.sum(small_deep + small_front, 1)
    return grads_front, grads_deep, small


def adam(param, first_m, second_m, grad, decay):
    first_new = BETA * first_m + (1.0 - BETA) * grad
    second_new = BETA * second_m + (1.0 - BETA) * grad * grad
    correct = 1.0 - BETA**STEP
    update = -RATE * (
        first_new / correct / (jnp.sqrt(second_new / correct) + EPS_ADAM) + decay * param
    )
    return (first_new, second_new, update)


def shards(byte_ids, layouts, weights, vectors, m_weights, v_weights, m_vectors, v_vectors):
    devices = lax.axis_size(AXES)
    micro = byte_ids.shape[0]
    count = float(micro * layouts.shape[1] * devices * byte_ids.shape[2])
    stacked = lax.all_gather(weights.astype(BF16), AXES, axis=0, tiled=True)
    vecs = lax.all_gather(vectors.astype(BF16), AXES, axis=1, tiled=True)
    grads_front, grads_deep, small = device_grads(
        stacked, vecs, byte_ids.reshape(-1, byte_ids.shape[-1]), layouts.reshape(-1), count
    )
    local = jnp.concatenate([grads_front, grads_deep], 0)
    owned = lax.psum_scatter(local.astype(F32), AXES, scatter_dimension=0, tiled=True)
    small = lax.psum(small, AXES)
    loss = small[6, 0] / count
    vec_grads = small[:6]
    width = vectors.shape[1]
    owned_vecs = lax.dynamic_slice(vec_grads, (0, lax.axis_index(AXES) * width), (6, width))
    squares = lax.psum(jnp.sum(owned * owned), AXES) + jnp.sum(vec_grads * vec_grads)
    grad_norm = jnp.sqrt(squares)
    factor = CLIP / jnp.maximum(grad_norm, CLIP)
    first_w, second_w, update_w = adam(weights, m_weights, v_weights, owned * factor, DECAY)
    first_v, second_v, update_v = adam(vectors, m_vectors, v_vectors, owned_vecs * factor, 0.0)
    return (loss, grad_norm, first_w, second_w, update_w, first_v, second_v, update_v)


def solution(mesh):
    in_specs = (
        P(None, AXES, None),
        P(None, AXES),
        P(AXES, None),
        P(None, AXES),
        P(AXES, None),
        P(AXES, None),
        P(None, AXES),
        P(None, AXES),
    )
    out_specs = (
        P(),
        P(),
        P(AXES, None),
        P(AXES, None),
        P(AXES, None),
        P(None, AXES),
        P(None, AXES),
        P(None, AXES),
    )
    return jax.shard_map(shards, mesh=mesh, in_specs=in_specs, out_specs=out_specs, check_vma=False)
```

time: 732 us -> 489 us (0.67); the launches traced: 723 us -> 488 us
  matrix products: 174 us -> 0 us
  Pallas kernels: 0 us -> 101 us
  local copies, waits for them, and re-layouts: 83.2 us -> 6.69 us
  other arithmetic: 69.1 us -> 26 us
  waiting for transfers between devices: 294 us -> 254 us
    dot_general x58 -> x0, matrix products: 174 us -> none  [the longest x14 51.7 us: product_nt(): lax.dot_general(left, right, (((1,), (1,)), ((), ())), preferred_element_...]
    pallas_call x0 -> x3, Pallas kernels: none -> 101 us  [the longest x1 45.6 us: device_grads(): pl.pallas_call(partial(deep_kernel, count), out_shape=(shape((ROW_END - R...]
    unnamed x4 -> x2, waiting for transfers between devices: 46.2 us -> 0.03 us
    unnamed x342 -> x22, local copies, waits for them, and re-layouts: 26.4 us -> 1.76 us
    reduce_sum x19 -> x2, other arithmetic: 23.9 us -> 1.88 us  [the longest x1 1.84 us: shards(): jnp.sum(owned * owned)]
    add x6 -> x1, other arithmetic: 20.3 us -> 0.01 us  [step_inputs(): ahead = jnp.where(places + 1 < last, ahead, -1)]
    reshape x8 -> x0, local copies, waits for them, and re-layouts: 18.9 us -> none  [the longest x4 10.9 us: forward(): upward = product_nt(deep, up_w).reshape(length, D)]
    slice x19 -> x2, local copies, waits for them, and re-layouts: 16.6 us -> 0.59 us  [the longest x1 0.51 us: shards(): loss = small[6, 0] / count]
  transfers between devices with their start and end apart: 3 -> 2, of which waited for: 3 -> 2; matrix products, arithmetic and copies ran while one was open for 13% -> 2% of each run, Pallas kernels for 0% -> 0%
where the time goes in v1:
time: 489 us; the launch traced here: 488 us
  waiting for transfers between devices  254 us (52%)
  Pallas kernels  101 us (21%)
  blocking collectives  81.2 us (17%)
  other arithmetic  26 us (5%)
  between operations  18.5 us (4%)
  local copies, waits for them, and re-layouts  6.69 us (1%)
    reduce_scatter x1, waiting for transfers between devices, shards(): lax.psum_scatter(local.astype(F32), AXES, scatter_dimension=0, tiled=True)  217 us
    pallas_call x1, Pallas kernels, device_grads(): pl.pallas_call(partial(deep_kernel, count), out_shape=(shape((ROW_END - R...  45.6 us
    all_gather x1, blocking collectives, shards(): vecs = lax.all_gather(vectors.astype(BF16), AXES, axis=1, tiled=True)  44 us
    psum x1, blocking collectives, shards(): small = lax.psum(small, AXES)  37.2 us
    all_gather x1, waiting for transfers between devices, shards(): stacked = lax.all_gather(weights.astype(BF16), AXES, axis=0, tiled=True)  36.7 us
    pallas_call x1, Pallas kernels, device_grads(): pl.pallas_call(partial(attend_back_kernel, short_len, slots), out_shape=(...  31.8 us
    pallas_call x1, Pallas kernels, device_grads(): pl.pallas_call(partial(attend_kernel, short_len, slots), out_shape=(shape...  23.9 us
    convert_element_type x1, other arithmetic, shards(): local.astype(F32)  15 us
  transfers between devices with their start and end apart: 2, of which 2 were waited for; matrix products, arithmetic and copies ran while one was open for 2% of the time, Pallas kernels for 0%

profile of v1, /device:TPU:0, one launch (start us, length us, event | category | flops | bytes accessed | tf_op | source)
XLA Modules:
  0.0 487.6 jit_solution(16691926626896318891)
XLA Ops:
  7.2 0.0 all-gather.3.cloned.1.call-start
  7.2 1.8 convert_element_type.13
  9.0 0.0 all-gather.3.cloned.1.call-update
  9.1 0.0 reduce-scatter.2.cloned.1.call-start
  9.1 0.7 copy.35
  9.8 0.1 slice.18
  9.9 0.7 compare_bitcast_fusion
  10.6 0.1 compare_select_fusion.1
  10.7 0.3 stack.12
  11.0 0.1 copy.27
  11.1 0.3 stack.13
  11.4 0.1 copy.28
  11.6 0.7 reduce
  12.3 0.3 stack.11
  12.6 0.1 copy.26
  12.8 0.6 pad_bitcast_fusion
  13.4 0.9 copy.31.cols_ref
  14.4 0.7 convert_bitcast_fusion
  15.0 44.0 %all-gather = bf16[32,16,6]{1,2,0:T(8,128)(2,1)S(1)} all-gather(bf16[1,16,6]{1,2,0:T(8,128)(2,1)S(1)} %convert_bitcast_fusion), channel_id=1, replica_groups=mesh['dp'=4,'fsdp'=8] {'dp','fsdp'}, dimensions={0}, use_global_device_ids=true | all-gather | bytes 6336 | tf_op jit(solution)/shard_map/all_gather | solution.py:569
  59.0 0.1 reshape.59
  59.2 1.5 copy.29
  60.7 0.5 multiply_power_fusion.slope_ref
  61.2 0.6 pad_convert_fusion.vec_ref
  61.8 36.7 %all-gather.3.cloned.1.call-done.w_hbm = bf16[9728,512]{1,0:T(8,128)(2,1)} async-done(((bf16[304,512]{1,0:T(8,128)(2,1)}), bf16[9728,512]{1,0:T(8,128)(2,1)}) %all-gather.3.cloned.1.call-update) | async-done | bytes 9961488 | tf_op jit(solution)/shard_map/all_gather | solution.py:568
  98.5 23.9 %attend.1 = (bf16[768,1536]{1,0:T(8,128)(2,1)}, f32[768,512]{1,0:T(8,128)}, bf16[768,512]{1,0:T(8,128)(2,1)}, bf16[768,1536]{1,0:T(8,128)(2,1)}, f32[2,8,1,384]{...) custom-call(s32[2]{0:T(128)} %bitcast.33, f32[8]{0:T(128)} %multiply_power_fusion.slope_ref, ...), custom_call_target="tpu_custom_call" | custom-call | tf_op jit(solution)/shard_map/attend/pallas_call | solution.py:482
  122.4 45.6 %deep.1 = (bf16[5888,512]{1,0:T(8,128)(2,1)}, f32[256,512]{1,0:T(8,128)}, f32[768,512]{1,0:T(8,128)}, f32[8,8,512]{2,1,0:T(8,128)}) custom-call(s32[3,768,3]{2,1,0:T(8,128)} %bitcast.26, s32[16,768]{1,0:T(8,128)} %get-tuple-element.43.lines_ref, f32[8,512]{1,0:T(8,128)} %pad_convert_fusion.vec_ref, f32[768,512]{1,0:T(8,128)} %get-tuple-element.21.resid_ref, ...), custom_call_target="tpu_custom_call" | custom-call | tf_op jit(solution)/shard_map/deep/pallas_call | solution.py:505
  167.9 0.0 copy-start
  168.0 31.8 %attend_back.1 = (bf16[3840,512]{1,0:T(8,128)(2,1)}, f32[8,8,512]{2,1,0:T(8,128)}) custom-call(s32[2]{0:T(128)} %bitcast.34, f32[8]{0:T(128)} %multiply_power_fusion.slope_ref, s32[16,768]{1,0:T(8,128)} %get-tuple-element.43.lines_ref, f32[8,512]{1,0:T(8,128)} %pad_convert_fusion.vec_ref, f32[768,512]{1,0:T(8,128)} %get-tuple-element.23.dresid_ref, ...), custom_call_target="tpu_custom_call" | custom-call | tf_op jit(solution)/shard_map/attend_back/pallas_call | solution.py:532
  199.8 0.0 copy-done
  199.8 15.0 %maximum_convert_fusion = f32[9728,512]{1,0:T(8,128)} fusion(bf16[5888,512]{1,0:T(8,128)(2,1)S(1)} %copy-done, bf16[3840,512]{1,0:T(8,128)(2,1)} %get-tuple-element.32), kind=kLoop, calls=%fused_computation | loop fusion | flops 19922944 | bytes 29884416 | tf_op jit(solution)/shard_map/convert_element_type | solution.py:574
  214.8 0.0 copy-start.8
  214.8 0.0 copy-start.1
  214.8 0.0 copy-start.2
  214.8 0.0 copy-start.3
  214.8 0.0 reduce-scatter.2.cloned.1.call-update
  214.9 0.8 copy-done.4
  215.7 0.1 copy-done.5
  215.8 217.1 %reduce-scatter.2.cloned.1.call-done = f32[304,512]{1,0:T(8,128)} async-done(((f32[9728,512]{1,0:T(8,128)}), f32[304,512]{1,0:T(8,128)}) %reduce-scatter.2.cloned.1.call-update) | async-done | bytes 622608 | tf_op jit(solution)/shard_map/reduce_scatter | solution.py:574
  432.9 1.8 multiply_reduce_fusion
  434.8 37.2 %all-reduce.4 = (f32[8,512]{1,0:T(8,128)S(1)}, f32[]{:T(128)}) all-reduce(f32[8,512]{1,0:T(8,128)S(1)} %add_reduce_fusion, f32[]{:T(128)} %multiply_reduce_fusion), channel_id=1, replica_groups=mesh['dp'=4,'fsdp'=8] {'dp','fsdp'}, use_global_device_ids=true, to_apply=%region_1.2 | all-reduce | flops 4097 | bytes 32776 | tf_op jit(solution)/shard_map/psum | solution.py:575
  472.0 0.6 fusion.4
  472.6 0.5 slice.19
  475.1 0.0 copy-done.6
  475.1 0.0 copy-done.7
  475.2 0.0 copy-done.8
  475.2 0.7 add_multiply_fusion.1
  475.9 0.0 copy-done.1
  475.9 2.7 add_multiply_fusion
  (14 shorter events, 0.1 us)
Async XLA Ops:
  7.2 91.3 %all-gather.3.cloned.1.call-start = ((), (), s32[]{:S(2)}) async-start(), calls=%async_computation.1 | async-start | bytes 10272768 | tf_op jit(solution)/shard_map/all_gather | solution.py:568
  9.1 423.9 %reduce-scatter.2.cloned.1.call-start = ((), (), s32[]{:S(2)}) async-start(), calls=%async_computation.2 | async-start | bytes 20545536 | tf_op jit(solution)/shard_map/reduce_scatter | solution.py:574
  167.9 31.8 %copy-start = (bf16[5888,512]{1,0:T(8,128)(2,1)S(1)}, bf16[5888,512]{1,0:T(8,128)(2,1)}, u32[]{:S(2)}) copy-start(bf16[5888,512]{1,0:T(8,128)(2,1)} %get-tuple-element.33) | copy-start | bytes 18087940
  214.8 0.9 copy-start.4
  214.8 1.0 copy-start.5
  214.8 260.4 %copy-start.6 = (f32[6,16]{1,0:T(8,128)S(1)}, f32[6,16]{1,0:T(8,128)}, u32[]{:S(2)}) copy-start(f32[6,16]{1,0:T(8,128)} %param.11) | copy-start | bytes 1156
  214.8 260.4 %copy-start.7 = (f32[6,16]{1,0:T(8,128)S(1)}, f32[6,16]{1,0:T(8,128)}, u32[]{:S(2)}) copy-start(f32[6,16]{1,0:T(8,128)} %param.15) | copy-start | bytes 1156
  214.8 260.4 %copy-start.8 = (f32[6,16]{1,0:T(8,128)S(1)}, f32[6,16]{1,0:T(8,128)}, u32[]{:S(2)}) copy-start(f32[6,16]{1,0:T(8,128)} %param.14) | copy-start | bytes 1156
  214.8 261.1 %copy-start.1 = (f32[304,512]{1,0:T(8,128)S(1)}, f32[304,512]{1,0:T(8,128)}, u32[]{:S(2)}) copy-start(f32[304,512]{1,0:T(8,128)} %param.10) | copy-start | bytes 1867780
  214.8 261.1 %copy-start.2 = (f32[304,512]{1,0:T(8,128)S(1)}, f32[304,512]{1,0:T(8,128)}, u32[]{:S(2)}) copy-start(f32[304,512]{1,0:T(8,128)} %param.13) | copy-start | bytes 1867780
  214.8 261.1 %copy-start.3 = (f32[304,512]{1,0:T(8,128)S(1)}, f32[304,512]{1,0:T(8,128)}, u32[]{:S(2)}) copy-start(f32[304,512]{1,0:T(8,128)} %param.12) | copy-start | bytes 1867780
Sparse Core Ops, SparseCore 0:
  11.4 87.0 all-gather.2
  215.0 217.9 reduce-scatter.1

commit v2 on v1

--- a/solution.py
+++ b/solution.py
@@ -38,6 +38,9 @@
 
 BLOCK = 256
 AXES = ("dp", "fsdp")
+SHARD = ROW_END // 32
+GATHER_CUT = 208
+SCATTER_CUT = 400
 
 
 def nn(left, right):
@@ -84,18 +87,59 @@
     return pl.ds(pl.multiple_of(index * size, size), size)
 
 
-def attend_kernel(short_len, slots, lay_ref, slope_ref, cols_ref, vec_ref, w_hbm,
-                  shifted_ref, short_ref, normed_ref, qkv_ref, lse_ref, mixed_ref, resid_ref,
-                  w_ref, dist_ref, mask_ref, lse_cols, sems):
+class Fetch:
+    def __init__(self, pieces, coords_ref, w_ref, sems, base, low, high):
+        self.jobs = []
+        if len(pieces) == 1:
+            size = high - low
+            copy = pltpu.make_async_copy(
+                pieces[0].at[pl.ds(low, size)], w_ref.at[pl.ds(low - base, size)], sems.at[0]
+            )
+            self.jobs.append((None, copy))
+            return
+        dp, z, core = coords_ref[0], coords_ref[1], coords_ref[2]
+        shard = SHARD
+        first, last = low // shard, (high - 1) // shard
+        number = 0
+        for side in range(2):
+            for k in range(4):
+                for part in range(4):
+                    for kind, (begin, size) in enumerate(((0, GATHER_CUT), (GATHER_CUT, shard - GATHER_CUT))):
+                        d, e = (k, part) if kind == 0 else (part, k)
+                        owner = (dp ^ d) * 8 + (z ^ e) * 2 + (core ^ side)
+                        wanted = (owner >= first) & (owner <= last)
+                        place = jnp.where(wanted, owner * shard - base + begin, 0)
+                        copy = pltpu.make_async_copy(
+                            pieces[side * 8 + kind * 4 + k].at[pl.ds(part * size, size)],
+                            w_ref.at[pl.ds(pl.multiple_of(place, 16), size)],
+                            sems.at[number],
+                        )
+                        self.jobs.append((wanted, copy))
+                        number += 1
+
+    def start(self):
+        for wanted, copy in self.jobs:
+            if wanted is None:
+                copy.start()
+            else:
+                pl.when(wanted)(copy.start)
+
+    def wait(self):
+        for wanted, copy in self.jobs:
+            if wanted is None:
+                copy.wait()
+            else:
+                pl.when(wanted)(copy.wait)
+
+
+def attend_kernel(short_len, slots, pieces, coords_ref, lay_ref, slope_ref, cols_ref, vec_ref, *refs):
+    w_hbm, refs = refs[:pieces], refs[pieces:]
+    (shifted_ref, short_ref, normed_ref, qkv_ref, lse_ref, mixed_ref, resid_ref,
+     w_ref, dist_ref, mask_ref, lse_cols, sems) = refs
     rows = short_len * slots
-    bounds = (ROW_E, ROW_QKV, ROW_O, ROW_F1)
-    copies = [
-        pltpu.make_async_copy(w_hbm.at[pl.ds(low, high - low)], w_ref.at[pl.ds(low, high - low)], sems.at[k])
-        for k, (low, high) in enumerate(zip(bounds[:-1], bounds[1:]))
-    ]
-    for copy in copies:
-        copy.start()
-    copies[0].wait()
+    fetch = Fetch(w_hbm, coords_ref, w_ref, sems, 0, 0, ROW_F1)
+    fetch.start()
+    fetch.wait()
     gain, offset = vec_ref[0:1, :], vec_ref[1:2, :]
 
     def pool_step(block, carry):
@@ -110,7 +154,6 @@
         return carry
 
     lax.fori_loop(0, rows // BLOCK, pool_step, 0)
-    copies[1].wait()
 
     def qkv_step(block, carry):
         at = rows_of(block)
@@ -168,8 +211,6 @@
         for head in range(HEADS):
             lse_ref[slot, head] = turned[head : head + 1, :]
 
-    copies[2].wait()
-
     def out_step(block, carry):
         at = rows_of(block)
         resid_ref[at, :] = short_ref[at, :] + nn(mixed_ref[at, :], w_ref[ROW_O:ROW_F1, :])
@@ -188,21 +229,26 @@
     return hidden * cdf, cdf + hidden * bell * 0.3989422804014327
 
 
-def deep_kernel(count, cols_ref, lines_ref, vec_ref, resid_ref, w_hbm,
-                grads_ref, table_ref, dresid_ref, small_ref,
-                w_ref, normed_ref, act_ref, slope_ref, deep_ref, final_ref, dlog_ref, dup_ref, low_ref,
-                ddeep_ref, dhid_ref, sems):
+def split_store(keep_ref, send_ref, core, rows, values):
+    half = D // 2
+    low, high = values[:, :half].astype(BF16), values[:, half:].astype(BF16)
+    keep_ref[rows, :] = jnp.where(core == 0, low, high)
+    send_ref[rows, :] = jnp.where(core == 0, high, low)
+
+
+def deep_kernel(count, pieces, coords_ref, cols_ref, lines_ref, vec_ref, resid_ref, *refs):
+    w_hbm, refs = refs[:pieces], refs[pieces:]
+    (keep_ref, send_ref, table_ref, dresid_ref, small_ref,
+     w_ref, e_ref, normed_ref, act_ref, slope_ref, deep_ref, final_ref, dlog_ref, dup_ref, low_ref,
+     ddeep_ref, dhid_ref, sums_ref, sems, e_sems) = refs
     rows = resid_ref.shape[0]
     blocks = rows // BLOCK
-    base = ROW_F1 - VOCAB
-    bounds = (ROW_F1, ROW_F2, ROW_U, ROW_END)
-    copies = [
-        pltpu.make_async_copy(w_hbm.at[pl.ds(low, high - low)], w_ref.at[pl.ds(low - base, high - low)], sems.at[k])
-        for k, (low, high) in enumerate(zip(bounds[:-1], bounds[1:]))
-    ]
-    copies.append(pltpu.make_async_copy(w_hbm.at[pl.ds(0, VOCAB)], w_ref.at[pl.ds(0, VOCAB)], sems.at[3]))
-    for copy in copies:
-        copy.start()
+    base = deep_base(pieces)
+    core = coords_ref[2]
+    fetch = Fetch(w_hbm, coords_ref, w_ref, sems, base, ROW_F1, ROW_END)
+    fetch_e = Fetch(w_hbm, coords_ref, e_ref, e_sems, 0, 0, VOCAB)
+    fetch.start()
+    fetch_e.start()
     f1, f2, up, head = ROW_F1 - base, ROW_F2 - base, ROW_U - base, ROW_H - base
     gain2, offset2 = vec_ref[2:3, :], vec_ref[3:4, :]
     gain_f, offset_f = vec_ref[4:5, :], vec_ref[5:6, :]
@@ -215,20 +261,20 @@
         return carry
 
     lax.fori_loop(0, blocks, norm_step, 0)
-    copies[0].wait()
+    fetch.wait()
+    fetch_e.wait()
 
     def hidden_step(index, carry):
         block, chunk = index // (FF // wide), index % (FF // wide)
         at = rows_of(block)
         lanes = rows_of(chunk, wide)
-        hidden = nt(normed_ref[at, :], w_ref[pl.ds(pl.multiple_of(f1 + chunk * wide, VOCAB), wide), :])
+        hidden = nt(normed_ref[at, :], w_ref[pl.ds(pl.multiple_of(f1 + chunk * wide, 16), wide), :])
         act, slope = gelu_parts(hidden)
         act_ref[at, lanes] = act.astype(BF16)
         slope_ref[at, lanes] = slope
         return carry
 
     lax.fori_loop(0, blocks * (FF // wide), hidden_step, 0)
-    copies[1].wait()
 
     def deep_step(block, carry):
         at = rows_of(block)
@@ -236,18 +282,15 @@
         return carry
 
     lax.fori_loop(0, blocks, deep_step, 0)
-    copies[2].wait()
-    copies[3].wait()
-
-    small_ref[...] = jnp.zeros_like(small_ref)
+    sums_ref[...] = jnp.zeros_like(sums_ref)
 
     def head_step(index, carry):
         j, block = index // blocks, index % blocks
         at = rows_of(block)
         there = rows_of(index)
-        up_rows = pl.ds(pl.multiple_of(up + j * D, VOCAB), D)
+        up_rows = pl.ds(pl.multiple_of(up + j * D, 16), D)
         columns = cols_ref[j, at, :]
-        joined = nn(one_hot_rows(columns[:, 0:1]), w_ref[0:VOCAB, :]) + nt(deep_ref[at, :], w_ref[up_rows, :])
+        joined = nn(one_hot_rows(columns[:, 0:1]), e_ref[0:VOCAB, :]) + nt(deep_ref[at, :], w_ref[up_rows, :])
         unit, scale = norm_parts(joined)
         final = (unit * gain_f + offset_f).astype(BF16)
         final_ref[there, :] = final
@@ -278,18 +321,18 @@
         def _():
             ddeep_ref[at, :] += back
 
-        small_ref[4, :, :] += fold_rows(dfinal * unit)
-        small_ref[5, :, :] += fold_rows(dfinal)
-        small_ref[6, :, :] += jnp.broadcast_to(fold_rows(losses), (8, D))
+        sums_ref[4, :, :] += fold_rows(dfinal * unit)
+        sums_ref[5, :, :] += fold_rows(dfinal)
+        sums_ref[6, :, :] += jnp.broadcast_to(fold_rows(losses), (8, D))
         return carry
 
     lax.fori_loop(0, POOL * blocks, head_step, 0)
 
     out_up, out_head = ROW_U - ROW_F1, ROW_H - ROW_F1
-    grads_ref[out_head : out_head + VOCAB, :] = tn(dlog_ref[...], final_ref[...]).astype(BF16)
+    split_store(keep_ref, send_ref, core, pl.ds(out_head, VOCAB), tn(dlog_ref[...], final_ref[...]))
     for j in range(POOL):
         there = pl.ds(j * rows, rows)
-        grads_ref[out_up + j * D : out_up + (j + 1) * D, :] = tn(dup_ref[there, :], deep_ref[...]).astype(BF16)
+        split_store(keep_ref, send_ref, core, pl.ds(out_up + j * D, D), tn(dup_ref[there, :], deep_ref[...]))
         hot = one_hot_cols(lines_ref[j : j + 1, :])
         part = nn(hot, dup_ref[there, :]) + nn(hot, low_ref[there, :])
         if j == 0:
@@ -303,7 +346,7 @@
         block, chunk = index // (FF // wide), index % (FF // wide)
         at = rows_of(block)
         lanes = rows_of(chunk, wide)
-        dact = nt(deep_ref[at, :], w_ref[pl.ds(pl.multiple_of(f2 + chunk * wide, VOCAB), wide), :])
+        dact = nt(deep_ref[at, :], w_ref[pl.ds(pl.multiple_of(f2 + chunk * wide, 16), wide), :])
         dhid_ref[at, lanes] = (dact * slope_ref[at, lanes]).astype(BF16)
         return carry
 
@@ -311,8 +354,9 @@
 
     def dff_step(chunk, carry):
         lanes = rows_of(chunk, wide)
-        grads_ref[lanes, :] = tn(dhid_ref[:, lanes], normed_ref[...]).astype(BF16)
-        grads_ref[pl.ds(pl.multiple_of(FF + chunk * wide, wide), wide), :] = tn(act_ref[:, lanes], deep_ref[...]).astype(BF16)
+        split_store(keep_ref, send_ref, core, lanes, tn(dhid_ref[:, lanes], normed_ref[...]))
+        there = pl.ds(pl.multiple_of(FF + chunk * wide, wide), wide)
+        split_store(keep_ref, send_ref, core, there, tn(act_ref[:, lanes], deep_ref[...]))
         return carry
 
     lax.fori_loop(0, FF // wide, dff_step, 0)
@@ -322,31 +366,29 @@
         dnormed = nn(dhid_ref[at, :], w_ref[f1 : f1 + FF, :])
         unit, scale = norm_parts(resid_ref[at, :])
         dresid_ref[at, :] = ddeep_ref[at, :] + norm_back(unit, scale, gain2, dnormed)
-        small_ref[2, :, :] += fold_rows(dnormed * unit)
-        small_ref[3, :, :] += fold_rows(dnormed)
+        sums_ref[2, :, :] += fold_rows(dnormed * unit)
+        sums_ref[3, :, :] += fold_rows(dnormed)
         return carry
 
     lax.fori_loop(0, blocks, dnorm_step, 0)
-
-
-def attend_back_kernel(short_len, slots, lay_ref, slope_ref, lines_ref, vec_ref, dresid_ref,
-                       shifted_ref, short_ref, normed_ref, qkv_ref, lse_ref, mixed_ref, table_ref, w_hbm,
-                       grads_ref, small_ref,
-                       w_ref, dist_ref, mask_ref, dbranch_ref, dmix_ref, dqkv_ref, dshort_ref, sems):
+    for k in range(8):
+        small_ref[k : k + 1, :] = jnp.sum(sums_ref[k], 0, keepdims=True)
+
+
+def attend_back_kernel(short_len, slots, pieces, coords_ref, lay_ref, slope_ref, lines_ref, vec_ref, dresid_ref,
+                       shifted_ref, short_ref, normed_ref, qkv_ref, lse_ref, mixed_ref, table_ref, deep_small_ref, *refs):
+    w_hbm, refs = refs[:pieces], refs[pieces:]
+    (keep_ref, send_ref, small_ref,
+     w_ref, dist_ref, mask_ref, dbranch_ref, dmix_ref, dqkv_ref, dshort_ref, sums_ref, sems) = refs
     rows = short_len * slots
     blocks = rows // BLOCK
-    base = ROW_P
-    bounds = (ROW_O, ROW_QKV, ROW_P)
-    ends = (ROW_F1, ROW_O, ROW_QKV)
-    copies = [
-        pltpu.make_async_copy(w_hbm.at[pl.ds(low, high - low)], w_ref.at[pl.ds(low - base, high - low)], sems.at[k])
-        for k, (low, high) in enumerate(zip(bounds, ends))
-    ]
-    for copy in copies:
-        copy.start()
+    base = 0
+    core = coords_ref[2]
+    fetch = Fetch(w_hbm, coords_ref, w_ref, sems, 0, 0, ROW_F1)
+    fetch.start()
     pool, proj, out = ROW_P - base, ROW_QKV - base, ROW_O - base
-    small_ref[...] = jnp.zeros_like(small_ref)
-    copies[0].wait()
+    sums_ref[...] = jnp.zeros_like(sums_ref)
+    fetch.wait()
 
     def dmix_step(block, carry):
         at = rows_of(block)
@@ -356,7 +398,7 @@
         return carry
 
     lax.fori_loop(0, blocks, dmix_step, 0)
-    grads_ref[ROW_O:ROW_F1, :] = tn(mixed_ref[...], dbranch_ref[...]).astype(BF16)
+    split_store(keep_ref, send_ref, core, pl.ds(ROW_O, D), tn(mixed_ref[...], dbranch_ref[...]))
 
     left_lanes = lax.broadcasted_iota(jnp.int32, (short_len, 2 * HEAD), 1) < HEAD
     tile = 128
@@ -413,34 +455,164 @@
 
         lax.fori_loop(0, HEADS // 2, head_step, 0)
 
-    copies[1].wait()
     gain = vec_ref[0:1, :]
     for part in range(3):
-        grads_ref[ROW_QKV + part * D : ROW_QKV + (part + 1) * D, :] = tn(
-            dqkv_ref[:, part * D : (part + 1) * D], normed_ref[...]
-        ).astype(BF16)
+        grad = tn(dqkv_ref[:, part * D : (part + 1) * D], normed_ref[...])
+        split_store(keep_ref, send_ref, core, pl.ds(ROW_QKV + part * D, D), grad)
 
     def dshort_step(block, carry):
         at = rows_of(block)
         dnormed = nn(dqkv_ref[at, :], w_ref[proj : proj + 3 * D, :])
         unit, scale = norm_parts(short_ref[at, :])
         dshort_ref[at, :] = (dresid_ref[at, :] + norm_back(unit, scale, gain, dnormed)).astype(BF16)
-        small_ref[0, :, :] += fold_rows(dnormed * unit)
-        small_ref[1, :, :] += fold_rows(dnormed)
+        sums_ref[0, :, :] += fold_rows(dnormed * unit)
+        sums_ref[1, :, :] += fold_rows(dnormed)
         return carry
 
     lax.fori_loop(0, blocks, dshort_step, 0)
-    copies[2].wait()
     table = table_ref[...]
     for j in range(POOL):
         cols = slice(j * D, (j + 1) * D)
-        grads_ref[ROW_P + j * D : ROW_P + (j + 1) * D, :] = tn(shifted_ref[:, cols], dshort_ref[...]).astype(BF16)
+        split_store(keep_ref, send_ref, core, pl.ds(ROW_P + j * D, D), tn(shifted_ref[:, cols], dshort_ref[...]))
         dshift = nt(dshort_ref[...], w_ref[pool + j * D : pool + (j + 1) * D, :])
         high = dshift.astype(BF16)
         low = (dshift - high.astype(F32)).astype(BF16)
         hot = one_hot_cols(lines_ref[POOL + j : POOL + j + 1, :])
         table = table + nn(hot, high) + nn(hot, low)
-    grads_ref[ROW_E:ROW_P, :] = table.astype(BF16)
+    split_store(keep_ref, send_ref, core, pl.ds(ROW_E, VOCAB), table)
+    small_ref[...] = deep_small_ref[...]
+    for k in range(2):
+        small_ref[k : k + 1, :] = jnp.sum(sums_ref[k], 0, keepdims=True)
+    half = D // 2
+    for k in range(2):
+        send_ref[ROW_F1 + 16 * k : ROW_F1 + 16 * (k + 1), :] = two_parts(small_ref[:, k * half : (k + 1) * half])
+
+
+def two_parts(values):
+    high = values.astype(BF16)
+    low = (values - high.astype(F32)).astype(BF16)
+    return jnp.concatenate([high.astype(F32), low.astype(F32)], 0).astype(BF16)
+
+
+def one_value(parts):
+    parts = parts.astype(F32)
+    return parts[:8] + parts[8:]
+
+
+def core_sum_kernel(coords_ref, keep_front, keep_deep, recv_front, recv_deep, small_ref,
+                    p0, p1, p2, p3, q0, q1, q2, q3,
+                    keep_ref, recv_ref, sems):
+    copies = [
+        pltpu.make_async_copy(source, target, sems.at[k])
+        for k, (source, target) in enumerate((
+            (keep_deep, keep_ref.at[pl.ds(ROW_F1, ROW_END - ROW_F1)]),
+            (recv_deep, recv_ref.at[pl.ds(ROW_F1, ROW_END - ROW_F1)]),
+            (keep_front, keep_ref.at[pl.ds(0, ROW_F1)]),
+            (recv_front.at[pl.ds(0, ROW_F1)], recv_ref.at[pl.ds(0, ROW_F1)]),
+            (recv_front.at[pl.ds(ROW_F1, 32)], recv_ref.at[pl.ds(ROW_END, 32)]),
+        ))
+    ]
+    for copy in copies:
+        copy.start()
+    for copy in copies:
+        copy.wait()
+    dp, z = coords_ref[0], coords_ref[1]
+    quarter = D // 4
+    line = 2 * SHARD
+
+    def total(half, column, x, zed, begin, size):
+        row = half * (8 * line) + x * (4 * line) + zed * line + begin
+        at = pl.ds(pl.multiple_of(row, 16), size)
+        lanes = pl.ds(pl.multiple_of(column * quarter, quarter), quarter)
+        return (keep_ref[at, lanes].astype(F32) + recv_ref[at, lanes].astype(F32)).astype(BF16)
+
+    rest = line - SCATTER_CUT
+    for k, p_ref in enumerate((p0, p1, p2, p3)):
+        there = dp ^ k
+
+        def p_step(index, carry):
+            half, zed = index // 4, index % 4
+            p_ref[pl.ds(pl.multiple_of(index * SCATTER_CUT, 16), SCATTER_CUT), :] = total(
+                half, there // 2, there % 2, zed, 0, SCATTER_CUT
+            )
+            return carry
+
+        lax.fori_loop(0, 8, p_step, 0)
+    for k, q_ref in enumerate((q0, q1, q2, q3)):
+        zed = z ^ k
+
+        def q_step(index, carry):
+            half, there = index // 4, index % 4
+            q_ref[pl.ds(pl.multiple_of(index * rest, 16), rest), :] = total(
+                half, there // 2, there % 2, zed, SCATTER_CUT, rest
+            )
+            return carry
+
+        lax.fori_loop(0, 8, q_step, 0)
+    for k in range(2):
+        both = small_ref[:, 2 * k * quarter : 2 * (k + 1) * quarter] + one_value(
+            recv_ref[ROW_END + 16 * k : ROW_END + 16 * (k + 1), :]
+        )
+        for side in range(2):
+            parts = two_parts(both[:, side * quarter : (side + 1) * quarter])
+            row = 8 * SCATTER_CUT + 16 * (2 * k + side)
+            for p_ref in (p0, p1, p2, p3):
+                p_ref[row : row + 16, :] = parts
+
+
+def first_sum_kernel(coords_ref, p0, p1, p2, p3, q0, q1, q2, q3,
+                     s0, s1, s2, s3, t0, t1, t2, t3):
+    dp, z = coords_ref[0], coords_ref[1]
+    rest = 2 * SHARD - SCATTER_CUT
+
+    def total(refs, row, size):
+        at = pl.ds(pl.multiple_of(row, 16), size)
+        return (refs[0][at, :].astype(F32) + refs[1][at, :].astype(F32)) + (
+            refs[2][at, :].astype(F32) + refs[3][at, :].astype(F32)
+        )
+
+    for k, s_ref in enumerate((s0, s1, s2, s3)):
+        for half in range(2):
+            s_ref[half * SCATTER_CUT : (half + 1) * SCATTER_CUT, :] = total(
+                (p0, p1, p2, p3), (half * 4 + (z ^ k)) * SCATTER_CUT, SCATTER_CUT
+            ).astype(BF16)
+    for k, t_ref in enumerate((t0, t1, t2, t3)):
+        for half in range(2):
+            t_ref[half * rest : (half + 1) * rest, :] = total(
+                (q0, q1, q2, q3), (half * 4 + (dp ^ k)) * rest, rest
+            ).astype(BF16)
+    for k in range(4):
+        row = 8 * SCATTER_CUT + 16 * k
+        value = sum(one_value(ref[row : row + 16, :]) for ref in (p0, p1, p2, p3))
+        parts = two_parts(value)
+        for s_ref in (s0, s1, s2, s3):
+            s_ref[2 * SCATTER_CUT + 16 * k : 2 * SCATTER_CUT + 16 * (k + 1), :] = parts
+
+
+def last_sum_kernel(coords_ref, s0, s1, s2, s3, t0, t1, t2, t3, mine_ref, other_ref, small_ref, square_ref):
+    own = coords_ref[0] // 2
+    line = 2 * SHARD
+    rest = line - SCATTER_CUT
+
+    def total(refs, half, size):
+        at = pl.ds(pl.multiple_of(half * size, 16), size)
+        return (refs[0][at, :].astype(F32) + refs[1][at, :].astype(F32)) + (
+            refs[2][at, :].astype(F32) + refs[3][at, :].astype(F32)
+        )
+
+    squares = jnp.zeros((8, D // 4), F32)
+    for half, out_ref in ((own, mine_ref), (1 - own, other_ref)):
+        first = total((s0, s1, s2, s3), half, SCATTER_CUT)
+        second = total((t0, t1, t2, t3), half, rest)
+        out_ref[0:SCATTER_CUT, :] = first
+        out_ref[SCATTER_CUT:line, :] = second
+        squares = squares + fold_rows(first * first) + fold_rows(second * second)
+    for k in range(4):
+        row = 2 * SCATTER_CUT + 16 * k
+        small_ref[:, k * (D // 4) : (k + 1) * (D // 4)] = sum(
+            one_value(ref[row : row + 16, :]) for ref in (s0, s1, s2, s3)
+        )
+    square_ref[...] = squares
 
 
 def step_inputs(byte_ids, layouts):
@@ -467,20 +639,31 @@
 LIMIT = 58 * 1024 * 1024
 
 
-def device_grads(stacked, vecs, byte_ids, layouts, count):
+def deep_base(pieces):
+    return ROW_F1 if pieces == 1 else ROW_F1 // SHARD * SHARD
+
+
+def device_grads(pieces, coords, vecs, byte_ids, layouts, count, exchange):
     slots, length = byte_ids.shape
     short_len = length // POOL
     rows = slots * short_len
     lines = step_inputs(byte_ids, layouts)
+    by_place = lines.reshape(3, POOL, rows).transpose(1, 2, 0)
     lines = jnp.pad(lines, ((0, 16 - lines.shape[0]), (0, 0)))
     cols = lines.T
-    by_place = lines[: 3 * POOL].reshape(3, POOL, rows).transpose(1, 2, 0)
     slopes = 2.0 ** (-8.0 * (jnp.arange(HEADS, dtype=F32) + 1.0) / HEADS)
     vecs = jnp.pad(vecs.astype(F32), ((0, 2), (0, 0)))
     shape = jax.ShapeDtypeStruct
     params = pltpu.CompilerParams(vmem_limit_bytes=LIMIT)
+    number = len(pieces)
+    whole_shards = number > 1
+    front_rows = -(-ROW_F1 // SHARD) * SHARD if whole_shards else ROW_F1
+    deep_rows = ROW_END - deep_base(number)
+    table_rows = SHARD if whole_shards else VOCAB
+    jobs = 64 if whole_shards else 1
+    half = D // 2
     shifted, short, normed, qkv, lse, mixed, resid = pl.pallas_call(
-        partial(attend_kernel, short_len, slots),
+        partial(attend_kernel, short_len, slots, number),
         out_shape=(
             shape((rows, POOL * D), BF16),
             shape((rows, D), F32),
@@ -490,30 +673,32 @@
             shape((rows, D), BF16),
             shape((rows, D), F32),
         ),
-        in_specs=[SMEM, SMEM, VMEM, VMEM, ANY],
+        in_specs=[SMEM, SMEM, SMEM, VMEM, VMEM] + [ANY] * number,
         out_specs=(VMEM,) * 7,
         scratch_shapes=[
-            pltpu.VMEM((ROW_F1, D), BF16),
+            pltpu.VMEM((front_rows, D), BF16),
             pltpu.VMEM((short_len, short_len), F32),
             pltpu.VMEM((short_len, short_len), F32),
             pltpu.VMEM((short_len, 2 * HEAD), F32),
-            pltpu.SemaphoreType.DMA((3,)),
+            pltpu.SemaphoreType.DMA((jobs,)),
         ],
         compiler_params=params,
         name="attend",
-    )(layouts, slopes, cols, vecs, stacked)
-    grads_deep, table, dresid, small_deep = pl.pallas_call(
-        partial(deep_kernel, count),
+    )(coords, layouts, slopes, cols, vecs, *pieces)
+    keep_deep, send_deep, table, dresid, small_deep = pl.pallas_call(
+        partial(deep_kernel, count, number),
         out_shape=(
-            shape((ROW_END - ROW_F1, D), BF16),
+            shape((ROW_END - ROW_F1, half), BF16),
+            shape((ROW_END - ROW_F1, half), BF16),
             shape((VOCAB, D), F32),
             shape((rows, D), F32),
-            shape((8, 8, D), F32),
+            shape((8, D), F32),
         ),
-        in_specs=[VMEM, VMEM, VMEM, VMEM, ANY],
-        out_specs=(VMEM,) * 4,
+        in_specs=[SMEM] + [VMEM] * 4 + [ANY] * number,
+        out_specs=(VMEM,) * 5,
         scratch_shapes=[
-            pltpu.VMEM((ROW_END - ROW_F1 + VOCAB, D), BF16),
+            pltpu.VMEM((deep_rows, D), BF16),
+            pltpu.VMEM((table_rows, D), BF16),
             pltpu.VMEM((rows, D), BF16),
             pltpu.VMEM((rows, FF), BF16),
             pltpu.VMEM((rows, FF), F32),
@@ -524,31 +709,128 @@
             pltpu.VMEM((POOL * rows, D), BF16),
             pltpu.VMEM((rows, D), F32),
             pltpu.VMEM((rows, FF), BF16),
-            pltpu.SemaphoreType.DMA((4,)),
+            pltpu.VMEM((8, 8, D), F32),
+            pltpu.SemaphoreType.DMA((jobs,)),
+            pltpu.SemaphoreType.DMA((jobs,)),
         ],
         compiler_params=params,
         name="deep",
-    )(by_place, lines, vecs, resid, stacked)
-    grads_front, small_front = pl.pallas_call(
-        partial(attend_back_kernel, short_len, slots),
-        out_shape=(shape((ROW_F1, D), BF16), shape((8, 8, D), F32)),
-        in_specs=[SMEM, SMEM] + [VMEM] * 10 + [ANY],
-        out_specs=(VMEM,) * 2,
+    )(coords, by_place, lines, vecs, resid, *pieces)
+    recv_deep = exchange(send_deep)
+    keep_front, send_front, small = pl.pallas_call(
+        partial(attend_back_kernel, short_len, slots, number),
+        out_shape=(shape((ROW_F1, half), BF16), shape((ROW_F1 + 32, half), BF16), shape((8, D), F32)),
+        in_specs=[SMEM, SMEM, SMEM] + [VMEM] * 11 + [ANY] * number,
+        out_specs=(VMEM,) * 3,
         scratch_shapes=[
-            pltpu.VMEM((ROW_F1 - ROW_P, D), BF16),
+            pltpu.VMEM((front_rows, D), BF16),
             pltpu.VMEM((short_len, short_len), F32),
             pltpu.VMEM((short_len, short_len), F32),
             pltpu.VMEM((rows, D), BF16),
             pltpu.VMEM((rows, D), BF16),
             pltpu.VMEM((rows, 3 * D), BF16),
             pltpu.VMEM((rows, D), BF16),
-            pltpu.SemaphoreType.DMA((3,)),
+            pltpu.VMEM((2, 8, D), F32),
+            pltpu.SemaphoreType.DMA((jobs,)),
         ],
         compiler_params=params,
+        cost_estimate=pl.CostEstimate(flops=13_000_000_000, bytes_accessed=20_000_000, transcendentals=2_400_000),
         name="attend_back",
-    )(layouts, slopes, lines, vecs, dresid, shifted, short, normed, qkv, lse, mixed, table, stacked)
-    small = jnp.sum(small_deep + small_front, 1)
-    return grads_front, grads_deep, small
+    )(coords, layouts, slopes, lines, vecs, dresid, shifted, short, normed, qkv, lse, mixed, table, small_deep, *pieces)
+    recv_front = exchange(send_front)
+    return keep_front, recv_front, keep_deep, recv_deep, small
+
+
+def swap_with(array, line=0, zed=0, core=0):
+    lines, rest = lax.axis_size("dp"), lax.axis_size("fsdp")
+    pairs = [
+        (d * rest + f, (d ^ line) * rest + (f ^ (2 * zed + core)))
+        for d in range(lines)
+        for f in range(rest)
+    ]
+    return lax.ppermute(array, AXES, pairs)
+
+
+def gather_pieces(shard):
+    first, second = shard[:GATHER_CUT], shard[GATHER_CUT:]
+    along = jnp.concatenate([first] + [swap_with(first, zed=k) for k in (1, 2, 3)], 0)
+    across = jnp.concatenate([second] + [swap_with(second, line=k) for k in (1, 2, 3)], 0)
+    pieces = [along] + [swap_with(along, line=k) for k in (1, 2, 3)]
+    pieces += [across] + [swap_with(across, zed=k) for k in (1, 2, 3)]
+    return pieces + [swap_with(piece, core=1) for piece in pieces]
+
+
+def gather_vectors(vectors):
+    width = vectors.shape[1]
+    spread = jnp.zeros((8, lax.axis_size(AXES) * width), BF16)
+    spread = lax.dynamic_update_slice(spread, jnp.pad(vectors, ((0, 2), (0, 0))), (0, lax.axis_index(AXES) * width))
+    spread = spread + swap_with(spread, core=1)
+    for k in (1, 2):
+        spread = spread + swap_with(spread, line=k)
+    for k in (1, 2):
+        spread = spread + swap_with(spread, zed=k)
+    return spread[:6]
+
+
+def scatter_sum(coords, keep_front, recv_front, keep_deep, recv_deep, small):
+    shape = jax.ShapeDtypeStruct
+    params = pltpu.CompilerParams(vmem_limit_bytes=LIMIT)
+    quarter = D // 4
+    line = 2 * SHARD
+    rest = line - SCATTER_CUT
+    parts = pl.pallas_call(
+        core_sum_kernel,
+        out_shape=(shape((8 * SCATTER_CUT + 64, quarter), BF16),) * 4 + (shape((8 * rest, quarter), BF16),) * 4,
+        in_specs=[SMEM] + [ANY] * 4 + [VMEM],
+        out_specs=(VMEM,) * 8,
+        scratch_shapes=[
+            pltpu.VMEM((ROW_END, D // 2), BF16),
+            pltpu.VMEM((ROW_END + 32, D // 2), BF16),
+            pltpu.SemaphoreType.DMA((5,)),
+        ],
+        compiler_params=params,
+        name="core_sum",
+    )(coords, keep_front, keep_deep, recv_front, recv_deep, small)
+    first = [parts[0]] + [swap_with(parts[k], line=k) for k in (1, 2, 3)]
+    first += [parts[4]] + [swap_with(parts[4 + k], zed=k) for k in (1, 2, 3)]
+    parts = pl.pallas_call(
+        first_sum_kernel,
+        out_shape=(shape((2 * SCATTER_CUT + 64, quarter), BF16),) * 4 + (shape((2 * rest, quarter), BF16),) * 4,
+        in_specs=[SMEM] + [VMEM] * 8,
+        out_specs=(VMEM,) * 8,
+        compiler_params=params,
+        name="first_sum",
+    )(coords, *first)
+    second = [parts[0]] + [swap_with(parts[k], zed=k) for k in (1, 2, 3)]
+    second += [parts[4]] + [swap_with(parts[4 + k], line=k) for k in (1, 2, 3)]
+    mine, other, small, squares = pl.pallas_call(
+        last_sum_kernel,
+        out_shape=(shape((line, quarter), F32),) * 2 + (shape((8, D), F32), shape((8, quarter), F32)),
+        in_specs=[SMEM] + [VMEM] * 8,
+        out_specs=(VMEM,) * 4,
+        compiler_params=params,
+        name="last_sum",
+    )(coords, *second)
+    row, core = coords[0] // 2, coords[2]
+    theirs = swap_with(other, line=2)
+    half = jnp.concatenate(
+        [jnp.where(row == 0, mine, theirs), jnp.where(row == 0, theirs, mine)], 1
+    )
+    keep = jnp.where(core == 0, half[:SHARD], half[SHARD:])
+    send = jnp.where(core == 0, half[SHARD:], half[:SHARD])
+    back = swap_with(send, core=1)
+    owned = jnp.concatenate([jnp.where(core == 0, keep, back), jnp.where(core == 0, back, keep)], 1)
+    return owned, small, jnp.sum(squares)
+
+
+def sum_all(value):
+    value = jnp.broadcast_to(value, (8, 128))
+    value = value + swap_with(value, core=1)
+    for k in (1, 2):
+        value = value + swap_with(value, line=k)
+    for k in (1, 2):
+        value = value + swap_with(value, zed=k)
+    return value[0, 0]
 
 
 def adam(param, first_m, second_m, grad, decay):
@@ -565,19 +847,40 @@
     devices = lax.axis_size(AXES)
     micro = byte_ids.shape[0]
     count = float(micro * layouts.shape[1] * devices * byte_ids.shape[2])
-    stacked = lax.all_gather(weights.astype(BF16), AXES, axis=0, tiled=True)
-    vecs = lax.all_gather(vectors.astype(BF16), AXES, axis=1, tiled=True)
-    grads_front, grads_deep, small = device_grads(
-        stacked, vecs, byte_ids.reshape(-1, byte_ids.shape[-1]), layouts.reshape(-1), count
-    )
-    local = jnp.concatenate([grads_front, grads_deep], 0)
-    owned = lax.psum_scatter(local.astype(F32), AXES, scatter_dimension=0, tiled=True)
-    small = lax.psum(small, AXES)
+    lines, rest = lax.axis_size("dp"), lax.axis_size("fsdp")
+    place = lax.axis_index("fsdp")
+    coords = jnp.stack([lax.axis_index("dp"), place // 2, place % 2, 0]).astype(jnp.int32)
+    paired = lines == 4 and rest == 8 and weights.shape[0] == SHARD
+    weights_low = weights.astype(BF16)
+    vectors_low = vectors.astype(BF16)
+    width = vectors.shape[1]
+    mine = lax.axis_index(AXES) * width
+    flat_ids, flat_layouts = byte_ids.reshape(-1, byte_ids.shape[-1]), layouts.reshape(-1)
+    if paired:
+        pieces = gather_pieces(weights_low)
+        vecs = gather_vectors(vectors_low)
+        parts = device_grads(pieces, coords, vecs, flat_ids, flat_layouts, count, partial(swap_with, core=1))
+        owned, small, squares = scatter_sum(coords, *parts)
+        squares = sum_all(squares)
+    else:
+        coords = coords * 0
+        pieces = [lax.all_gather(weights_low, AXES, axis=0, tiled=True)]
+        vecs = lax.all_gather(vectors_low, AXES, axis=1, tiled=True)
+        parts = device_grads(pieces, coords, vecs, flat_ids, flat_layouts, count, lambda array: array)
+        keep_front, send_front, keep_deep, send_deep, small = parts
+        local = jnp.concatenate(
+            [
+                jnp.concatenate([keep_front, send_front[:ROW_F1]], 1),
+                jnp.concatenate([keep_deep, send_deep], 1),
+            ],
+            0,
+        )
+        owned = lax.psum_scatter(local.astype(F32), AXES, scatter_dimension=0, tiled=True)
+        small, squares = lax.psum((small, jnp.sum(owned * owned)), AXES)
     loss = small[6, 0] / count
     vec_grads = small[:6]
-    width = vectors.shape[1]
-    owned_vecs = lax.dynamic_slice(vec_grads, (0, lax.axis_index(AXES) * width), (6, width))
-    squares = lax.psum(jnp.sum(owned * owned), AXES) + jnp.sum(vec_grads * vec_grads)
+    owned_vecs = lax.dynamic_slice(vec_grads, (0, mine), (6, width))
+    squares = squares + jnp.sum(vec_grads * vec_grads)
     grad_norm = jnp.sqrt(squares)
     factor = CLIP / jnp.maximum(grad_norm, CLIP)
     first_w, second_w, update_w = adam(weights, m_weights, v_weights, owned * factor, DECAY)

time: 489 us -> 318 us (0.65)
  waiting for transfers between devices: 254 us -> 102 us
  blocking collectives: 81.2 us -> 0 us
  starting transfers between devices: 0.08 us -> 63.3 us
  Pallas kernels: 101 us -> 122 us
  other arithmetic: 26 us -> 9.97 us
  between operations: 18.5 us -> 5.47 us
  local copies, waits for them, and re-layouts: 6.69 us -> 14.9 us
    reduce_scatter x1 -> x0, waiting for transfers between devices: 217 us -> none  [shards(): lax.psum_scatter(local.astype(F32), AXES, scatter_dimension=0, tiled=True)]
    ppermute x0 -> x46, waiting for transfers between devices: none -> 102 us  [swap_with(): return lax.ppermute(array, AXES, pairs)]
    ppermute x0 -> x46, starting transfers between devices: none -> 63.3 us  [swap_with(): return lax.ppermute(array, AXES, pairs)]
    all_gather x1 -> x0, blocking collectives: 44 us -> none  [shards(): vecs = lax.all_gather(vectors.astype(BF16), AXES, axis=1, tiled=True)]
    psum x1 -> x0, blocking collectives: 37.2 us -> none  [shards(): small = lax.psum(small, AXES)]
    all_gather x1 -> x0, waiting for transfers between devices: 36.7 us -> none  [shards(): stacked = lax.all_gather(weights.astype(BF16), AXES, axis=0, tiled=True)]
    pallas_call x3 -> x6, Pallas kernels: 101 us -> 122 us  [the longest x1 48.4 us: device_grads(): pl.pallas_call(partial(deep_kernel, count, number), out_shape=(shape((ROW...]
    convert_element_type x2, other arithmetic: 16.8 us -> 1.12 us  [the longest x1 1.12 us: shards(): weights_low = weights.astype(BF16)]
  transfers between devices with their start and end apart: 2 -> 46, of which waited for: 2 -> 22; matrix products, arithmetic and copies ran while one was open for 2% -> 5% of each run, Pallas kernels for 0% -> 10%
where the time goes in v2:
time: 318 us
  Pallas kernels  122 us (38%)
  waiting for transfers between devices  102 us (32%)
  starting transfers between devices  63.3 us (20%)
  local copies, waits for them, and re-layouts  14.9 us (5%)
  other arithmetic  9.97 us (3%)
  between operations  5.47 us (2%)
    ppermute x46, waiting for transfers between devices, swap_with(): return lax.ppermute(array, AXES, pairs)  102 us
    ppermute x46, starting transfers between devices, swap_with(): return lax.ppermute(array, AXES, pairs)  63.3 us
    pallas_call x1, Pallas kernels, device_grads(): pl.pallas_call(partial(deep_kernel, count, number), out_shape=(shape((ROW...  48.4 us
    pallas_call x1, Pallas kernels, device_grads(): pl.pallas_call(partial(attend_back_kernel, short_len, slots, number), out...  33.2 us
    pallas_call x1, Pallas kernels, device_grads(): pl.pallas_call(partial(attend_kernel, short_len, slots, number), out_shap...  25.1 us
    pallas_call x1, Pallas kernels, scatter_sum(): pl.pallas_call(core_sum_kernel, out_shape=(shape((8 * SCATTER_CUT + 64, q...  9.28 us
  transfers between devices with their start and end apart: 46, of which 22 were waited for; matrix products, arithmetic and copies ran while one was open for 5% of the time, Pallas kernels for 10%

profile of v2, /device:TPU:0, one launch (start us, length us, event | category | flops | bytes accessed | tf_op | source)
XLA Modules:
  0.0 317.5 jit_solution(8138572520366055862)
XLA Ops:
  1.8 4.0 %collective-permute-start.13 = (bf16[96,512]{1,0:T(8,128)(2,1)S(1)}, bf16[96,512]{1,0:T(8,128)(2,1)S(1)}, u32[]{:S(2)}, u32[]{:S(2)}) collective-permute-start(bf16[96,512]{1,0:T(8,128)(2,1)S(1)} %slice.43), channel_id=1, source_target_pairs={{0,24},{1,25},{2,26},{3,27},{4,28},{5,29},{6,30},{7,31},{8,16},{9,... | collective-permute-start | bytes 294920 | tf_op jit(solution)/shard_map/ppermute | solution.py:751
  6.4 2.5 collective-permute-done.13
  9.0 1.7 collective-permute-done.12
  11.1 3.7 %collective-permute-start.7 = (bf16[208,512]{1,0:T(8,128)(2,1)S(1)}, bf16[208,512]{1,0:T(8,128)(2,1)S(1)}, u32[]{:S(2)}, u32[]{:S(2)}) collective-permute-start(bf16[208,512]{1,0:T(8,128)(2,1)S(1)} %slice.42), channel_id=1, source_target_pairs={{0,6},{1,7},{2,4},{3,5},{4,2},{5,3},{6,0},{7,1},{8,14},{9,15},{10,... | collective-permute-start | bytes 638984 | tf_op jit(solution)/shard_map/ppermute | solution.py:751
  17.2 1.5 collective-permute-start.1
  18.7 2.2 collective-permute-done.1
  20.9 1.4 collective-permute-start.2
  22.3 2.2 collective-permute-done.2
  24.6 1.4 collective-permute-start.3
  26.0 7.6 %collective-permute-done.6 = bf16[208,512]{1,0:T(8,128)(2,1)S(1)} collective-permute-done((bf16[208,512]{1,0:T(8,128)(2,1)S(1)}, bf16[208,512]{1,0:T(8,128)(2,1)S(1)}, u32[]{:S(2)}, u32[]{:S(2)}) %collective-permute-start.6) | collective-permute-done | bytes 213024 | tf_op jit(solution)/shard_map/ppermute | solution.py:751
  33.6 1.7 collective-permute-start.10
  35.3 1.3 collective-permute-start.9
  37.2 4.5 %collective-permute-done.4 = bf16[8,512]{1,0:T(8,128)(2,1)S(1)} collective-permute-done((bf16[8,512]{1,0:T(8,128)(2,1)S(1)}, bf16[8,512]{1,0:T(8,128)(2,1)S(1)}, u32[]{:S(2)}, u32[]{:S(2)}) %collective-permute-start.4) | collective-permute-done | bytes 8224 | tf_op jit(solution)/shard_map/ppermute | solution.py:751
  41.8 2.6 collective-permute-start.16
  44.5 11.2 %collective-permute-done.16.refs_7_ = bf16[384,512]{1,0:T(8,128)(2,1)S(1)} collective-permute-done((bf16[384,512]{1,0:T(8,128)(2,1)S(1)}, bf16[384,512]{1,0:T(8,128)(2,1)S(1)}, u32[]{:S(2)}, u32[]{:S(2)}) %collective-permute-start.16) | collective-permute-done | bytes 393248 | tf_op jit(solution)/shard_map/ppermute | solution.py:751
  55.7 14.5 %collective-permute-start.14 = (bf16[384,512]{1,0:T(8,128)(2,1)S(1)}, bf16[384,512]{1,0:T(8,128)(2,1)S(1)}, u32[]{:S(2)}, u32[]{:S(2)}) collective-permute-start(bf16[384,512]{1,0:T(8,128)(2,1)S(1)} %pad_maximum_fusion.1.refs_4_), channel_id=1, source_target_pairs={{0,2},{1,3},{2,0},{3,1},{4,6},{5,7},{6,4},{7,5},{8,10},{9,11},{10,... | collective-permute-start | bytes 1179656 | tf_op jit(solution)/shard_map/ppermute | solution.py:751
  70.2 6.0 %collective-permute-done.15.refs_6_ = bf16[384,512]{1,0:T(8,128)(2,1)} collective-permute-done((bf16[384,512]{1,0:T(8,128)(2,1)S(1)}, bf16[384,512]{1,0:T(8,128)(2,1)}, u32[]{:S(2)}, u32[]{:S(2)}) %collective-permute-start.15) | collective-permute-done | bytes 393248 | tf_op jit(solution)/shard_map/ppermute | solution.py:751
  76.2 6.9 %collective-permute-done.14.refs_5_ = bf16[384,512]{1,0:T(8,128)(2,1)S(1)} collective-permute-done((bf16[384,512]{1,0:T(8,128)(2,1)S(1)}, bf16[384,512]{1,0:T(8,128)(2,1)S(1)}, u32[]{:S(2)}, u32[]{:S(2)}) %collective-permute-start.14) | collective-permute-done | bytes 393248 | tf_op jit(solution)/shard_map/ppermute | solution.py:751
  91.8 1.4 copy.27
  95.2 25.1 %attend.1 = (bf16[768,1536]{1,0:T(8,128)(2,1)}, f32[768,512]{1,0:T(8,128)}, bf16[768,512]{1,0:T(8,128)(2,1)}, bf16[768,1536]{1,0:T(8,128)(2,1)}, f32[2,8,1,384]{...) custom-call(s32[4]{0:T(128)} %pad_add_fusion.1.coords_ref, s32[2]{0:T(128)} %bitcast.29, ...), custom_call_target="tpu_custom_call" | custom-call | tf_op jit(solution)/shard_map/attend/pallas_call | solution.py:665
  120.3 48.4 %deep.1 = (bf16[5888,256]{1,0:T(8,128)(2,1)}, bf16[5888,256]{1,0:T(8,128)(2,1)}, f32[256,512]{1,0:T(8,128)}, f32[768,512]{1,0:T(8,128)}, f32[8,512]{1,0:T(8,128)}) custom-call(s32[4]{0:T(128)} %pad_add_fusion.1.coords_ref, s32[3,768,3]{2,1,0:T(8,128)} %bitcast.23, s32[16,768]{1,0:T(8,128)} %get-tuple-element.89.lines_ref, ...), custom_call_target="tpu_custom_call" | custom-call | tf_op jit(solution)/shard_map/deep/pallas_call | solution.py:688
  168.9 33.2 %attend_back.1 = (bf16[3840,256]{1,0:T(8,128)(2,1)}, bf16[3872,256]{1,0:T(8,128)(2,1)}, f32[8,512]{1,0:T(8,128)}) custom-call(s32[4]{0:T(128)} %pad_add_fusion.1.coords_ref, s32[2]{0:T(128)} %bitcast.30, f32[8]{0:T(128)} %multiply_power_fusion.slope_ref, s32[16,768]{1,0:T(8,128)} %get-tuple-element.89.lines_ref, f32[8,512]{1,0:T(8,128)} %select_convert_fusion.vec_ref, ...), custom_call_target="tpu_custom_call" | custom-call | flops 12999999488 | bytes 20000000 | tf_op jit(solution)/shard_map/attend_back/pallas_call | solution.py:720
  202.5 3.8 %collective-permute-done.25.recv_front = bf16[3872,256]{1,0:T(8,128)(2,1)S(1)} collective-permute-done((bf16[3872,256]{1,0:T(8,128)(2,1)}, bf16[3872,256]{1,0:T(8,128)(2,1)S(1)}, u32[]{:S(2)}, u32[]{:S(2)}) %collective-permute-start.25) | collective-permute-done | bytes 1982496 | tf_op jit(solution)/shard_map/ppermute | solution.py:751
  206.4 1.3 copy-done.6
  208.6 9.3 %core_sum.1 = (bf16[3264,128]{1,0:T(8,128)(2,1)}, bf16[3264,128]{1,0:T(8,128)(2,1)}, bf16[3264,128]{1,0:T(8,128)(2,1)}, bf16[3264,128]{1,0:T(8,128)(2,1)}, bf16[...) custom-call(s32[4]{0:T(128)} %pad_add_fusion.1.coords_ref, ...), custom_call_target="tpu_custom_call" | custom-call | tf_op jit(solution)/shard_map/core_sum/pallas_call | solution.py:781
  218.0 1.5 collective-permute-start.27
  220.3 1.3 collective-permute-start.29
  221.6 1.4 collective-permute-start.31
  222.9 12.1 %collective-permute-done.30.q1 = bf16[1664,128]{1,0:T(8,128)(2,1)S(1)} collective-permute-done((bf16[1664,128]{1,0:T(8,128)(2,1)}, bf16[1664,128]{1,0:T(8,128)(2,1)S(1)}, u32[]{:S(2)}, u32[]{:S(2)}) %collective-permute-start.30) | collective-permute-done | bytes 426016 | tf_op jit(solution)/shard_map/ppermute | solution.py:751
  235.0 2.4 collective-permute-start.32
  237.4 16.3 %collective-permute-done.31.q2 = bf16[1664,128]{1,0:T(8,128)(2,1)S(1)} collective-permute-done((bf16[1664,128]{1,0:T(8,128)(2,1)}, bf16[1664,128]{1,0:T(8,128)(2,1)S(1)}, u32[]{:S(2)}, u32[]{:S(2)}) %collective-permute-start.31) | collective-permute-done | bytes 426016 | tf_op jit(solution)/shard_map/ppermute | solution.py:751
  253.7 4.5 %collective-permute-done.28.p2 = bf16[3264,128]{1,0:T(8,128)(2,1)S(1)} collective-permute-done((bf16[3264,128]{1,0:T(8,128)(2,1)}, bf16[3264,128]{1,0:T(8,128)(2,1)S(1)}, u32[]{:S(2)}, u32[]{:S(2)}) %collective-permute-start.28) | collective-permute-done | bytes 835616 | tf_op jit(solution)/shard_map/ppermute | solution.py:751
  259.4 4.0 %first_sum.1 = (bf16[864,128]{1,0:T(8,128)(2,1)}, bf16[864,128]{1,0:T(8,128)(2,1)}, bf16[864,128]{1,0:T(8,128)(2,1)}, bf16[864,128]{1,0:T(8,128)(2,1)}, bf16[416...) custom-call(s32[4]{0:T(128)} %pad_add_fusion.1.coords_ref, ...), custom_call_target="tpu_custom_call" | custom-call | tf_op jit(solution)/shard_map/first_sum/pallas_call | solution.py:796
  263.4 4.1 %collective-permute-start.33 = (bf16[864,128]{1,0:T(8,128)(2,1)}, bf16[864,128]{1,0:T(8,128)(2,1)S(1)}, u32[]{:S(2)}, u32[]{:S(2)}) collective-permute-start(bf16[864,128]{1,0:T(8,128)(2,1)} %get-tuple-element.67), channel_id=1, source_target_pairs={{0,2},{1,3},{2,0},{3,1},{4,6},{5,7},{6,4},{7,5},{8,10},{9,11},{10,... | collective-permute-start | bytes 663560 | tf_op jit(solution)/shard_map/ppermute | solution.py:751
  267.5 2.4 collective-permute-start.35
  269.9 1.5 collective-permute-start.36
  272.1 2.7 collective-permute-done.36.t1
  274.8 1.6 collective-permute-start.38
  277.4 3.2 %collective-permute-done.38.t3 = bf16[416,128]{1,0:T(8,128)(2,1)S(1)} collective-permute-done((bf16[416,128]{1,0:T(8,128)(2,1)}, bf16[416,128]{1,0:T(8,128)(2,1)S(1)}, u32[]{:S(2)}, u32[]{:S(2)}) %collective-permute-start.38) | collective-permute-done | bytes 106528 | tf_op jit(solution)/shard_map/ppermute | solution.py:751
  280.6 5.0 %collective-permute-done.34.s2 = bf16[864,128]{1,0:T(8,128)(2,1)S(1)} collective-permute-done((bf16[864,128]{1,0:T(8,128)(2,1)}, bf16[864,128]{1,0:T(8,128)(2,1)S(1)}, u32[]{:S(2)}, u32[]{:S(2)}) %collective-permute-start.34) | collective-permute-done | bytes 221216 | tf_op jit(solution)/shard_map/ppermute | solution.py:751
  286.4 2.3 last_sum.1
  290.8 1.5 collective-permute-start.44
  294.1 2.5 collective-permute-done.40
  298.5 2.5 collective-permute-done.41
  301.0 3.3 %collective-permute-start.42 = (f32[8,128]{1,0:T(8,128)S(1)}, f32[8,128]{1,0:T(8,128)S(1)}, u32[]{:S(2)}, u32[]{:S(2)}) collective-permute-start(f32[8,128]{1,0:T(8,128)S(1)} %add.121), channel_id=1, source_target_pairs={{0,2},{1,3},{2,0},{3,1},{4,6},{5,7},{6,4},{7,5},{8,10},{9,11},{10,... | collective-permute-start | bytes 12296 | tf_op jit(solution)/shard_map/ppermute | solution.py:751
  304.3 1.6 collective-permute-done.42
  305.9 1.9 collective-permute-start.43
  313.7 1.6 add_multiply_fusion
  (168 shorter events, 31.3 us)
Async XLA Ops:
  1.8 74.4 %copy-start.31 = (s32[2,1]{0,1:T(1,128)S(1)}, s32[2,1]{0,1:T(1,128)}, u32[]{:S(2)}) copy-start(s32[2,1]{0,1:T(1,128)} %param.9) | copy-start | bytes 28
  1.8 7.1 %collective-permute-start.13 = (bf16[96,512]{1,0:T(8,128)(2,1)S(1)}, bf16[96,512]{1,0:T(8,128)(2,1)S(1)}, u32[]{:S(2)}, u32[]{:S(2)}) collective-permute-start(bf16[96,512]{1,0:T(8,128)(2,1)S(1)} %slice.43), channel_id=1, source_target_pairs={{0,24},{1,25},{2,26},{3,27},{4,28},{5,29},{6,30},{7,31},{8,16},{9,... | collective-permute-start | bytes 294920 | tf_op jit(solution)/shard_map/ppermute | solution.py:751
  5.8 4.9 %collective-permute-start.12 = (bf16[96,512]{1,0:T(8,128)(2,1)S(1)}, bf16[96,512]{1,0:T(8,128)(2,1)S(1)}, u32[]{:S(2)}, u32[]{:S(2)}) collective-permute-start(bf16[96,512]{1,0:T(8,128)(2,1)S(1)} %slice.43), channel_id=1, source_target_pairs={{0,16},{1,17},{2,18},{3,19},{4,20},{5,21},{6,22},{7,23},{8,24},{9,... | collective-permute-start | bytes 294920 | tf_op jit(solution)/shard_map/ppermute | solution.py:751
  6.3 4.7 %collective-permute-start.11 = (bf16[96,512]{1,0:T(8,128)(2,1)S(1)}, bf16[96,512]{1,0:T(8,128)(2,1)S(1)}, u32[]{:S(2)}, u32[]{:S(2)}) collective-permute-start(bf16[96,512]{1,0:T(8,128)(2,1)S(1)} %slice.43), channel_id=1, source_target_pairs={{0,8},{1,9},{2,10},{3,11},{4,12},{5,13},{6,14},{7,15},{8,0},{9,1},... | collective-permute-start | bytes 294920 | tf_op jit(solution)/shard_map/ppermute | solution.py:751
  11.0 76.5 %copy-start.1 = (bf16[384,512]{1,0:T(8,128)(2,1)}, bf16[384,512]{1,0:T(8,128)(2,1)S(1)}, u32[]{:S(2)}) copy-start(bf16[384,512]{1,0:T(8,128)(2,1)S(1)} %pad_maximum_fusion.1.refs_4_) | copy-start | bytes 1179652
  11.0 33.3 %collective-permute-start.21 = (bf16[384,512]{1,0:T(8,128)(2,1)S(1)}, bf16[384,512]{1,0:T(8,128)(2,1)S(1)}, u32[]{:S(2)}, u32[]{:S(2)}) collective-permute-start(bf16[384,512]{1,0:T(8,128)(2,1)S(1)} %pad_maximum_fusion.1.refs_4_), channel_id=1, source_target_pairs={{0,1},{1,0},{2,3},{3,2},{4,5},{5,4},{6,7},{7,6},{8,9},{9,8},{10,11... | collective-permute-start | bytes 1179656 | tf_op jit(solution)/shard_map/ppermute | solution.py:751
  11.1 14.8 %collective-permute-start.7 = (bf16[208,512]{1,0:T(8,128)(2,1)S(1)}, bf16[208,512]{1,0:T(8,128)(2,1)S(1)}, u32[]{:S(2)}, u32[]{:S(2)}) collective-permute-start(bf16[208,512]{1,0:T(8,128)(2,1)S(1)} %slice.42), channel_id=1, source_target_pairs={{0,6},{1,7},{2,4},{3,5},{4,2},{5,3},{6,0},{7,1},{8,14},{9,15},{10,... | collective-permute-start | bytes 638984 | tf_op jit(solution)/shard_map/ppermute | solution.py:751
  14.8 18.8 %collective-permute-start.6 = (bf16[208,512]{1,0:T(8,128)(2,1)S(1)}, bf16[208,512]{1,0:T(8,128)(2,1)S(1)}, u32[]{:S(2)}, u32[]{:S(2)}) collective-permute-start(bf16[208,512]{1,0:T(8,128)(2,1)S(1)} %slice.42), channel_id=1, source_target_pairs={{0,4},{1,5},{2,6},{3,7},{4,0},{5,1},{6,2},{7,3},{8,12},{9,13},{10,... | collective-permute-start | bytes 638984 | tf_op jit(solution)/shard_map/ppermute | solution.py:751
  14.8 18.8 %collective-permute-start.5 = (bf16[208,512]{1,0:T(8,128)(2,1)S(1)}, bf16[208,512]{1,0:T(8,128)(2,1)S(1)}, u32[]{:S(2)}, u32[]{:S(2)}) collective-permute-start(bf16[208,512]{1,0:T(8,128)(2,1)S(1)} %slice.42), channel_id=1, source_target_pairs={{0,2},{1,3},{2,0},{3,1},{4,6},{5,7},{6,4},{7,5},{8,10},{9,11},{10,... | collective-permute-start | bytes 638984 | tf_op jit(solution)/shard_map/ppermute | solution.py:751
  15.8 1.2 collective-permute-start
  17.2 3.7 %collective-permute-start.1 = (bf16[8,512]{1,0:T(8,128)(2,1)S(1)}, bf16[8,512]{1,0:T(8,128)(2,1)S(1)}, u32[]{:S(2)}, u32[]{:S(2)}) collective-permute-start(bf16[8,512]{1,0:T(8,128)(2,1)S(1)} %add.114), channel_id=1, source_target_pairs={{0,8},{1,9},{2,10},{3,11},{4,12},{5,13},{6,14},{7,15},{8,0},{9,1},... | collective-permute-start | bytes 24584 | tf_op jit(solution)/shard_map/ppermute | solution.py:751
  20.9 3.7 %collective-permute-start.2 = (bf16[8,512]{1,0:T(8,128)(2,1)S(1)}, bf16[8,512]{1,0:T(8,128)(2,1)S(1)}, u32[]{:S(2)}, u32[]{:S(2)}) collective-permute-start(bf16[8,512]{1,0:T(8,128)(2,1)S(1)} %add.115), channel_id=1, source_target_pairs={{0,16},{1,17},{2,18},{3,19},{4,20},{5,21},{6,22},{7,23},{8,24},{9,... | collective-permute-start | bytes 24584 | tf_op jit(solution)/shard_map/ppermute | solution.py:751
  24.6 12.6 %collective-permute-start.3 = (bf16[8,512]{1,0:T(8,128)(2,1)S(1)}, bf16[8,512]{1,0:T(8,128)(2,1)S(1)}, u32[]{:S(2)}, u32[]{:S(2)}) collective-permute-start(bf16[8,512]{1,0:T(8,128)(2,1)S(1)} %add.116), channel_id=1, source_target_pairs={{0,2},{1,3},{2,0},{3,1},{4,6},{5,7},{6,4},{7,5},{8,10},{9,11},{10,... | collective-permute-start | bytes 24584 | tf_op jit(solution)/shard_map/ppermute | solution.py:751
  33.6 50.0 %collective-permute-start.10 = (bf16[832,512]{1,0:T(8,128)(2,1)S(1)}, bf16[832,512]{1,0:T(8,128)(2,1)S(1)}, u32[]{:S(2)}, u32[]{:S(2)}) collective-permute-start(bf16[832,512]{1,0:T(8,128)(2,1)S(1)} %pad_maximum_fusion.refs_0_), channel_id=1, source_target_pairs={{0,24},{1,25},{2,26},{3,27},{4,28},{5,29},{6,30},{7,31},{8,16},{9,... | collective-permute-start | bytes 2555912 | tf_op jit(solution)/shard_map/ppermute | solution.py:751
  35.3 48.4 %collective-permute-start.9 = (bf16[832,512]{1,0:T(8,128)(2,1)S(1)}, bf16[832,512]{1,0:T(8,128)(2,1)S(1)}, u32[]{:S(2)}, u32[]{:S(2)}) collective-permute-start(bf16[832,512]{1,0:T(8,128)(2,1)S(1)} %pad_maximum_fusion.refs_0_), channel_id=1, source_target_pairs={{0,16},{1,17},{2,18},{3,19},{4,20},{5,21},{6,22},{7,23},{8,24},{9,... | collective-permute-start | bytes 2555912 | tf_op jit(solution)/shard_map/ppermute | solution.py:751
  36.6 47.5 %collective-permute-start.8 = (bf16[832,512]{1,0:T(8,128)(2,1)S(1)}, bf16[832,512]{1,0:T(8,128)(2,1)}, u32[]{:S(2)}, u32[]{:S(2)}) collective-permute-start(bf16[832,512]{1,0:T(8,128)(2,1)S(1)} %pad_maximum_fusion.refs_0_), channel_id=1, source_target_pairs={{0,8},{1,9},{2,10},{3,11},{4,12},{5,13},{6,14},{7,15},{8,0},{9,1},... | collective-permute-start | bytes 2555912 | tf_op jit(solution)/shard_map/ppermute | solution.py:751
  37.2 4.6 %collective-permute-start.4 = (bf16[8,512]{1,0:T(8,128)(2,1)S(1)}, bf16[8,512]{1,0:T(8,128)(2,1)S(1)}, u32[]{:S(2)}, u32[]{:S(2)}) collective-permute-start(bf16[8,512]{1,0:T(8,128)(2,1)S(1)} %add.117), channel_id=1, source_target_pairs={{0,4},{1,5},{2,6},{3,7},{4,0},{5,1},{6,2},{7,3},{8,12},{9,13},{10,... | collective-permute-start | bytes 24584 | tf_op jit(solution)/shard_map/ppermute | solution.py:751
  41.8 13.9 %collective-permute-start.16 = (bf16[384,512]{1,0:T(8,128)(2,1)S(1)}, bf16[384,512]{1,0:T(8,128)(2,1)S(1)}, u32[]{:S(2)}, u32[]{:S(2)}) collective-permute-start(bf16[384,512]{1,0:T(8,128)(2,1)S(1)} %pad_maximum_fusion.1.refs_4_), channel_id=1, source_target_pairs={{0,6},{1,7},{2,4},{3,5},{4,2},{5,3},{6,0},{7,1},{8,14},{9,15},{10,... | collective-permute-start | bytes 1179656 | tf_op jit(solution)/shard_map/ppermute | solution.py:751
  44.4 31.8 %collective-permute-start.15 = (bf16[384,512]{1,0:T(8,128)(2,1)S(1)}, bf16[384,512]{1,0:T(8,128)(2,1)}, u32[]{:S(2)}, u32[]{:S(2)}) collective-permute-start(bf16[384,512]{1,0:T(8,128)(2,1)S(1)} %pad_maximum_fusion.1.refs_4_), channel_id=1, source_target_pairs={{0,4},{1,5},{2,6},{3,7},{4,0},{5,1},{6,2},{7,3},{8,12},{9,13},{10,... | collective-permute-start | bytes 1179656 | tf_op jit(solution)/shard_map/ppermute | solution.py:751
  55.7 27.4 %collective-permute-start.14 = (bf16[384,512]{1,0:T(8,128)(2,1)S(1)}, bf16[384,512]{1,0:T(8,128)(2,1)S(1)}, u32[]{:S(2)}, u32[]{:S(2)}) collective-permute-start(bf16[384,512]{1,0:T(8,128)(2,1)S(1)} %pad_maximum_fusion.1.refs_4_), channel_id=1, source_target_pairs={{0,2},{1,3},{2,0},{3,1},{4,6},{5,7},{6,4},{7,5},{8,10},{9,11},{10,... | collective-permute-start | bytes 1179656 | tf_op jit(solution)/shard_map/ppermute | solution.py:751
  76.1 6.9 %collective-permute-start.24 = (bf16[384,512]{1,0:T(8,128)(2,1)S(1)}, bf16[384,512]{1,0:T(8,128)(2,1)S(1)}, u32[]{:S(2)}, u32[]{:S(2)}) collective-permute-start(bf16[384,512]{1,0:T(8,128)(2,1)S(1)} %collective-permute-done.16.refs_7_), channel_id=1, source_target_pairs={{0,1},{1,0},{2,3},{3,2},{4,5},{5,4},{6,7},{7,6},{8,9},{9,8},{10,11... | collective-permute-start | bytes 1179656 | tf_op jit(solution)/shard_map/ppermute | solution.py:751
  83.1 11.4 %collective-permute-start.17 = (bf16[832,512]{1,0:T(8,128)(2,1)S(1)}, bf16[832,512]{1,0:T(8,128)(2,1)}, u32[]{:S(2)}, u32[]{:S(2)}) collective-permute-start(bf16[832,512]{1,0:T(8,128)(2,1)S(1)} %pad_maximum_fusion.refs_0_), channel_id=1, source_target_pairs={{0,1},{1,0},{2,3},{3,2},{4,5},{5,4},{6,7},{7,6},{8,9},{9,8},{10,11... | collective-permute-start | bytes 2555912 | tf_op jit(solution)/shard_map/ppermute | solution.py:751
  83.1 6.8 %collective-permute-start.23 = (bf16[384,512]{1,0:T(8,128)(2,1)}, bf16[384,512]{1,0:T(8,128)(2,1)}, u32[]{:S(2)}, u32[]{:S(2)}) collective-permute-start(bf16[384,512]{1,0:T(8,128)(2,1)} %collective-permute-done.15.refs_6_), channel_id=1, source_target_pairs={{0,1},{1,0},{2,3},{3,2},{4,5},{5,4},{6,7},{7,6},{8,9},{9,8},{10,11... | collective-permute-start | bytes 1179656 | tf_op jit(solution)/shard_map/ppermute | solution.py:751
  83.6 10.9 %collective-permute-start.20 = (bf16[832,512]{1,0:T(8,128)(2,1)S(1)}, bf16[832,512]{1,0:T(8,128)(2,1)}, u32[]{:S(2)}, u32[]{:S(2)}) collective-permute-start(bf16[832,512]{1,0:T(8,128)(2,1)S(1)} %collective-permute-done.10.refs_3_), channel_id=1, source_target_pairs={{0,1},{1,0},{2,3},{3,2},{4,5},{5,4},{6,7},{7,6},{8,9},{9,8},{10,11... | collective-permute-start | bytes 2555912 | tf_op jit(solution)/shard_map/ppermute | solution.py:751
  83.7 10.8 %collective-permute-start.19 = (bf16[832,512]{1,0:T(8,128)(2,1)S(1)}, bf16[832,512]{1,0:T(8,128)(2,1)}, u32[]{:S(2)}, u32[]{:S(2)}) collective-permute-start(bf16[832,512]{1,0:T(8,128)(2,1)S(1)} %collective-permute-done.9.refs_2_), channel_id=1, source_target_pairs={{0,1},{1,0},{2,3},{3,2},{4,5},{5,4},{6,7},{7,6},{8,9},{9,8},{10,11... | collective-permute-start | bytes 2555912 | tf_op jit(solution)/shard_map/ppermute | solution.py:751
  84.1 10.4 %collective-permute-start.18 = (bf16[832,512]{1,0:T(8,128)(2,1)}, bf16[832,512]{1,0:T(8,128)(2,1)}, u32[]{:S(2)}, u32[]{:S(2)}) collective-permute-start(bf16[832,512]{1,0:T(8,128)(2,1)} %collective-permute-done.8.refs_1_), channel_id=1, source_target_pairs={{0,1},{1,0},{2,3},{3,2},{4,5},{5,4},{6,7},{7,6},{8,9},{9,8},{10,11... | collective-permute-start | bytes 2555912 | tf_op jit(solution)/shard_map/ppermute | solution.py:751
  89.9 4.6 %collective-permute-start.22 = (bf16[384,512]{1,0:T(8,128)(2,1)}, bf16[384,512]{1,0:T(8,128)(2,1)S(1)}, u32[]{:S(2)}, u32[]{:S(2)}) collective-permute-start(bf16[384,512]{1,0:T(8,128)(2,1)} %copy-done.9), channel_id=1, source_target_pairs={{0,1},{1,0},{2,3},{3,2},{4,5},{5,4},{6,7},{7,6},{8,9},{9,8},{10,11... | collective-permute-start | bytes 1179656 | tf_op jit(solution)/shard_map/ppermute | solution.py:751
  168.7 37.7 %collective-permute-start.26 = (bf16[5888,256]{1,0:T(8,128)(2,1)}, bf16[5888,256]{1,0:T(8,128)(2,1)S(1)}, u32[]{:S(2)}, u32[]{:S(2)}) collective-permute-start(bf16[5888,256]{1,0:T(8,128)(2,1)} %get-tuple-element.56), channel_id=1, source_target_pairs={{0,1},{1,0},{2,3},{3,2},{4,5},{5,4},{6,7},{7,6},{8,9},{9,8},{10,11... | collective-permute-start | bytes 9043976 | tf_op jit(solution)/shard_map/ppermute | solution.py:751
  202.1 4.3 %collective-permute-start.25 = (bf16[3872,256]{1,0:T(8,128)(2,1)}, bf16[3872,256]{1,0:T(8,128)(2,1)S(1)}, u32[]{:S(2)}, u32[]{:S(2)}) collective-permute-start(bf16[3872,256]{1,0:T(8,128)(2,1)} %get-tuple-element.55), channel_id=1, source_target_pairs={{0,1},{1,0},{2,3},{3,2},{4,5},{5,4},{6,7},{7,6},{8,9},{9,8},{10,11... | collective-permute-start | bytes 5947400 | tf_op jit(solution)/shard_map/ppermute | solution.py:751
  217.9 17.1 %collective-permute-start.30 = (bf16[1664,128]{1,0:T(8,128)(2,1)}, bf16[1664,128]{1,0:T(8,128)(2,1)S(1)}, u32[]{:S(2)}, u32[]{:S(2)}) collective-permute-start(bf16[1664,128]{1,0:T(8,128)(2,1)} %get-tuple-element.63), channel_id=1, source_target_pairs={{0,2},{1,3},{2,0},{3,1},{4,6},{5,7},{6,4},{7,5},{8,10},{9,11},{10,... | collective-permute-start | bytes 1277960 | tf_op jit(solution)/shard_map/ppermute | solution.py:751
  218.0 35.7 %collective-permute-start.27 = (bf16[3264,128]{1,0:T(8,128)(2,1)}, bf16[3264,128]{1,0:T(8,128)(2,1)S(1)}, u32[]{:S(2)}, u32[]{:S(2)}) collective-permute-start(bf16[3264,128]{1,0:T(8,128)(2,1)} %get-tuple-element.59), channel_id=1, source_target_pairs={{0,8},{1,9},{2,10},{3,11},{4,12},{5,13},{6,14},{7,15},{8,0},{9,1},... | collective-permute-start | bytes 2506760 | tf_op jit(solution)/shard_map/ppermute | solution.py:751
  219.5 38.7 %collective-permute-start.28 = (bf16[3264,128]{1,0:T(8,128)(2,1)}, bf16[3264,128]{1,0:T(8,128)(2,1)S(1)}, u32[]{:S(2)}, u32[]{:S(2)}) collective-permute-start(bf16[3264,128]{1,0:T(8,128)(2,1)} %get-tuple-element.60), channel_id=1, source_target_pairs={{0,16},{1,17},{2,18},{3,19},{4,20},{5,21},{6,22},{7,23},{8,24},{9,... | collective-permute-start | bytes 2506760 | tf_op jit(solution)/shard_map/ppermute | solution.py:751
  220.3 38.0 %collective-permute-start.29 = (bf16[3264,128]{1,0:T(8,128)(2,1)}, bf16[3264,128]{1,0:T(8,128)(2,1)S(1)}, u32[]{:S(2)}, u32[]{:S(2)}) collective-permute-start(bf16[3264,128]{1,0:T(8,128)(2,1)} %get-tuple-element.61), channel_id=1, source_target_pairs={{0,24},{1,25},{2,26},{3,27},{4,28},{5,29},{6,30},{7,31},{8,16},{9,... | collective-permute-start | bytes 2506760 | tf_op jit(solution)/shard_map/ppermute | solution.py:751
  221.6 32.1 %collective-permute-start.31 = (bf16[1664,128]{1,0:T(8,128)(2,1)}, bf16[1664,128]{1,0:T(8,128)(2,1)S(1)}, u32[]{:S(2)}, u32[]{:S(2)}) collective-permute-start(bf16[1664,128]{1,0:T(8,128)(2,1)} %get-tuple-element.64), channel_id=1, source_target_pairs={{0,4},{1,5},{2,6},{3,7},{4,0},{5,1},{6,2},{7,3},{8,12},{9,13},{10,... | collective-permute-start | bytes 1277960 | tf_op jit(solution)/shard_map/ppermute | solution.py:751
  235.0 18.7 %collective-permute-start.32 = (bf16[1664,128]{1,0:T(8,128)(2,1)}, bf16[1664,128]{1,0:T(8,128)(2,1)S(1)}, u32[]{:S(2)}, u32[]{:S(2)}) collective-permute-start(bf16[1664,128]{1,0:T(8,128)(2,1)} %get-tuple-element.65), channel_id=1, source_target_pairs={{0,6},{1,7},{2,4},{3,5},{4,2},{5,3},{6,0},{7,1},{8,14},{9,15},{10,... | collective-permute-start | bytes 1277960 | tf_op jit(solution)/shard_map/ppermute | solution.py:751
  263.4 17.2 %collective-permute-start.33 = (bf16[864,128]{1,0:T(8,128)(2,1)}, bf16[864,128]{1,0:T(8,128)(2,1)S(1)}, u32[]{:S(2)}, u32[]{:S(2)}) collective-permute-start(bf16[864,128]{1,0:T(8,128)(2,1)} %get-tuple-element.67), channel_id=1, source_target_pairs={{0,2},{1,3},{2,0},{3,1},{4,6},{5,7},{6,4},{7,5},{8,10},{9,11},{10,... | collective-permute-start | bytes 663560 | tf_op jit(solution)/shard_map/ppermute | solution.py:751
  267.5 18.2 %collective-permute-start.34 = (bf16[864,128]{1,0:T(8,128)(2,1)}, bf16[864,128]{1,0:T(8,128)(2,1)S(1)}, u32[]{:S(2)}, u32[]{:S(2)}) collective-permute-start(bf16[864,128]{1,0:T(8,128)(2,1)} %get-tuple-element.68), channel_id=1, source_target_pairs={{0,4},{1,5},{2,6},{3,7},{4,0},{5,1},{6,2},{7,3},{8,12},{9,13},{10,... | collective-permute-start | bytes 663560 | tf_op jit(solution)/shard_map/ppermute | solution.py:751
  267.5 18.2 %collective-permute-start.35 = (bf16[864,128]{1,0:T(8,128)(2,1)}, bf16[864,128]{1,0:T(8,128)(2,1)S(1)}, u32[]{:S(2)}, u32[]{:S(2)}) collective-permute-start(bf16[864,128]{1,0:T(8,128)(2,1)} %get-tuple-element.69), channel_id=1, source_target_pairs={{0,6},{1,7},{2,4},{3,5},{4,2},{5,3},{6,0},{7,1},{8,14},{9,15},{10,... | collective-permute-start | bytes 663560 | tf_op jit(solution)/shard_map/ppermute | solution.py:751
  269.9 4.9 %collective-permute-start.36 = (bf16[416,128]{1,0:T(8,128)(2,1)}, bf16[416,128]{1,0:T(8,128)(2,1)S(1)}, u32[]{:S(2)}, u32[]{:S(2)}) collective-permute-start(bf16[416,128]{1,0:T(8,128)(2,1)} %get-tuple-element.71), channel_id=1, source_target_pairs={{0,8},{1,9},{2,10},{3,11},{4,12},{5,13},{6,14},{7,15},{8,0},{9,1},... | collective-permute-start | bytes 319496 | tf_op jit(solution)/shard_map/ppermute | solution.py:751
  271.4 6.1 %collective-permute-start.37 = (bf16[416,128]{1,0:T(8,128)(2,1)}, bf16[416,128]{1,0:T(8,128)(2,1)S(1)}, u32[]{:S(2)}, u32[]{:S(2)}) collective-permute-start(bf16[416,128]{1,0:T(8,128)(2,1)} %get-tuple-element.72), channel_id=1, source_target_pairs={{0,16},{1,17},{2,18},{3,19},{4,20},{5,21},{6,22},{7,23},{8,24},{9,... | collective-permute-start | bytes 319496 | tf_op jit(solution)/shard_map/ppermute | solution.py:751
  274.8 5.8 %collective-permute-start.38 = (bf16[416,128]{1,0:T(8,128)(2,1)}, bf16[416,128]{1,0:T(8,128)(2,1)S(1)}, u32[]{:S(2)}, u32[]{:S(2)}) collective-permute-start(bf16[416,128]{1,0:T(8,128)(2,1)} %get-tuple-element.73), channel_id=1, source_target_pairs={{0,24},{1,25},{2,26},{3,27},{4,28},{5,29},{6,30},{7,31},{8,16},{9,... | collective-permute-start | bytes 319496 | tf_op jit(solution)/shard_map/ppermute | solution.py:751
  290.7 1.6 collective-permute-start.39
  290.8 17.1 %collective-permute-start.44 = (f32[608,128]{1,0:T(8,128)}, f32[608,128]{1,0:T(8,128)S(1)}, u32[]{:S(2)}, u32[]{:S(2)}) collective-permute-start(f32[608,128]{1,0:T(8,128)} %get-tuple-element.77), channel_id=1, source_target_pairs={{0,16},{1,17},{2,18},{3,19},{4,20},{5,21},{6,22},{7,23},{8,24},{9,... | collective-permute-start | bytes 933896 | tf_op jit(solution)/shard_map/ppermute | solution.py:751
  293.0 3.7 %collective-permute-start.40 = (f32[8,128]{1,0:T(8,128)S(1)}, f32[8,128]{1,0:T(8,128)S(1)}, u32[]{:S(2)}, u32[]{:S(2)}) collective-permute-start(f32[8,128]{1,0:T(8,128)S(1)} %broadcast_add_fusion), channel_id=1, source_target_pairs={{0,8},{1,9},{2,10},{3,11},{4,12},{5,13},{6,14},{7,15},{8,0},{9,1},... | collective-permute-start | bytes 12296 | tf_op jit(solution)/shard_map/ppermute | solution.py:751
  297.3 3.7 %collective-permute-start.41 = (f32[8,128]{1,0:T(8,128)S(1)}, f32[8,128]{1,0:T(8,128)S(1)}, u32[]{:S(2)}, u32[]{:S(2)}) collective-permute-start(f32[8,128]{1,0:T(8,128)S(1)} %fusion.6), channel_id=1, source_target_pairs={{0,16},{1,17},{2,18},{3,19},{4,20},{5,21},{6,22},{7,23},{8,24},{9,... | collective-permute-start | bytes 12296 | tf_op jit(solution)/shard_map/ppermute | solution.py:751
  301.0 4.9 %collective-permute-start.42 = (f32[8,128]{1,0:T(8,128)S(1)}, f32[8,128]{1,0:T(8,128)S(1)}, u32[]{:S(2)}, u32[]{:S(2)}) collective-permute-start(f32[8,128]{1,0:T(8,128)S(1)} %add.121), channel_id=1, source_target_pairs={{0,2},{1,3},{2,0},{3,1},{4,6},{5,7},{6,4},{7,5},{8,10},{9,11},{10,... | collective-permute-start | bytes 12296 | tf_op jit(solution)/shard_map/ppermute | solution.py:751
  305.9 5.0 %collective-permute-start.43 = (f32[8,128]{1,0:T(8,128)S(1)}, f32[8,128]{1,0:T(8,128)S(1)}, u32[]{:S(2)}, u32[]{:S(2)}) collective-permute-start(f32[8,128]{1,0:T(8,128)S(1)} %add.122), channel_id=1, source_target_pairs={{0,4},{1,5},{2,6},{3,7},{4,0},{5,1},{6,2},{7,3},{8,12},{9,13},{10,... | collective-permute-start | bytes 12296 | tf_op jit(solution)/shard_map/ppermute | solution.py:751
  309.1 4.5 %collective-permute-start.45 = (f32[304,256]{1,0:T(8,128)S(1)}, f32[304,256]{1,0:T(8,128)S(1)}, u32[]{:S(2)}, u32[]{:S(2)}) collective-permute-start(f32[304,256]{1,0:T(8,128)S(1)} %broadcast_select_fusion.4), channel_id=1, source_target_pairs={{0,1},{1,0},{2,3},{3,2},{4,5},{5,4},{6,7},{7,6},{8,9},{9,8},{10,11... | collective-permute-start | bytes 933896 | tf_op jit(solution)/shard_map/ppermute | solution.py:751
  (31 other events, 380.9 us)

commit v3 on v2

--- a/solution.py
+++ b/solution.py
@@ -2,6 +2,7 @@
 
 import jax
 import jax.numpy as jnp
+import numpy as np
 from jax import lax
 from jax.experimental import pallas as pl
 from jax.experimental.pallas import tpu as pltpu
@@ -85,6 +86,17 @@
 
 def rows_of(index, size=BLOCK):
     return pl.ds(pl.multiple_of(index * size, size), size)
+
+
+def gathered_parts(coords_ref):
+    dp, z, core = coords_ref[0], coords_ref[1], coords_ref[2]
+    for side in range(2):
+        for k in range(4):
+            for part in range(4):
+                for kind in range(2):
+                    d, e = (k, part) if kind == 0 else (part, k)
+                    line = dp ^ d
+                    yield side * 8 + kind * 4 + k, part, kind, line // 2, (line % 2) * 8 + (z ^ e) * 2 + (core ^ side)
 
 
 class Fetch:
@@ -97,25 +109,18 @@
             )
             self.jobs.append((None, copy))
             return
-        dp, z, core = coords_ref[0], coords_ref[1], coords_ref[2]
-        shard = SHARD
-        first, last = low // shard, (high - 1) // shard
-        number = 0
-        for side in range(2):
-            for k in range(4):
-                for part in range(4):
-                    for kind, (begin, size) in enumerate(((0, GATHER_CUT), (GATHER_CUT, shard - GATHER_CUT))):
-                        d, e = (k, part) if kind == 0 else (part, k)
-                        owner = (dp ^ d) * 8 + (z ^ e) * 2 + (core ^ side)
-                        wanted = (owner >= first) & (owner <= last)
-                        place = jnp.where(wanted, owner * shard - base + begin, 0)
-                        copy = pltpu.make_async_copy(
-                            pieces[side * 8 + kind * 4 + k].at[pl.ds(part * size, size)],
-                            w_ref.at[pl.ds(pl.multiple_of(place, 16), size)],
-                            sems.at[number],
-                        )
-                        self.jobs.append((wanted, copy))
-                        number += 1
+        first, last = low // SHARD, (high - 1) // SHARD
+        half = D // 2
+        for number, (piece, part, kind, y, shard) in enumerate(gathered_parts(coords_ref)):
+            begin, size, step = ((0, GATHER_CUT, GATHER_CUT + 16), (GATHER_CUT, SHARD - GATHER_CUT, SHARD - GATHER_CUT))[kind]
+            wanted = (shard >= first) & (shard <= last)
+            place = jnp.where(wanted, shard * SHARD - base + begin, 0)
+            copy = pltpu.make_async_copy(
+                pieces[piece].at[pl.ds(part * step, size)],
+                w_ref.at[pl.ds(pl.multiple_of(place, 16), size), pl.ds(pl.multiple_of(y * half, half), half)],
+                sems.at[number],
+            )
+            self.jobs.append((wanted, copy))
 
     def start(self):
         for wanted, copy in self.jobs:
@@ -132,20 +137,66 @@
                 pl.when(wanted)(copy.wait)
 
 
-def attend_kernel(short_len, slots, pieces, coords_ref, lay_ref, slope_ref, cols_ref, vec_ref, *refs):
+def attend_kernel(short_len, slots, pieces, coords_ref, lay_ref, slope_ref, ids_ref, *refs):
     w_hbm, refs = refs[:pieces], refs[pieces:]
-    (shifted_ref, short_ref, normed_ref, qkv_ref, lse_ref, mixed_ref, resid_ref,
-     w_ref, dist_ref, mask_ref, lse_cols, sems) = refs
+    if pieces == 1:
+        vec_in_ref, refs = refs[0], refs[1:]
+    (shifted_ref, short_ref, normed_ref, qkv_ref, lse_ref, mixed_ref, resid_ref, lines_ref, cols_ref, vec_ref,
+     w_ref, dist_ref, mask_ref, lse_cols, part_ref, sems, part_sems) = refs
     rows = short_len * slots
     fetch = Fetch(w_hbm, coords_ref, w_ref, sems, 0, 0, ROW_F1)
     fetch.start()
+    copies = []
+    if pieces > 1:
+        for piece, part, kind, _, _ in gathered_parts(coords_ref):
+            if kind == 0:
+                place = pl.ds(part * (GATHER_CUT + 16) + GATHER_CUT, 16)
+                number = len(copies)
+                copies.append(
+                    pltpu.make_async_copy(w_hbm[piece].at[place], part_ref.at[number], part_sems.at[number])
+                )
+        for copy in copies:
+            copy.start()
+
+    ids = ids_ref[...]
+    group = lax.broadcasted_iota(jnp.int32, (1, rows), 1)
+    starts = group == 0
+    for slot in range(slots):
+        starts = starts | (group == slot * short_len)
+        starts = starts | ((group == slot * short_len + short_len // 2) & (lay_ref[slot] == 1))
+    ends = group == rows - 1
+    for slot in range(slots):
+        ends = ends | (group == (slot + 1) * short_len - 1)
+        ends = ends | ((group == slot * short_len + short_len // 2 - 1) & (lay_ref[slot] == 1))
+    before, after = pltpu.roll(ids, 1, 1), pltpu.roll(ids, rows - 1, 1)
+    own = [ids[j : j + 1] for j in range(POOL)]
+    back = [jnp.where(starts, -1, before[1:2]), jnp.where(starts, -1, before[2:3]), ids[0:1]]
+    ahead = [ids[1:2], ids[2:3], jnp.where(ends, -1, after[0:1])]
+    for j in range(POOL):
+        lines_ref[j : j + 1, :] = own[j]
+        lines_ref[POOL + j : POOL + j + 1, :] = back[j]
+        lines_ref[2 * POOL + j : 2 * POOL + j + 1, :] = ahead[j]
+    lines_ref[3 * POOL :, :] = jnp.zeros((16 - 3 * POOL, rows), jnp.int32)
+    turned = jnp.concatenate([lines_ref[...].astype(F32), jnp.zeros((112, rows), F32)], 0).T.astype(jnp.int32)
+    for j in range(POOL):
+        cols_ref[j] = pltpu.roll(turned, 128 - j, 1)
+
+    for copy in copies:
+        copy.wait()
+    if pieces > 1:
+        both = part_ref[0].astype(F32)
+        for k in range(1, len(copies)):
+            both = both + part_ref[k].astype(F32)
+        vec_ref[...] = jnp.concatenate([both[:8], both[8:]], 1)
+    else:
+        vec_ref[...] = vec_in_ref[...]
     fetch.wait()
     gain, offset = vec_ref[0:1, :], vec_ref[1:2, :]
 
     def pool_step(block, carry):
         at = rows_of(block)
         for j in range(POOL):
-            hot = one_hot_rows(cols_ref[at, POOL + j : POOL + j + 1])
+            hot = one_hot_rows(cols_ref[j, at, POOL : POOL + 1])
             shifted_ref[at, j * D : (j + 1) * D] = nn(hot, w_ref[ROW_E:ROW_P, :]).astype(BF16)
         short = nn(shifted_ref[at, :], w_ref[ROW_P:ROW_QKV, :])
         short_ref[at, :] = short
@@ -238,17 +289,34 @@
 
 def deep_kernel(count, pieces, coords_ref, cols_ref, lines_ref, vec_ref, resid_ref, *refs):
     w_hbm, refs = refs[:pieces], refs[pieces:]
+    if pieces > 1:
+        tail_hbm, refs = refs[0], refs[1:]
     (keep_ref, send_ref, table_ref, dresid_ref, small_ref,
      w_ref, e_ref, normed_ref, act_ref, slope_ref, deep_ref, final_ref, dlog_ref, dup_ref, low_ref,
-     ddeep_ref, dhid_ref, sums_ref, sems, e_sems) = refs
+     ddeep_ref, dhid_ref, sums_ref, sems, e_sems, tail_sems) = refs
     rows = resid_ref.shape[0]
     blocks = rows // BLOCK
     base = deep_base(pieces)
     core = coords_ref[2]
-    fetch = Fetch(w_hbm, coords_ref, w_ref, sems, base, ROW_F1, ROW_END)
-    fetch_e = Fetch(w_hbm, coords_ref, e_ref, e_sems, 0, 0, VOCAB)
-    fetch.start()
-    fetch_e.start()
+    fetches = [
+        Fetch(w_hbm, coords_ref, w_ref, sems, base, ROW_F1, ROW_END if pieces == 1 else ROW_END // 2),
+        Fetch(w_hbm, coords_ref, e_ref, e_sems, 0, 0, VOCAB),
+    ]
+    for fetch in fetches:
+        fetch.start()
+    copies = []
+    if pieces > 1:
+        half = ROW_END // 2
+        for y in range(2):
+            copies.append(
+                pltpu.make_async_copy(
+                    tail_hbm.at[pl.ds(y * half, half)],
+                    w_ref.at[pl.ds(half - base, half), pl.ds(y * (D // 2), D // 2)],
+                    tail_sems.at[y],
+                )
+            )
+    for copy in copies:
+        copy.start()
     f1, f2, up, head = ROW_F1 - base, ROW_F2 - base, ROW_U - base, ROW_H - base
     gain2, offset2 = vec_ref[2:3, :], vec_ref[3:4, :]
     gain_f, offset_f = vec_ref[4:5, :], vec_ref[5:6, :]
@@ -261,8 +329,10 @@
         return carry
 
     lax.fori_loop(0, blocks, norm_step, 0)
-    fetch.wait()
-    fetch_e.wait()
+    for fetch in fetches:
+        fetch.wait()
+    for copy in copies:
+        copy.wait()
 
     def hidden_step(index, carry):
         block, chunk = index // (FF // wide), index % (FF // wide)
@@ -295,7 +365,7 @@
         final = (unit * gain_f + offset_f).astype(BF16)
         final_ref[there, :] = final
         logits = nt(final, w_ref[head : head + VOCAB, :])
-        nexts = columns[:, 2:3]
+        nexts = columns[:, 2 * POOL : 2 * POOL + 1]
         lanes = lax.broadcasted_iota(jnp.int32, logits.shape, 1)
         target = jnp.where(lanes == nexts, 1.0, 0.0)
         valid = jnp.where(nexts >= 0, 1.0, 0.0)
@@ -615,24 +685,6 @@
     square_ref[...] = squares
 
 
-def step_inputs(byte_ids, layouts):
-    slots, length = byte_ids.shape
-    places = jnp.arange(length, dtype=jnp.int32)[None, :]
-    half = length // 2
-    split = (layouts == 1)[:, None]
-    first = jnp.where(split & (places >= half), half, 0)
-    last = jnp.where(split & (places < half), half, length)
-    back = jnp.pad(byte_ids[:, :-2], ((0, 0), (2, 0)))
-    back = jnp.where(places - 2 >= first, back, -1)
-    ahead = jnp.pad(byte_ids[:, 1:], ((0, 0), (0, 1)))
-    ahead = jnp.where(places + 1 < last, ahead, -1)
-    kinds = jnp.stack([byte_ids, back, ahead], 0)
-    kinds = kinds.reshape(3, slots, length // POOL, POOL).transpose(0, 3, 1, 2)
-    kinds = kinds.reshape(3, POOL, slots * (length // POOL))
-    lines = kinds.reshape(3 * POOL, -1)
-    return lines
-
-
 VMEM = pl.BlockSpec(memory_space=pltpu.VMEM)
 SMEM = pl.BlockSpec(memory_space=pltpu.SMEM)
 ANY = pl.BlockSpec(memory_space=pl.ANY)
@@ -643,16 +695,11 @@
     return ROW_F1 if pieces == 1 else ROW_F1 // SHARD * SHARD
 
 
-def device_grads(pieces, coords, vecs, byte_ids, layouts, count, exchange):
-    slots, length = byte_ids.shape
-    short_len = length // POOL
-    rows = slots * short_len
-    lines = step_inputs(byte_ids, layouts)
-    by_place = lines.reshape(3, POOL, rows).transpose(1, 2, 0)
-    lines = jnp.pad(lines, ((0, 16 - lines.shape[0]), (0, 0)))
-    cols = lines.T
-    slopes = 2.0 ** (-8.0 * (jnp.arange(HEADS, dtype=F32) + 1.0) / HEADS)
-    vecs = jnp.pad(vecs.astype(F32), ((0, 2), (0, 0)))
+def device_grads(pieces, tail, vecs, coords, ids, layouts, count, exchange):
+    slots = layouts.shape[0]
+    rows = ids.shape[1]
+    short_len = rows // slots
+    slopes = np.float32(2.0) ** (-8.0 * (np.arange(HEADS, dtype=np.float32) + 1.0) / HEADS)
     shape = jax.ShapeDtypeStruct
     params = pltpu.CompilerParams(vmem_limit_bytes=LIMIT)
     number = len(pieces)
@@ -661,8 +708,10 @@
     deep_rows = ROW_END - deep_base(number)
     table_rows = SHARD if whole_shards else VOCAB
     jobs = 64 if whole_shards else 1
+    more = [] if vecs is None else [vecs]
+    rest = [] if tail is None else [tail]
     half = D // 2
-    shifted, short, normed, qkv, lse, mixed, resid = pl.pallas_call(
+    shifted, short, normed, qkv, lse, mixed, resid, lines, cols, vecs = pl.pallas_call(
         partial(attend_kernel, short_len, slots, number),
         out_shape=(
             shape((rows, POOL * D), BF16),
@@ -672,19 +721,25 @@
             shape((slots, HEADS, 1, short_len), F32),
             shape((rows, D), BF16),
             shape((rows, D), F32),
+            shape((16, rows), jnp.int32),
+            shape((POOL, rows, 128), jnp.int32),
+            shape((8, D), F32),
         ),
-        in_specs=[SMEM, SMEM, SMEM, VMEM, VMEM] + [ANY] * number,
-        out_specs=(VMEM,) * 7,
+        in_specs=[SMEM, SMEM, SMEM, VMEM] + [ANY] * number + [VMEM] * len(more),
+        out_specs=(VMEM,) * 10,
         scratch_shapes=[
             pltpu.VMEM((front_rows, D), BF16),
             pltpu.VMEM((short_len, short_len), F32),
             pltpu.VMEM((short_len, short_len), F32),
             pltpu.VMEM((short_len, 2 * HEAD), F32),
+            pltpu.VMEM((32, 16, D // 2), BF16),
             pltpu.SemaphoreType.DMA((jobs,)),
+            pltpu.SemaphoreType.DMA((32,)),
         ],
         compiler_params=params,
+        cost_estimate=pl.CostEstimate(flops=9_000_000_000, bytes_accessed=20_000_000, transcendentals=2_400_000),
         name="attend",
-    )(coords, layouts, slopes, cols, vecs, *pieces)
+    )(coords, layouts, slopes, ids, *pieces, *more)
     keep_deep, send_deep, table, dresid, small_deep = pl.pallas_call(
         partial(deep_kernel, count, number),
         out_shape=(
@@ -694,7 +749,7 @@
             shape((rows, D), F32),
             shape((8, D), F32),
         ),
-        in_specs=[SMEM] + [VMEM] * 4 + [ANY] * number,
+        in_specs=[SMEM] + [VMEM] * 4 + [ANY] * (number + len(rest)),
         out_specs=(VMEM,) * 5,
         scratch_shapes=[
             pltpu.VMEM((deep_rows, D), BF16),
@@ -712,10 +767,11 @@
             pltpu.VMEM((8, 8, D), F32),
             pltpu.SemaphoreType.DMA((jobs,)),
             pltpu.SemaphoreType.DMA((jobs,)),
+            pltpu.SemaphoreType.DMA((2,)),
         ],
         compiler_params=params,
         name="deep",
-    )(coords, by_place, lines, vecs, resid, *pieces)
+    )(coords, cols, lines, vecs, resid, *pieces, *rest)
     recv_deep = exchange(send_deep)
     keep_front, send_front, small = pl.pallas_call(
         partial(attend_back_kernel, short_len, slots, number),
@@ -751,25 +807,28 @@
     return lax.ppermute(array, AXES, pairs)
 
 
-def gather_pieces(shard):
-    first, second = shard[:GATHER_CUT], shard[GATHER_CUT:]
+def swap_halves(coords, shard):
+    half = D // 2
+    upper = coords[0] // 2 == 1
+    left, right = shard[:, :half], shard[:, half:]
+    keep, send = jnp.where(upper, right, left), jnp.where(upper, left, right)
+    other = swap_with(send, line=2)
+    return jnp.where(upper, other, keep), jnp.where(upper, keep, other)
+
+
+def gather_pieces(block, vectors):
+    half = D // 2
+    width = vectors.shape[1]
+    start = lax.axis_index(AXES) * width
+    own = lax.dynamic_update_slice(
+        jnp.zeros((16, half), BF16), vectors, (8 * (start // half), start % half)
+    )
+    first, second = jnp.concatenate([block[:GATHER_CUT], own], 0), block[GATHER_CUT:]
     along = jnp.concatenate([first] + [swap_with(first, zed=k) for k in (1, 2, 3)], 0)
     across = jnp.concatenate([second] + [swap_with(second, line=k) for k in (1, 2, 3)], 0)
     pieces = [along] + [swap_with(along, line=k) for k in (1, 2, 3)]
     pieces += [across] + [swap_with(across, zed=k) for k in (1, 2, 3)]
     return pieces + [swap_with(piece, core=1) for piece in pieces]
-
-
-def gather_vectors(vectors):
-    width = vectors.shape[1]
-    spread = jnp.zeros((8, lax.axis_size(AXES) * width), BF16)
-    spread = lax.dynamic_update_slice(spread, jnp.pad(vectors, ((0, 2), (0, 0))), (0, lax.axis_index(AXES) * width))
-    spread = spread + swap_with(spread, core=1)
-    for k in (1, 2):
-        spread = spread + swap_with(spread, line=k)
-    for k in (1, 2):
-        spread = spread + swap_with(spread, zed=k)
-    return spread[:6]
 
 
 def scatter_sum(coords, keep_front, recv_front, keep_deep, recv_deep, small):
@@ -855,18 +914,22 @@
     vectors_low = vectors.astype(BF16)
     width = vectors.shape[1]
     mine = lax.axis_index(AXES) * width
-    flat_ids, flat_layouts = byte_ids.reshape(-1, byte_ids.shape[-1]), layouts.reshape(-1)
+    flat_layouts = layouts.reshape(-1)
+    ids = byte_ids.reshape(flat_layouts.shape[0], -1, POOL).transpose(2, 0, 1).reshape(POOL, -1)
+    ids = jnp.pad(ids, ((0, 8 - POOL), (0, 0)))
     if paired:
-        pieces = gather_pieces(weights_low)
-        vecs = gather_vectors(vectors_low)
-        parts = device_grads(pieces, coords, vecs, flat_ids, flat_layouts, count, partial(swap_with, core=1))
+        front, back = swap_halves(coords, weights_low)
+        tail = lax.all_gather(back, AXES, axis=0, tiled=True)
+        pieces = gather_pieces(front, vectors_low)
+        parts = device_grads(pieces, tail, None, coords, ids, flat_layouts, count, partial(swap_with, core=1))
         owned, small, squares = scatter_sum(coords, *parts)
         squares = sum_all(squares)
     else:
         coords = coords * 0
         pieces = [lax.all_gather(weights_low, AXES, axis=0, tiled=True)]
         vecs = lax.all_gather(vectors_low, AXES, axis=1, tiled=True)
-        parts = device_grads(pieces, coords, vecs, flat_ids, flat_layouts, count, lambda array: array)
+        vecs = jnp.pad(vecs.astype(F32), ((0, 2), (0, 0)))
+        parts = device_grads(pieces, None, vecs, coords, ids, flat_layouts, count, lambda array: array)
         keep_front, send_front, keep_deep, send_deep, small = parts
         local = jnp.concatenate(
             [

time: 318 us -> 300 us (0.943)
  waiting for transfers between devices: 102 us -> 82 us
  between operations: 5.47 us -> 18.9 us
  local copies, waits for them, and re-layouts: 14.9 us -> 8.8 us
  starting transfers between devices: 63.3 us -> 58 us
    ppermute x46 -> x42, waiting for transfers between devices: 102 us -> 82 us  [swap_with(): return lax.ppermute(array, AXES, pairs)]
    ppermute x46 -> x42, starting transfers between devices: 63.3 us -> 57.9 us  [swap_with(): return lax.ppermute(array, AXES, pairs)]
    another operation x6 -> x0, local copies, waits for them, and re-layouts: 4.81 us -> none  [step_inputs(): kinds = jnp.stack([byte_ids, back, ahead], 0)]
  transfers between devices with their start and end apart: 46 -> 43, of which waited for: 22 -> 18; matrix products, arithmetic and copies ran while one was open for 5% -> 2% of each run, Pallas kernels for 10% -> 20%
where the time goes in v3:
time: 300 us
  Pallas kernels  123 us (41%)
  waiting for transfers between devices  82 us (27%)
  starting transfers between devices  58 us (19%)
  between operations  18.9 us (6%)
  other arithmetic  9.19 us (3%)
  local copies, waits for them, and re-layouts  8.8 us (3%)
    ppermute x42, waiting for transfers between devices, swap_with(): return lax.ppermute(array, AXES, pairs)  82 us
    ppermute x42, starting transfers between devices, swap_with(): return lax.ppermute(array, AXES, pairs)  57.9 us
    pallas_call x1, Pallas kernels, device_grads(): pl.pallas_call(partial(deep_kernel, count, number), out_shape=(shape((ROW...  48.5 us
    pallas_call x1, Pallas kernels, device_grads(): pl.pallas_call(partial(attend_back_kernel, short_len, slots, number), out...  33.1 us
    pallas_call x1, Pallas kernels, device_grads(): pl.pallas_call(partial(attend_kernel, short_len, slots, number), out_shap...  25.8 us
    pallas_call x1, Pallas kernels, scatter_sum(): pl.pallas_call(core_sum_kernel, out_shape=(shape((8 * SCATTER_CUT + 64, q...  9.28 us
  transfers between devices with their start and end apart: 43, of which 18 were waited for; matrix products, arithmetic and copies ran while one was open for 2% of the time, Pallas kernels for 20%

profile of v3, /device:TPU:0, one launch (start us, length us, event | category | flops | bytes accessed | tf_op | source)
XLA Modules:
  0.0 299.9 jit_solution(12346163714863582780)
XLA Ops:
  7.2 1.1 convert_element_type.6
  8.4 3.0 %collective-permute-start = (bf16[304,256]{1,0:T(8,128)(2,1)S(1)}, bf16[304,256]{1,0:T(8,128)(2,1)S(1)}, u32[]{:S(2)}, u32[]{:S(2)}) collective-permute-start(bf16[304,256]{1,0:T(8,128)(2,1)S(1)} %broadcast_select_fusion.9), channel_id=1, source_target_pairs={{0,16},{1,17},{2,18},{3,19},{4,20},{5,21},{6,22},{7,23},{8,24},{9,... | collective-permute-start | bytes 466952 | tf_op jit(solution)/shard_map/ppermute | solution.py:807
  11.4 4.0 %collective-permute-done = bf16[304,256]{1,0:T(8,128)(2,1)S(1)} collective-permute-done((bf16[304,256]{1,0:T(8,128)(2,1)S(1)}, bf16[304,256]{1,0:T(8,128)(2,1)S(1)}, u32[]{:S(2)}, u32[]{:S(2)}) %collective-permute-start) | collective-permute-done | bytes 155680 | tf_op jit(solution)/shard_map/ppermute | solution.py:807
  16.6 2.7 collective-permute-start.9
  20.2 4.1 %collective-permute-start.3 = (bf16[224,256]{1,0:T(8,128)(2,1)S(1)}, bf16[224,256]{1,0:T(8,128)(2,1)S(1)}, u32[]{:S(2)}, u32[]{:S(2)}) collective-permute-start(bf16[224,256]{1,0:T(8,128)(2,1)S(1)} %pad_maximum_fusion.2), channel_id=1, source_target_pairs={{0,6},{1,7},{2,4},{3,5},{4,2},{5,3},{6,0},{7,1},{8,14},{9,15},{10,... | collective-permute-start | bytes 344072 | tf_op jit(solution)/shard_map/ppermute | solution.py:807
  25.1 6.1 %collective-permute-done.1 = bf16[224,256]{1,0:T(8,128)(2,1)S(1)} collective-permute-done((bf16[224,256]{1,0:T(8,128)(2,1)S(1)}, bf16[224,256]{1,0:T(8,128)(2,1)S(1)}, u32[]{:S(2)}, u32[]{:S(2)}) %collective-permute-start.1) | collective-permute-done | bytes 114720 | tf_op jit(solution)/shard_map/ppermute | solution.py:807
  31.2 2.4 collective-permute-done.2
  33.6 2.5 collective-permute-start.6
  37.1 3.1 %collective-permute-start.12 = (bf16[384,256]{1,0:T(8,128)(2,1)S(1)}, bf16[384,256]{1,0:T(8,128)(2,1)S(1)}, u32[]{:S(2)}, u32[]{:S(2)}) collective-permute-start(bf16[384,256]{1,0:T(8,128)(2,1)S(1)} %pad_maximum_fusion.1.refs_4_), channel_id=1, source_target_pairs={{0,6},{1,7},{2,4},{3,5},{4,2},{5,3},{6,0},{7,1},{8,14},{9,15},{10,... | collective-permute-start | bytes 589832 | tf_op jit(solution)/shard_map/ppermute | solution.py:807
  40.2 5.6 %collective-permute-done.12.refs_7_ = bf16[384,256]{1,0:T(8,128)(2,1)S(1)} collective-permute-done((bf16[384,256]{1,0:T(8,128)(2,1)S(1)}, bf16[384,256]{1,0:T(8,128)(2,1)S(1)}, u32[]{:S(2)}, u32[]{:S(2)}) %collective-permute-start.12) | collective-permute-done | bytes 196640 | tf_op jit(solution)/shard_map/ppermute | solution.py:807
  45.8 7.5 %collective-permute-start.10 = (bf16[384,256]{1,0:T(8,128)(2,1)S(1)}, bf16[384,256]{1,0:T(8,128)(2,1)}, u32[]{:S(2)}, u32[]{:S(2)}) collective-permute-start(bf16[384,256]{1,0:T(8,128)(2,1)S(1)} %pad_maximum_fusion.1.refs_4_), channel_id=1, source_target_pairs={{0,2},{1,3},{2,0},{3,1},{4,6},{5,7},{6,4},{7,5},{8,10},{9,11},{10,... | collective-permute-start | bytes 589832 | tf_op jit(solution)/shard_map/ppermute | solution.py:807
  53.3 3.2 %collective-permute-done.11.refs_6_ = bf16[384,256]{1,0:T(8,128)(2,1)S(1)} collective-permute-done((bf16[384,256]{1,0:T(8,128)(2,1)S(1)}, bf16[384,256]{1,0:T(8,128)(2,1)S(1)}, u32[]{:S(2)}, u32[]{:S(2)}) %collective-permute-start.11) | collective-permute-done | bytes 196640 | tf_op jit(solution)/shard_map/ppermute | solution.py:807
  56.5 5.5 %collective-permute-done.10.refs_5_ = bf16[384,256]{1,0:T(8,128)(2,1)} collective-permute-done((bf16[384,256]{1,0:T(8,128)(2,1)S(1)}, bf16[384,256]{1,0:T(8,128)(2,1)}, u32[]{:S(2)}, u32[]{:S(2)}) %collective-permute-start.10) | collective-permute-done | bytes 196640 | tf_op jit(solution)/shard_map/ppermute | solution.py:807
  63.3 2.4 collective-permute-done.19.refs_14_
  69.2 25.8 %attend.1 = (bf16[768,1536]{1,0:T(8,128)(2,1)}, f32[768,512]{1,0:T(8,128)}, bf16[768,512]{1,0:T(8,128)(2,1)}, bf16[768,1536]{1,0:T(8,128)(2,1)}, f32[2,8,1,384]{...) custom-call(s32[4]{0:T(128)} %pad_add_fusion.coords_ref, ...), custom_call_target="tpu_custom_call" | custom-call | flops 8999999488 | bytes 20000000 | tf_op jit(solution)/shard_map/attend/pallas_call | solution.py:714
  95.0 48.5 %deep.1 = (bf16[5888,256]{1,0:T(8,128)(2,1)}, bf16[5888,256]{1,0:T(8,128)(2,1)}, f32[256,512]{1,0:T(8,128)}, f32[768,512]{1,0:T(8,128)}, f32[8,512]{1,0:T(8,128)}) custom-call(s32[4]{0:T(128)} %pad_add_fusion.coords_ref, s32[3,768,128]{2,1,0:T(8,128)} %get-tuple-element.48.cols_ref, s32[16,768]{1,0:T(8,128)} %get-tuple-element.46.lines_ref, ...), custom_call_target="tpu_custom_call" | custom-call | tf_op jit(solution)/shard_map/deep/pallas_call | solution.py:743
  144.1 33.1 %attend_back.1 = (bf16[3840,256]{1,0:T(8,128)(2,1)}, bf16[3872,256]{1,0:T(8,128)(2,1)}, f32[8,512]{1,0:T(8,128)}) custom-call(s32[4]{0:T(128)} %pad_add_fusion.coords_ref, s32[2]{0:T(128)} %bitcast.11, f32[8]{0:T(128)} %constant.100.clone.slope_ref, s32[16,768]{1,0:T(8,128)} %get-tuple-element.46.lines_ref, f32[8,512]{1,0:T(8,128)} %get-tuple-element.47.vec_ref, ...), custom_call_target="tpu_custom_call" | custom-call | flops 12999999488 | bytes 20000000 | tf_op jit(solution)/shard_map/attend_back/pallas_call | solution.py:776
  177.3 4.1 %collective-permute-done.21.recv_front = bf16[3872,256]{1,0:T(8,128)(2,1)S(1)} collective-permute-done((bf16[3872,256]{1,0:T(8,128)(2,1)}, bf16[3872,256]{1,0:T(8,128)(2,1)S(1)}, u32[]{:S(2)}, u32[]{:S(2)}) %collective-permute-start.21) | collective-permute-done | bytes 1982496 | tf_op jit(solution)/shard_map/ppermute | solution.py:807
  181.5 1.3 copy-done.2
  183.7 9.3 %core_sum.1 = (bf16[3264,128]{1,0:T(8,128)(2,1)}, bf16[3264,128]{1,0:T(8,128)(2,1)}, bf16[3264,128]{1,0:T(8,128)(2,1)}, bf16[3264,128]{1,0:T(8,128)(2,1)}, bf16[...) custom-call(s32[4]{0:T(128)} %pad_add_fusion.coords_ref, ...), custom_call_target="tpu_custom_call" | custom-call | tf_op jit(solution)/shard_map/core_sum/pallas_call | solution.py:840
  193.0 1.8 collective-permute-start.23
  194.8 1.4 collective-permute-start.24
  196.6 2.8 collective-permute-start.27
  199.4 11.8 %collective-permute-done.26.q1 = bf16[1664,128]{1,0:T(8,128)(2,1)S(1)} collective-permute-done((bf16[1664,128]{1,0:T(8,128)(2,1)}, bf16[1664,128]{1,0:T(8,128)(2,1)S(1)}, u32[]{:S(2)}, u32[]{:S(2)}) %collective-permute-start.26) | collective-permute-done | bytes 426016 | tf_op jit(solution)/shard_map/ppermute | solution.py:807
  211.1 1.6 collective-permute-start.28
  212.7 16.0 %collective-permute-done.27.q2 = bf16[1664,128]{1,0:T(8,128)(2,1)S(1)} collective-permute-done((bf16[1664,128]{1,0:T(8,128)(2,1)}, bf16[1664,128]{1,0:T(8,128)(2,1)S(1)}, u32[]{:S(2)}, u32[]{:S(2)}) %collective-permute-start.27) | collective-permute-done | bytes 426016 | tf_op jit(solution)/shard_map/ppermute | solution.py:807
  228.7 4.6 %collective-permute-done.24.p2 = bf16[3264,128]{1,0:T(8,128)(2,1)S(1)} collective-permute-done((bf16[3264,128]{1,0:T(8,128)(2,1)}, bf16[3264,128]{1,0:T(8,128)(2,1)S(1)}, u32[]{:S(2)}, u32[]{:S(2)}) %collective-permute-start.24) | collective-permute-done | bytes 835616 | tf_op jit(solution)/shard_map/ppermute | solution.py:807
  234.5 3.9 %first_sum.1 = (bf16[864,128]{1,0:T(8,128)(2,1)}, bf16[864,128]{1,0:T(8,128)(2,1)}, bf16[864,128]{1,0:T(8,128)(2,1)}, bf16[864,128]{1,0:T(8,128)(2,1)}, bf16[416...) custom-call(s32[4]{0:T(128)} %pad_add_fusion.coords_ref, ...), custom_call_target="tpu_custom_call" | custom-call | tf_op jit(solution)/shard_map/first_sum/pallas_call | solution.py:855
  238.4 3.9 %collective-permute-start.29 = (bf16[864,128]{1,0:T(8,128)(2,1)}, bf16[864,128]{1,0:T(8,128)(2,1)S(1)}, u32[]{:S(2)}, u32[]{:S(2)}) collective-permute-start(bf16[864,128]{1,0:T(8,128)(2,1)} %get-tuple-element.73), channel_id=1, source_target_pairs={{0,2},{1,3},{2,0},{3,1},{4,6},{5,7},{6,4},{7,5},{8,10},{9,11},{10,... | collective-permute-start | bytes 663560 | tf_op jit(solution)/shard_map/ppermute | solution.py:807
  243.2 1.6 collective-permute-start.31
  244.8 1.7 collective-permute-start.32
  246.5 1.4 collective-permute-start.33
  247.9 1.8 collective-permute-done.32.t1
  249.7 2.7 collective-permute-start.34
  252.5 3.0 %collective-permute-done.34.t3 = bf16[416,128]{1,0:T(8,128)(2,1)S(1)} collective-permute-done((bf16[416,128]{1,0:T(8,128)(2,1)}, bf16[416,128]{1,0:T(8,128)(2,1)S(1)}, u32[]{:S(2)}, u32[]{:S(2)}) %collective-permute-start.34) | collective-permute-done | bytes 106528 | tf_op jit(solution)/shard_map/ppermute | solution.py:807
  255.5 5.2 %collective-permute-done.30.s2 = bf16[864,128]{1,0:T(8,128)(2,1)S(1)} collective-permute-done((bf16[864,128]{1,0:T(8,128)(2,1)}, bf16[864,128]{1,0:T(8,128)(2,1)S(1)}, u32[]{:S(2)}, u32[]{:S(2)}) %collective-permute-start.30) | collective-permute-done | bytes 221216 | tf_op jit(solution)/shard_map/ppermute | solution.py:807
  261.6 2.3 last_sum.1
  263.9 1.4 reduce_sum.18
  266.1 1.5 collective-permute-start.40
  268.2 1.6 collective-permute-start.36
  269.9 2.1 collective-permute-done.36
  272.6 1.1 collective-permute-start.37
  273.7 2.5 collective-permute-done.37
  276.2 3.1 %collective-permute-start.38 = (f32[8,128]{1,0:T(8,128)S(1)}, f32[8,128]{1,0:T(8,128)S(1)}, u32[]{:S(2)}, u32[]{:S(2)}) collective-permute-start(f32[8,128]{1,0:T(8,128)S(1)} %add.80), channel_id=1, source_target_pairs={{0,2},{1,3},{2,0},{3,1},{4,6},{5,7},{6,4},{7,5},{8,10},{9,11},{10,... | collective-permute-start | bytes 12296 | tf_op jit(solution)/shard_map/ppermute | solution.py:807
  279.3 1.6 collective-permute-done.38
  280.9 2.6 collective-permute-start.39
  283.5 1.0 broadcast_select_fusion.1
  289.2 1.6 add_multiply_fusion
  (147 shorter events, 17.8 us)
Async XLA Ops:
  7.2 87.8 %all-gather.2.cloned.1.call-start = ((), (), s32[]{:S(2)}) async-start(), calls=%async_computation | async-start | bytes 5136384 | tf_op jit(solution)/shard_map/all_gather | solution.py:922
  7.2 59.3 %copy-start.31 = (s32[2,1,1152]{2,1,0:T(1,128)S(1)}, s32[2,1,1152]{2,1,0:T(1,128)}, u32[]{:S(2)}) copy-start(s32[2,1,1152]{2,1,0:T(1,128)} %param.9) | copy-start | bytes 27652
  8.4 7.1 %collective-permute-start = (bf16[304,256]{1,0:T(8,128)(2,1)S(1)}, bf16[304,256]{1,0:T(8,128)(2,1)S(1)}, u32[]{:S(2)}, u32[]{:S(2)}) collective-permute-start(bf16[304,256]{1,0:T(8,128)(2,1)S(1)} %broadcast_select_fusion.9), channel_id=1, source_target_pairs={{0,16},{1,17},{2,18},{3,19},{4,20},{5,21},{6,22},{7,23},{8,24},{9,... | collective-permute-start | bytes 466952 | tf_op jit(solution)/shard_map/ppermute | solution.py:807
  16.6 7.7 %collective-permute-start.9 = (bf16[96,256]{1,0:T(8,128)(2,1)S(1)}, bf16[96,256]{1,0:T(8,128)(2,1)S(1)}, u32[]{:S(2)}, u32[]{:S(2)}) collective-permute-start(bf16[96,256]{1,0:T(8,128)(2,1)S(1)} %slice.41), channel_id=1, source_target_pairs={{0,24},{1,25},{2,26},{3,27},{4,28},{5,29},{6,30},{7,31},{8,16},{9,... | collective-permute-start | bytes 147464 | tf_op jit(solution)/shard_map/ppermute | solution.py:807
  19.3 5.7 %collective-permute-start.8 = (bf16[96,256]{1,0:T(8,128)(2,1)S(1)}, bf16[96,256]{1,0:T(8,128)(2,1)S(1)}, u32[]{:S(2)}, u32[]{:S(2)}) collective-permute-start(bf16[96,256]{1,0:T(8,128)(2,1)S(1)} %slice.41), channel_id=1, source_target_pairs={{0,16},{1,17},{2,18},{3,19},{4,20},{5,21},{6,22},{7,23},{8,24},{9,... | collective-permute-start | bytes 147464 | tf_op jit(solution)/shard_map/ppermute | solution.py:807
  19.8 5.2 %collective-permute-start.7 = (bf16[96,256]{1,0:T(8,128)(2,1)S(1)}, bf16[96,256]{1,0:T(8,128)(2,1)S(1)}, u32[]{:S(2)}, u32[]{:S(2)}) collective-permute-start(bf16[96,256]{1,0:T(8,128)(2,1)S(1)} %slice.41), channel_id=1, source_target_pairs={{0,8},{1,9},{2,10},{3,11},{4,12},{5,13},{6,14},{7,15},{8,0},{9,1},... | collective-permute-start | bytes 147464 | tf_op jit(solution)/shard_map/ppermute | solution.py:807
  20.2 13.3 %collective-permute-start.3 = (bf16[224,256]{1,0:T(8,128)(2,1)S(1)}, bf16[224,256]{1,0:T(8,128)(2,1)S(1)}, u32[]{:S(2)}, u32[]{:S(2)}) collective-permute-start(bf16[224,256]{1,0:T(8,128)(2,1)S(1)} %pad_maximum_fusion.2), channel_id=1, source_target_pairs={{0,6},{1,7},{2,4},{3,5},{4,2},{5,3},{6,0},{7,1},{8,14},{9,15},{10,... | collective-permute-start | bytes 344072 | tf_op jit(solution)/shard_map/ppermute | solution.py:807
  24.3 9.2 %collective-permute-start.2 = (bf16[224,256]{1,0:T(8,128)(2,1)S(1)}, bf16[224,256]{1,0:T(8,128)(2,1)S(1)}, u32[]{:S(2)}, u32[]{:S(2)}) collective-permute-start(bf16[224,256]{1,0:T(8,128)(2,1)S(1)} %pad_maximum_fusion.2), channel_id=1, source_target_pairs={{0,4},{1,5},{2,6},{3,7},{4,0},{5,1},{6,2},{7,3},{8,12},{9,13},{10,... | collective-permute-start | bytes 344072 | tf_op jit(solution)/shard_map/ppermute | solution.py:807
  24.3 6.8 %collective-permute-start.1 = (bf16[224,256]{1,0:T(8,128)(2,1)S(1)}, bf16[224,256]{1,0:T(8,128)(2,1)S(1)}, u32[]{:S(2)}, u32[]{:S(2)}) collective-permute-start(bf16[224,256]{1,0:T(8,128)(2,1)S(1)} %pad_maximum_fusion.2), channel_id=1, source_target_pairs={{0,2},{1,3},{2,0},{3,1},{4,6},{5,7},{6,4},{7,5},{8,10},{9,11},{10,... | collective-permute-start | bytes 344072 | tf_op jit(solution)/shard_map/ppermute | solution.py:807
  25.0 43.3 %copy-start.6 = (bf16[384,256]{1,0:T(8,128)(2,1)}, bf16[384,256]{1,0:T(8,128)(2,1)S(1)}, u32[]{:S(2)}) copy-start(bf16[384,256]{1,0:T(8,128)(2,1)S(1)} %pad_maximum_fusion.1.refs_4_) | copy-start | bytes 589828
  25.0 15.2 %collective-permute-start.17 = (bf16[384,256]{1,0:T(8,128)(2,1)S(1)}, bf16[384,256]{1,0:T(8,128)(2,1)S(1)}, u32[]{:S(2)}, u32[]{:S(2)}) collective-permute-start(bf16[384,256]{1,0:T(8,128)(2,1)S(1)} %pad_maximum_fusion.1.refs_4_), channel_id=1, source_target_pairs={{0,1},{1,0},{2,3},{3,2},{4,5},{5,4},{6,7},{7,6},{8,9},{9,8},{10,11... | collective-permute-start | bytes 589832 | tf_op jit(solution)/shard_map/ppermute | solution.py:807
  33.5 34.8 %copy-start.7 = (bf16[896,256]{1,0:T(8,128)(2,1)}, bf16[896,256]{1,0:T(8,128)(2,1)S(1)}, u32[]{:S(2)}) copy-start(bf16[896,256]{1,0:T(8,128)(2,1)S(1)} %constant_dynamic-update-slice_fusion.refs_0_) | copy-start | bytes 1376260
  33.6 28.5 %collective-permute-start.6 = (bf16[896,256]{1,0:T(8,128)(2,1)S(1)}, bf16[896,256]{1,0:T(8,128)(2,1)S(1)}, u32[]{:S(2)}, u32[]{:S(2)}) collective-permute-start(bf16[896,256]{1,0:T(8,128)(2,1)S(1)} %constant_dynamic-update-slice_fusion.refs_0_), channel_id=1, source_target_pairs={{0,24},{1,25},{2,26},{3,27},{4,28},{5,29},{6,30},{7,31},{8,16},{9,... | collective-permute-start | bytes 1376264 | tf_op jit(solution)/shard_map/ppermute | solution.py:807
  36.0 26.5 %collective-permute-start.5 = (bf16[896,256]{1,0:T(8,128)(2,1)S(1)}, bf16[896,256]{1,0:T(8,128)(2,1)S(1)}, u32[]{:S(2)}, u32[]{:S(2)}) collective-permute-start(bf16[896,256]{1,0:T(8,128)(2,1)S(1)} %constant_dynamic-update-slice_fusion.refs_0_), channel_id=1, source_target_pairs={{0,16},{1,17},{2,18},{3,19},{4,20},{5,21},{6,22},{7,23},{8,24},{9,... | collective-permute-start | bytes 1376264 | tf_op jit(solution)/shard_map/ppermute | solution.py:807
  36.5 26.1 %collective-permute-start.4 = (bf16[896,256]{1,0:T(8,128)(2,1)S(1)}, bf16[896,256]{1,0:T(8,128)(2,1)S(1)}, u32[]{:S(2)}, u32[]{:S(2)}) collective-permute-start(bf16[896,256]{1,0:T(8,128)(2,1)S(1)} %constant_dynamic-update-slice_fusion.refs_0_), channel_id=1, source_target_pairs={{0,8},{1,9},{2,10},{3,11},{4,12},{5,13},{6,14},{7,15},{8,0},{9,1},... | collective-permute-start | bytes 1376264 | tf_op jit(solution)/shard_map/ppermute | solution.py:807
  37.1 8.7 %collective-permute-start.12 = (bf16[384,256]{1,0:T(8,128)(2,1)S(1)}, bf16[384,256]{1,0:T(8,128)(2,1)S(1)}, u32[]{:S(2)}, u32[]{:S(2)}) collective-permute-start(bf16[384,256]{1,0:T(8,128)(2,1)S(1)} %pad_maximum_fusion.1.refs_4_), channel_id=1, source_target_pairs={{0,6},{1,7},{2,4},{3,5},{4,2},{5,3},{6,0},{7,1},{8,14},{9,15},{10,... | collective-permute-start | bytes 589832 | tf_op jit(solution)/shard_map/ppermute | solution.py:807
  40.2 16.3 %collective-permute-start.11 = (bf16[384,256]{1,0:T(8,128)(2,1)S(1)}, bf16[384,256]{1,0:T(8,128)(2,1)S(1)}, u32[]{:S(2)}, u32[]{:S(2)}) collective-permute-start(bf16[384,256]{1,0:T(8,128)(2,1)S(1)} %pad_maximum_fusion.1.refs_4_), channel_id=1, source_target_pairs={{0,4},{1,5},{2,6},{3,7},{4,0},{5,1},{6,2},{7,3},{8,12},{9,13},{10,... | collective-permute-start | bytes 589832 | tf_op jit(solution)/shard_map/ppermute | solution.py:807
  45.8 16.3 %collective-permute-start.10 = (bf16[384,256]{1,0:T(8,128)(2,1)S(1)}, bf16[384,256]{1,0:T(8,128)(2,1)}, u32[]{:S(2)}, u32[]{:S(2)}) collective-permute-start(bf16[384,256]{1,0:T(8,128)(2,1)S(1)} %pad_maximum_fusion.1.refs_4_), channel_id=1, source_target_pairs={{0,2},{1,3},{2,0},{3,1},{4,6},{5,7},{6,4},{7,5},{8,10},{9,11},{10,... | collective-permute-start | bytes 589832 | tf_op jit(solution)/shard_map/ppermute | solution.py:807
  56.5 6.6 %collective-permute-start.20 = (bf16[384,256]{1,0:T(8,128)(2,1)S(1)}, bf16[384,256]{1,0:T(8,128)(2,1)S(1)}, u32[]{:S(2)}, u32[]{:S(2)}) collective-permute-start(bf16[384,256]{1,0:T(8,128)(2,1)S(1)} %collective-permute-done.12.refs_7_), channel_id=1, source_target_pairs={{0,1},{1,0},{2,3},{3,2},{4,5},{5,4},{6,7},{7,6},{8,9},{9,8},{10,11... | collective-permute-start | bytes 589832 | tf_op jit(solution)/shard_map/ppermute | solution.py:807
  62.1 6.2 %collective-permute-start.13 = (bf16[896,256]{1,0:T(8,128)(2,1)S(1)}, bf16[896,256]{1,0:T(8,128)(2,1)S(1)}, u32[]{:S(2)}, u32[]{:S(2)}) collective-permute-start(bf16[896,256]{1,0:T(8,128)(2,1)S(1)} %constant_dynamic-update-slice_fusion.refs_0_), channel_id=1, source_target_pairs={{0,1},{1,0},{2,3},{3,2},{4,5},{5,4},{6,7},{7,6},{8,9},{9,8},{10,11... | collective-permute-start | bytes 1376264 | tf_op jit(solution)/shard_map/ppermute | solution.py:807
  62.1 6.2 %collective-permute-start.16 = (bf16[896,256]{1,0:T(8,128)(2,1)S(1)}, bf16[896,256]{1,0:T(8,128)(2,1)S(1)}, u32[]{:S(2)}, u32[]{:S(2)}) collective-permute-start(bf16[896,256]{1,0:T(8,128)(2,1)S(1)} %collective-permute-done.6.refs_3_), channel_id=1, source_target_pairs={{0,1},{1,0},{2,3},{3,2},{4,5},{5,4},{6,7},{7,6},{8,9},{9,8},{10,11... | collective-permute-start | bytes 1376264 | tf_op jit(solution)/shard_map/ppermute | solution.py:807
  62.6 5.7 %collective-permute-start.15 = (bf16[896,256]{1,0:T(8,128)(2,1)S(1)}, bf16[896,256]{1,0:T(8,128)(2,1)}, u32[]{:S(2)}, u32[]{:S(2)}) collective-permute-start(bf16[896,256]{1,0:T(8,128)(2,1)S(1)} %collective-permute-done.5.refs_2_), channel_id=1, source_target_pairs={{0,1},{1,0},{2,3},{3,2},{4,5},{5,4},{6,7},{7,6},{8,9},{9,8},{10,11... | collective-permute-start | bytes 1376264 | tf_op jit(solution)/shard_map/ppermute | solution.py:807
  62.7 5.6 %collective-permute-start.14 = (bf16[896,256]{1,0:T(8,128)(2,1)S(1)}, bf16[896,256]{1,0:T(8,128)(2,1)}, u32[]{:S(2)}, u32[]{:S(2)}) collective-permute-start(bf16[896,256]{1,0:T(8,128)(2,1)S(1)} %collective-permute-done.4.refs_1_), channel_id=1, source_target_pairs={{0,1},{1,0},{2,3},{3,2},{4,5},{5,4},{6,7},{7,6},{8,9},{9,8},{10,11... | collective-permute-start | bytes 1376264 | tf_op jit(solution)/shard_map/ppermute | solution.py:807
  63.2 2.6 collective-permute-start.19
  66.4 1.8 collective-permute-start.18
  143.6 37.9 %collective-permute-start.22 = (bf16[5888,256]{1,0:T(8,128)(2,1)}, bf16[5888,256]{1,0:T(8,128)(2,1)S(1)}, u32[]{:S(2)}, u32[]{:S(2)}) collective-permute-start(bf16[5888,256]{1,0:T(8,128)(2,1)} %get-tuple-element.62), channel_id=1, source_target_pairs={{0,1},{1,0},{2,3},{3,2},{4,5},{5,4},{6,7},{7,6},{8,9},{9,8},{10,11... | collective-permute-start | bytes 9043976 | tf_op jit(solution)/shard_map/ppermute | solution.py:807
  177.2 4.3 %collective-permute-start.21 = (bf16[3872,256]{1,0:T(8,128)(2,1)}, bf16[3872,256]{1,0:T(8,128)(2,1)S(1)}, u32[]{:S(2)}, u32[]{:S(2)}) collective-permute-start(bf16[3872,256]{1,0:T(8,128)(2,1)} %get-tuple-element.61), channel_id=1, source_target_pairs={{0,1},{1,0},{2,3},{3,2},{4,5},{5,4},{6,7},{7,6},{8,9},{9,8},{10,11... | collective-permute-start | bytes 5947400 | tf_op jit(solution)/shard_map/ppermute | solution.py:807
  193.0 18.2 %collective-permute-start.26 = (bf16[1664,128]{1,0:T(8,128)(2,1)}, bf16[1664,128]{1,0:T(8,128)(2,1)S(1)}, u32[]{:S(2)}, u32[]{:S(2)}) collective-permute-start(bf16[1664,128]{1,0:T(8,128)(2,1)} %get-tuple-element.69), channel_id=1, source_target_pairs={{0,2},{1,3},{2,0},{3,1},{4,6},{5,7},{6,4},{7,5},{8,10},{9,11},{10,... | collective-permute-start | bytes 1277960 | tf_op jit(solution)/shard_map/ppermute | solution.py:807
  193.0 35.7 %collective-permute-start.23 = (bf16[3264,128]{1,0:T(8,128)(2,1)}, bf16[3264,128]{1,0:T(8,128)(2,1)S(1)}, u32[]{:S(2)}, u32[]{:S(2)}) collective-permute-start(bf16[3264,128]{1,0:T(8,128)(2,1)} %get-tuple-element.65), channel_id=1, source_target_pairs={{0,8},{1,9},{2,10},{3,11},{4,12},{5,13},{6,14},{7,15},{8,0},{9,1},... | collective-permute-start | bytes 2506760 | tf_op jit(solution)/shard_map/ppermute | solution.py:807
  194.8 38.5 %collective-permute-start.24 = (bf16[3264,128]{1,0:T(8,128)(2,1)}, bf16[3264,128]{1,0:T(8,128)(2,1)S(1)}, u32[]{:S(2)}, u32[]{:S(2)}) collective-permute-start(bf16[3264,128]{1,0:T(8,128)(2,1)} %get-tuple-element.66), channel_id=1, source_target_pairs={{0,16},{1,17},{2,18},{3,19},{4,20},{5,21},{6,22},{7,23},{8,24},{9,... | collective-permute-start | bytes 2506760 | tf_op jit(solution)/shard_map/ppermute | solution.py:807
  196.3 37.0 %collective-permute-start.25 = (bf16[3264,128]{1,0:T(8,128)(2,1)}, bf16[3264,128]{1,0:T(8,128)(2,1)S(1)}, u32[]{:S(2)}, u32[]{:S(2)}) collective-permute-start(bf16[3264,128]{1,0:T(8,128)(2,1)} %get-tuple-element.67), channel_id=1, source_target_pairs={{0,24},{1,25},{2,26},{3,27},{4,28},{5,29},{6,30},{7,31},{8,16},{9,... | collective-permute-start | bytes 2506760 | tf_op jit(solution)/shard_map/ppermute | solution.py:807
  196.6 32.1 %collective-permute-start.27 = (bf16[1664,128]{1,0:T(8,128)(2,1)}, bf16[1664,128]{1,0:T(8,128)(2,1)S(1)}, u32[]{:S(2)}, u32[]{:S(2)}) collective-permute-start(bf16[1664,128]{1,0:T(8,128)(2,1)} %get-tuple-element.70), channel_id=1, source_target_pairs={{0,4},{1,5},{2,6},{3,7},{4,0},{5,1},{6,2},{7,3},{8,12},{9,13},{10,... | collective-permute-start | bytes 1277960 | tf_op jit(solution)/shard_map/ppermute | solution.py:807
  211.1 17.6 %collective-permute-start.28 = (bf16[1664,128]{1,0:T(8,128)(2,1)}, bf16[1664,128]{1,0:T(8,128)(2,1)S(1)}, u32[]{:S(2)}, u32[]{:S(2)}) collective-permute-start(bf16[1664,128]{1,0:T(8,128)(2,1)} %get-tuple-element.71), channel_id=1, source_target_pairs={{0,6},{1,7},{2,4},{3,5},{4,2},{5,3},{6,0},{7,1},{8,14},{9,15},{10,... | collective-permute-start | bytes 1277960 | tf_op jit(solution)/shard_map/ppermute | solution.py:807
  238.4 49.9 %copy-start.32 = (f32[6,16]{1,0:T(8,128)S(1)}, f32[6,16]{1,0:T(8,128)}, u32[]{:S(2)}) copy-start(f32[6,16]{1,0:T(8,128)} %param.16) | copy-start | bytes 1156
  238.4 49.9 %copy-start.33 = (f32[6,16]{1,0:T(8,128)S(1)}, f32[6,16]{1,0:T(8,128)}, u32[]{:S(2)}) copy-start(f32[6,16]{1,0:T(8,128)} %param.15) | copy-start | bytes 1156
  238.4 17.1 %collective-permute-start.29 = (bf16[864,128]{1,0:T(8,128)(2,1)}, bf16[864,128]{1,0:T(8,128)(2,1)S(1)}, u32[]{:S(2)}, u32[]{:S(2)}) collective-permute-start(bf16[864,128]{1,0:T(8,128)(2,1)} %get-tuple-element.73), channel_id=1, source_target_pairs={{0,2},{1,3},{2,0},{3,1},{4,6},{5,7},{6,4},{7,5},{8,10},{9,11},{10,... | collective-permute-start | bytes 663560 | tf_op jit(solution)/shard_map/ppermute | solution.py:807
  242.4 18.4 %collective-permute-start.30 = (bf16[864,128]{1,0:T(8,128)(2,1)}, bf16[864,128]{1,0:T(8,128)(2,1)S(1)}, u32[]{:S(2)}, u32[]{:S(2)}) collective-permute-start(bf16[864,128]{1,0:T(8,128)(2,1)} %get-tuple-element.74), channel_id=1, source_target_pairs={{0,4},{1,5},{2,6},{3,7},{4,0},{5,1},{6,2},{7,3},{8,12},{9,13},{10,... | collective-permute-start | bytes 663560 | tf_op jit(solution)/shard_map/ppermute | solution.py:807
  243.2 17.6 %collective-permute-start.31 = (bf16[864,128]{1,0:T(8,128)(2,1)}, bf16[864,128]{1,0:T(8,128)(2,1)S(1)}, u32[]{:S(2)}, u32[]{:S(2)}) collective-permute-start(bf16[864,128]{1,0:T(8,128)(2,1)} %get-tuple-element.75), channel_id=1, source_target_pairs={{0,6},{1,7},{2,4},{3,5},{4,2},{5,3},{6,0},{7,1},{8,14},{9,15},{10,... | collective-permute-start | bytes 663560 | tf_op jit(solution)/shard_map/ppermute | solution.py:807
  244.8 4.9 %collective-permute-start.32 = (bf16[416,128]{1,0:T(8,128)(2,1)}, bf16[416,128]{1,0:T(8,128)(2,1)S(1)}, u32[]{:S(2)}, u32[]{:S(2)}) collective-permute-start(bf16[416,128]{1,0:T(8,128)(2,1)} %get-tuple-element.77), channel_id=1, source_target_pairs={{0,8},{1,9},{2,10},{3,11},{4,12},{5,13},{6,14},{7,15},{8,0},{9,1},... | collective-permute-start | bytes 319496 | tf_op jit(solution)/shard_map/ppermute | solution.py:807
  246.5 6.1 %collective-permute-start.33 = (bf16[416,128]{1,0:T(8,128)(2,1)}, bf16[416,128]{1,0:T(8,128)(2,1)S(1)}, u32[]{:S(2)}, u32[]{:S(2)}) collective-permute-start(bf16[416,128]{1,0:T(8,128)(2,1)} %get-tuple-element.78), channel_id=1, source_target_pairs={{0,16},{1,17},{2,18},{3,19},{4,20},{5,21},{6,22},{7,23},{8,24},{9,... | collective-permute-start | bytes 319496 | tf_op jit(solution)/shard_map/ppermute | solution.py:807
  249.7 5.8 %collective-permute-start.34 = (bf16[416,128]{1,0:T(8,128)(2,1)}, bf16[416,128]{1,0:T(8,128)(2,1)S(1)}, u32[]{:S(2)}, u32[]{:S(2)}) collective-permute-start(bf16[416,128]{1,0:T(8,128)(2,1)} %get-tuple-element.79), channel_id=1, source_target_pairs={{0,24},{1,25},{2,26},{3,27},{4,28},{5,29},{6,30},{7,31},{8,16},{9,... | collective-permute-start | bytes 319496 | tf_op jit(solution)/shard_map/ppermute | solution.py:807
  266.0 1.6 collective-permute-start.35
  266.1 17.5 %collective-permute-start.40 = (f32[608,128]{1,0:T(8,128)}, f32[608,128]{1,0:T(8,128)S(1)}, u32[]{:S(2)}, u32[]{:S(2)}) collective-permute-start(f32[608,128]{1,0:T(8,128)} %get-tuple-element.83), channel_id=1, source_target_pairs={{0,16},{1,17},{2,18},{3,19},{4,20},{5,21},{6,22},{7,23},{8,24},{9,... | collective-permute-start | bytes 933896 | tf_op jit(solution)/shard_map/ppermute | solution.py:807
  268.2 3.7 %collective-permute-start.36 = (f32[8,128]{1,0:T(8,128)S(1)}, f32[8,128]{1,0:T(8,128)S(1)}, u32[]{:S(2)}, u32[]{:S(2)}) collective-permute-start(f32[8,128]{1,0:T(8,128)S(1)} %broadcast_add_fusion), channel_id=1, source_target_pairs={{0,8},{1,9},{2,10},{3,11},{4,12},{5,13},{6,14},{7,15},{8,0},{9,1},... | collective-permute-start | bytes 12296 | tf_op jit(solution)/shard_map/ppermute | solution.py:807
  272.6 3.7 %collective-permute-start.37 = (f32[8,128]{1,0:T(8,128)S(1)}, f32[8,128]{1,0:T(8,128)S(1)}, u32[]{:S(2)}, u32[]{:S(2)}) collective-permute-start(f32[8,128]{1,0:T(8,128)S(1)} %fusion.7), channel_id=1, source_target_pairs={{0,16},{1,17},{2,18},{3,19},{4,20},{5,21},{6,22},{7,23},{8,24},{9,... | collective-permute-start | bytes 12296 | tf_op jit(solution)/shard_map/ppermute | solution.py:807
  276.2 4.7 %collective-permute-start.38 = (f32[8,128]{1,0:T(8,128)S(1)}, f32[8,128]{1,0:T(8,128)S(1)}, u32[]{:S(2)}, u32[]{:S(2)}) collective-permute-start(f32[8,128]{1,0:T(8,128)S(1)} %add.80), channel_id=1, source_target_pairs={{0,2},{1,3},{2,0},{3,1},{4,6},{5,7},{6,4},{7,5},{8,10},{9,11},{10,... | collective-permute-start | bytes 12296 | tf_op jit(solution)/shard_map/ppermute | solution.py:807
  280.9 5.5 %collective-permute-start.39 = (f32[8,128]{1,0:T(8,128)S(1)}, f32[8,128]{1,0:T(8,128)S(1)}, u32[]{:S(2)}, u32[]{:S(2)}) collective-permute-start(f32[8,128]{1,0:T(8,128)S(1)} %add.81), channel_id=1, source_target_pairs={{0,4},{1,5},{2,6},{3,7},{4,0},{5,1},{6,2},{7,3},{8,12},{9,13},{10,... | collective-permute-start | bytes 12296 | tf_op jit(solution)/shard_map/ppermute | solution.py:807
  284.6 4.5 %collective-permute-start.41 = (f32[304,256]{1,0:T(8,128)S(1)}, f32[304,256]{1,0:T(8,128)S(1)}, u32[]{:S(2)}, u32[]{:S(2)}) collective-permute-start(f32[304,256]{1,0:T(8,128)S(1)} %broadcast_select_fusion.4), channel_id=1, source_target_pairs={{0,1},{1,0},{2,3},{3,2},{4,5},{5,4},{6,7},{7,6},{8,9},{9,8},{10,11... | collective-permute-start | bytes 933896 | tf_op jit(solution)/shard_map/ppermute | solution.py:807
  (29 other events, 252.9 us)
Sparse Core Ops, SparseCore 0:
  16.3 72.2 all-gather.1

commit v4 on v3

--- a/solution.py
+++ b/solution.py
@@ -36,6 +36,8 @@
 ROW_U = ROW_F2 + FF
 ROW_H = ROW_U + POOL * D
 ROW_END = ROW_H + VOCAB
+ROW_HALF = ROW_END // 2
+assert ROW_HALF - ROW_F1 == FF // 2
 
 BLOCK = 256
 AXES = ("dp", "fsdp")
@@ -291,7 +293,7 @@
     w_hbm, refs = refs[:pieces], refs[pieces:]
     if pieces > 1:
         tail_hbm, refs = refs[0], refs[1:]
-    (keep_ref, send_ref, table_ref, dresid_ref, small_ref,
+    (keep_mid, send_mid, keep_ref, send_ref, table_ref, dresid_ref, small_ref,
      w_ref, e_ref, normed_ref, act_ref, slope_ref, deep_ref, final_ref, dlog_ref, dup_ref, low_ref,
      ddeep_ref, dhid_ref, sums_ref, sems, e_sems, tail_sems) = refs
     rows = resid_ref.shape[0]
@@ -398,7 +400,7 @@
 
     lax.fori_loop(0, POOL * blocks, head_step, 0)
 
-    out_up, out_head = ROW_U - ROW_F1, ROW_H - ROW_F1
+    out_up, out_head = ROW_U - ROW_HALF, ROW_H - ROW_HALF
     split_store(keep_ref, send_ref, core, pl.ds(out_head, VOCAB), tn(dlog_ref[...], final_ref[...]))
     for j in range(POOL):
         there = pl.ds(j * rows, rows)
@@ -422,14 +424,22 @@
 
     lax.fori_loop(0, blocks * (FF // wide), dhid_step, 0)
 
-    def dff_step(chunk, carry):
+    def dff_in(chunk, carry):
+        here = rows_of(chunk, wide)
+        split_store(keep_mid, send_mid, core, here, tn(dhid_ref[:, here], normed_ref[...]))
+        lanes = pl.ds(pl.multiple_of(FF // 2 + chunk * wide, wide), wide)
+        split_store(keep_ref, send_ref, core, here, tn(dhid_ref[:, lanes], normed_ref[...]))
+        return carry
+
+    lax.fori_loop(0, FF // wide // 2, dff_in, 0)
+
+    def dff_out(chunk, carry):
         lanes = rows_of(chunk, wide)
-        split_store(keep_ref, send_ref, core, lanes, tn(dhid_ref[:, lanes], normed_ref[...]))
-        there = pl.ds(pl.multiple_of(FF + chunk * wide, wide), wide)
+        there = pl.ds(pl.multiple_of(FF // 2 + chunk * wide, wide), wide)
         split_store(keep_ref, send_ref, core, there, tn(act_ref[:, lanes], deep_ref[...]))
         return carry
 
-    lax.fori_loop(0, FF // wide, dff_step, 0)
+    lax.fori_loop(0, FF // wide, dff_out, 0)
 
     def dnorm_step(block, carry):
         at = rows_of(block)
@@ -445,19 +455,22 @@
         small_ref[k : k + 1, :] = jnp.sum(sums_ref[k], 0, keepdims=True)
 
 
-def attend_back_kernel(short_len, slots, pieces, coords_ref, lay_ref, slope_ref, lines_ref, vec_ref, dresid_ref,
-                       shifted_ref, short_ref, normed_ref, qkv_ref, lse_ref, mixed_ref, table_ref, deep_small_ref, *refs):
+def shard_base(pieces, row):
+    return row if pieces == 1 else row // SHARD * SHARD
+
+
+def attend_back_kernel(short_len, slots, pieces, coords_ref, lay_ref, slope_ref, dresid_ref,
+                       normed_ref, qkv_ref, lse_ref, mixed_ref, *refs):
     w_hbm, refs = refs[:pieces], refs[pieces:]
-    (keep_ref, send_ref, small_ref,
-     w_ref, dist_ref, mask_ref, dbranch_ref, dmix_ref, dqkv_ref, dshort_ref, sums_ref, sems) = refs
+    (keep_ref, send_ref, dqkv_ref,
+     w_ref, dist_ref, mask_ref, dbranch_ref, dmix_ref, sems) = refs
     rows = short_len * slots
     blocks = rows // BLOCK
-    base = 0
+    base = shard_base(pieces, ROW_O)
     core = coords_ref[2]
-    fetch = Fetch(w_hbm, coords_ref, w_ref, sems, 0, 0, ROW_F1)
+    fetch = Fetch(w_hbm, coords_ref, w_ref, sems, base, ROW_O, ROW_F1)
     fetch.start()
-    pool, proj, out = ROW_P - base, ROW_QKV - base, ROW_O - base
-    sums_ref[...] = jnp.zeros_like(sums_ref)
+    out = ROW_O - base
     fetch.wait()
 
     def dmix_step(block, carry):
@@ -468,7 +481,7 @@
         return carry
 
     lax.fori_loop(0, blocks, dmix_step, 0)
-    split_store(keep_ref, send_ref, core, pl.ds(ROW_O, D), tn(mixed_ref[...], dbranch_ref[...]))
+    split_store(keep_ref, send_ref, core, pl.ds(3 * D, D), tn(mixed_ref[...], dbranch_ref[...]))
 
     left_lanes = lax.broadcasted_iota(jnp.int32, (short_len, 2 * HEAD), 1) < HEAD
     tile = 128
@@ -525,10 +538,24 @@
 
         lax.fori_loop(0, HEADS // 2, head_step, 0)
 
-    gain = vec_ref[0:1, :]
     for part in range(3):
         grad = tn(dqkv_ref[:, part * D : (part + 1) * D], normed_ref[...])
-        split_store(keep_ref, send_ref, core, pl.ds(ROW_QKV + part * D, D), grad)
+        split_store(keep_ref, send_ref, core, pl.ds(part * D, D), grad)
+
+
+def front_back_kernel(pieces, coords_ref, lines_ref, vec_ref, dresid_ref, shifted_ref, short_ref, dqkv_ref, table_ref,
+                      deep_small_ref, *refs):
+    w_hbm, refs = refs[:pieces], refs[pieces:]
+    keep_ref, send_ref, small_ref, w_ref, dshort_ref, sums_ref, sems = refs
+    rows = dresid_ref.shape[0]
+    blocks = rows // BLOCK
+    core = coords_ref[2]
+    fetch = Fetch(w_hbm, coords_ref, w_ref, sems, 0, 0 if pieces > 1 else ROW_E, ROW_O)
+    fetch.start()
+    pool, proj = ROW_P, ROW_QKV
+    sums_ref[...] = jnp.zeros_like(sums_ref)
+    gain = vec_ref[0:1, :]
+    fetch.wait()
 
     def dshort_step(block, carry):
         at = rows_of(block)
@@ -555,7 +582,7 @@
         small_ref[k : k + 1, :] = jnp.sum(sums_ref[k], 0, keepdims=True)
     half = D // 2
     for k in range(2):
-        send_ref[ROW_F1 + 16 * k : ROW_F1 + 16 * (k + 1), :] = two_parts(small_ref[:, k * half : (k + 1) * half])
+        send_ref[ROW_QKV + 16 * k : ROW_QKV + 16 * (k + 1), :] = two_parts(small_ref[:, k * half : (k + 1) * half])
 
 
 def two_parts(values):
@@ -569,120 +596,147 @@
     return parts[:8] + parts[8:]
 
 
-def core_sum_kernel(coords_ref, keep_front, keep_deep, recv_front, recv_deep, small_ref,
-                    p0, p1, p2, p3, q0, q1, q2, q3,
-                    keep_ref, recv_ref, sems):
+def lay_out(coords_ref, keep_ref, recv_ref, p_refs, q_refs):
+    dp, z = coords_ref[0], coords_ref[1]
+    quarter = D // 4
+    line = 2 * SHARD
+    rest = line - SCATTER_CUT
+
+    def total(column, x, zed, begin, size):
+        at = pl.ds(pl.multiple_of(x * (4 * line) + zed * line + begin, 16), size)
+        lanes = pl.ds(pl.multiple_of(column * quarter, quarter), quarter)
+        return (keep_ref[at, lanes].astype(F32) + recv_ref[at, lanes].astype(F32)).astype(BF16)
+
+    for k in range(4):
+        there = dp ^ k
+        for zed in range(4):
+            p_refs[k][zed * SCATTER_CUT : (zed + 1) * SCATTER_CUT, :] = total(
+                there // 2, there % 2, zed, 0, SCATTER_CUT
+            )
+        for line_to in range(4):
+            q_refs[k][line_to * rest : (line_to + 1) * rest, :] = total(
+                line_to // 2, line_to % 2, z ^ k, SCATTER_CUT, rest
+            )
+
+
+def core_sum_kernel(coords_ref, keep_ref, recv_ref, *out_refs):
+    lay_out(coords_ref, keep_ref, recv_ref, out_refs[:4], out_refs[4:])
+
+
+def core_sum_front_kernel(coords_ref, keep_front, keep_att, keep_mid, recv_front, recv_att, recv_mid, small_ref, *refs):
+    out_refs, (keep_ref, recv_ref, sems) = refs[:8], refs[8:]
     copies = [
         pltpu.make_async_copy(source, target, sems.at[k])
         for k, (source, target) in enumerate((
-            (keep_deep, keep_ref.at[pl.ds(ROW_F1, ROW_END - ROW_F1)]),
-            (recv_deep, recv_ref.at[pl.ds(ROW_F1, ROW_END - ROW_F1)]),
-            (keep_front, keep_ref.at[pl.ds(0, ROW_F1)]),
-            (recv_front.at[pl.ds(0, ROW_F1)], recv_ref.at[pl.ds(0, ROW_F1)]),
-            (recv_front.at[pl.ds(ROW_F1, 32)], recv_ref.at[pl.ds(ROW_END, 32)]),
+            (keep_att, keep_ref.at[pl.ds(ROW_QKV, ROW_F1 - ROW_QKV)]),
+            (recv_att, recv_ref.at[pl.ds(ROW_QKV, ROW_F1 - ROW_QKV)]),
+            (keep_mid, keep_ref.at[pl.ds(ROW_F1, ROW_HALF - ROW_F1)]),
+            (recv_mid, recv_ref.at[pl.ds(ROW_F1, ROW_HALF - ROW_F1)]),
+            (keep_front, keep_ref.at[pl.ds(0, ROW_QKV)]),
+            (recv_front.at[pl.ds(0, ROW_QKV)], recv_ref.at[pl.ds(0, ROW_QKV)]),
+            (recv_front.at[pl.ds(ROW_QKV, 32)], recv_ref.at[pl.ds(ROW_HALF, 32)]),
         ))
     ]
     for copy in copies:
         copy.start()
     for copy in copies:
         copy.wait()
-    dp, z = coords_ref[0], coords_ref[1]
+    lay_out(coords_ref, keep_ref, recv_ref, out_refs[:4], out_refs[4:])
     quarter = D // 4
-    line = 2 * SHARD
-
-    def total(half, column, x, zed, begin, size):
-        row = half * (8 * line) + x * (4 * line) + zed * line + begin
-        at = pl.ds(pl.multiple_of(row, 16), size)
-        lanes = pl.ds(pl.multiple_of(column * quarter, quarter), quarter)
-        return (keep_ref[at, lanes].astype(F32) + recv_ref[at, lanes].astype(F32)).astype(BF16)
-
-    rest = line - SCATTER_CUT
-    for k, p_ref in enumerate((p0, p1, p2, p3)):
-        there = dp ^ k
-
-        def p_step(index, carry):
-            half, zed = index // 4, index % 4
-            p_ref[pl.ds(pl.multiple_of(index * SCATTER_CUT, 16), SCATTER_CUT), :] = total(
-                half, there // 2, there % 2, zed, 0, SCATTER_CUT
-            )
-            return carry
-
-        lax.fori_loop(0, 8, p_step, 0)
-    for k, q_ref in enumerate((q0, q1, q2, q3)):
-        zed = z ^ k
-
-        def q_step(index, carry):
-            half, there = index // 4, index % 4
-            q_ref[pl.ds(pl.multiple_of(index * rest, 16), rest), :] = total(
-                half, there // 2, there % 2, zed, SCATTER_CUT, rest
-            )
-            return carry
-
-        lax.fori_loop(0, 8, q_step, 0)
     for k in range(2):
         both = small_ref[:, 2 * k * quarter : 2 * (k + 1) * quarter] + one_value(
-            recv_ref[ROW_END + 16 * k : ROW_END + 16 * (k + 1), :]
+            recv_ref[ROW_HALF + 16 * k : ROW_HALF + 16 * (k + 1), :]
         )
         for side in range(2):
             parts = two_parts(both[:, side * quarter : (side + 1) * quarter])
-            row = 8 * SCATTER_CUT + 16 * (2 * k + side)
-            for p_ref in (p0, p1, p2, p3):
+            row = 4 * SCATTER_CUT + 16 * (2 * k + side)
+            for p_ref in out_refs[:4]:
                 p_ref[row : row + 16, :] = parts
 
 
-def first_sum_kernel(coords_ref, p0, p1, p2, p3, q0, q1, q2, q3,
-                     s0, s1, s2, s3, t0, t1, t2, t3):
+def sum_of(refs, row, size):
+    at = pl.ds(pl.multiple_of(row, 16), size)
+    return (refs[0][at, :].astype(F32) + refs[1][at, :].astype(F32)) + (
+        refs[2][at, :].astype(F32) + refs[3][at, :].astype(F32)
+    )
+
+
+def first_sum_kernel(coords_ref, *refs):
+    sources = ((refs[0:4], refs[4:8]), (refs[8:12], refs[12:16]))
+    s_refs, t_refs = refs[16:20], refs[20:24]
     dp, z = coords_ref[0], coords_ref[1]
     rest = 2 * SHARD - SCATTER_CUT
-
-    def total(refs, row, size):
-        at = pl.ds(pl.multiple_of(row, 16), size)
-        return (refs[0][at, :].astype(F32) + refs[1][at, :].astype(F32)) + (
-            refs[2][at, :].astype(F32) + refs[3][at, :].astype(F32)
-        )
-
-    for k, s_ref in enumerate((s0, s1, s2, s3)):
-        for half in range(2):
-            s_ref[half * SCATTER_CUT : (half + 1) * SCATTER_CUT, :] = total(
-                (p0, p1, p2, p3), (half * 4 + (z ^ k)) * SCATTER_CUT, SCATTER_CUT
+    for half, (p_refs, q_refs) in enumerate(sources):
+        for k in range(4):
+            s_refs[k][half * SCATTER_CUT : (half + 1) * SCATTER_CUT, :] = sum_of(
+                p_refs, (z ^ k) * SCATTER_CUT, SCATTER_CUT
             ).astype(BF16)
-    for k, t_ref in enumerate((t0, t1, t2, t3)):
-        for half in range(2):
-            t_ref[half * rest : (half + 1) * rest, :] = total(
-                (q0, q1, q2, q3), (half * 4 + (dp ^ k)) * rest, rest
-            ).astype(BF16)
+            t_refs[k][half * rest : (half + 1) * rest, :] = sum_of(q_refs, (dp ^ k) * rest, rest).astype(BF16)
     for k in range(4):
-        row = 8 * SCATTER_CUT + 16 * k
-        value = sum(one_value(ref[row : row + 16, :]) for ref in (p0, p1, p2, p3))
+        row = 4 * SCATTER_CUT + 16 * k
+        value = sum(one_value(ref[row : row + 16, :]) for ref in sources[0][0])
         parts = two_parts(value)
-        for s_ref in (s0, s1, s2, s3):
+        for s_ref in s_refs:
             s_ref[2 * SCATTER_CUT + 16 * k : 2 * SCATTER_CUT + 16 * (k + 1), :] = parts
 
 
-def last_sum_kernel(coords_ref, s0, s1, s2, s3, t0, t1, t2, t3, mine_ref, other_ref, small_ref, square_ref):
-    own = coords_ref[0] // 2
-    line = 2 * SHARD
-    rest = line - SCATTER_CUT
-
-    def total(refs, half, size):
-        at = pl.ds(pl.multiple_of(half * size, 16), size)
-        return (refs[0][at, :].astype(F32) + refs[1][at, :].astype(F32)) + (
-            refs[2][at, :].astype(F32) + refs[3][at, :].astype(F32)
-        )
-
+def last_sum_kernel(coords_ref, *refs):
+    s_refs, t_refs, out_refs, (small_ref, square_ref, sum_ref) = refs[:4], refs[4:8], refs[8:12], refs[12:]
+    y, core = coords_ref[0] // 2, coords_ref[2]
+    rest = 2 * SHARD - SCATTER_CUT
     squares = jnp.zeros((8, D // 4), F32)
-    for half, out_ref in ((own, mine_ref), (1 - own, other_ref)):
-        first = total((s0, s1, s2, s3), half, SCATTER_CUT)
-        second = total((t0, t1, t2, t3), half, rest)
-        out_ref[0:SCATTER_CUT, :] = first
-        out_ref[SCATTER_CUT:line, :] = second
+    for k in range(2):
+        half = y ^ k
+        first = sum_of(s_refs, half * SCATTER_CUT, SCATTER_CUT)
+        second = sum_of(t_refs, half * rest, rest)
         squares = squares + fold_rows(first * first) + fold_rows(second * second)
+        sum_ref[0:SCATTER_CUT, :] = first
+        sum_ref[SCATTER_CUT:, :] = second
+        for other in range(2):
+            out_refs[2 * other + k][...] = sum_ref[pl.ds(pl.multiple_of((core ^ other) * SHARD, 8), SHARD), :]
     for k in range(4):
         row = 2 * SCATTER_CUT + 16 * k
         small_ref[:, k * (D // 4) : (k + 1) * (D // 4)] = sum(
-            one_value(ref[row : row + 16, :]) for ref in (s0, s1, s2, s3)
+            one_value(ref[row : row + 16, :]) for ref in s_refs
         )
     square_ref[...] = squares
+
+
+def adam(param, first_m, second_m, grad, decay):
+    first_new = BETA * first_m + (1.0 - BETA) * grad
+    second_new = BETA * second_m + (1.0 - BETA) * grad * grad
+    correct = 1.0 - BETA**STEP
+    update = -RATE * (
+        first_new / correct / (jnp.sqrt(second_new / correct) + EPS_ADAM) + decay * param
+    )
+    return (first_new, second_new, update)
+
+
+def update_kernel(count, coords_ref, g0, g1, g2, g3, q0, q1, q2, q3, small_ref, w_ref, mw_ref, vw_ref, w_vec, m_vec, v_vec,
+                  loss_ref, norm_ref, mw_out, vw_out, uw_out, m_out, v_out, u_out):
+    y, core, mine = coords_ref[0] // 2, coords_ref[2], coords_ref[3]
+    small = small_ref[...]
+    line = lax.broadcasted_iota(jnp.int32, small.shape, 0)
+    gradient = jnp.where(line < 6, small, 0.0)
+    squares = (q0[...] + q1[...]) + (q2[...] + q3[...])
+
+    def whole(values):
+        return jnp.sum(jnp.sum(values, 0, keepdims=True), 1, keepdims=True)
+
+    norm = jnp.sqrt(whole(squares) + whole(gradient * gradient))
+    factor = CLIP / jnp.maximum(norm, CLIP)
+    norm_ref[...] = norm
+    loss_ref[...] = small[6:7, 0:1] / count
+    quarter = D // 4
+    for k, grad_ref in enumerate((g0, g1, g2, g3)):
+        place = (core ^ (k // 2)) * 2 + (y ^ (k % 2))
+        lanes = pl.ds(pl.multiple_of(place * quarter, quarter), quarter)
+        mw_out[:, lanes], vw_out[:, lanes], uw_out[:, lanes] = adam(
+            w_ref[:, lanes], mw_ref[:, lanes], vw_ref[:, lanes], grad_ref[...] * factor, DECAY
+        )
+    width = w_vec.shape[1]
+    owned = pltpu.roll(gradient, lax.rem(small.shape[1] - mine * width, small.shape[1]), 1)[:6, :width]
+    m_out[...], v_out[...], u_out[...] = adam(w_vec[...], m_vec[...], v_vec[...], owned * factor, 0.0)
 
 
 VMEM = pl.BlockSpec(memory_space=pltpu.VMEM)
@@ -692,10 +746,10 @@
 
 
 def deep_base(pieces):
-    return ROW_F1 if pieces == 1 else ROW_F1 // SHARD * SHARD
-
-
-def device_grads(pieces, tail, vecs, coords, ids, layouts, count, exchange):
+    return shard_base(pieces, ROW_F1)
+
+
+def device_grads(pieces, tail, vecs, coords, ids, layouts, count, paired):
     slots = layouts.shape[0]
     rows = ids.shape[1]
     short_len = rows // slots
@@ -740,17 +794,19 @@
         cost_estimate=pl.CostEstimate(flops=9_000_000_000, bytes_accessed=20_000_000, transcendentals=2_400_000),
         name="attend",
     )(coords, layouts, slopes, ids, *pieces, *more)
-    keep_deep, send_deep, table, dresid, small_deep = pl.pallas_call(
+    keep_mid, send_mid, keep_deep, send_deep, table, dresid, small_deep = pl.pallas_call(
         partial(deep_kernel, count, number),
         out_shape=(
-            shape((ROW_END - ROW_F1, half), BF16),
-            shape((ROW_END - ROW_F1, half), BF16),
+            shape((ROW_HALF - ROW_F1, half), BF16),
+            shape((ROW_HALF - ROW_F1, half), BF16),
+            shape((ROW_END - ROW_HALF, half), BF16),
+            shape((ROW_END - ROW_HALF, half), BF16),
             shape((VOCAB, D), F32),
             shape((rows, D), F32),
             shape((8, D), F32),
         ),
         in_specs=[SMEM] + [VMEM] * 4 + [ANY] * (number + len(rest)),
-        out_specs=(VMEM,) * 5,
+        out_specs=(VMEM,) * 7,
         scratch_shapes=[
             pltpu.VMEM((deep_rows, D), BF16),
             pltpu.VMEM((table_rows, D), BF16),
@@ -772,29 +828,102 @@
         compiler_params=params,
         name="deep",
     )(coords, cols, lines, vecs, resid, *pieces, *rest)
-    recv_deep = exchange(send_deep)
-    keep_front, send_front, small = pl.pallas_call(
+    out_base = shard_base(number, ROW_O)
+    keep_att, send_att, dqkv = pl.pallas_call(
         partial(attend_back_kernel, short_len, slots, number),
-        out_shape=(shape((ROW_F1, half), BF16), shape((ROW_F1 + 32, half), BF16), shape((8, D), F32)),
-        in_specs=[SMEM, SMEM, SMEM] + [VMEM] * 11 + [ANY] * number,
+        out_shape=(
+            shape((ROW_F1 - ROW_QKV, half), BF16),
+            shape((ROW_F1 - ROW_QKV, half), BF16),
+            shape((rows, 3 * D), BF16),
+        ),
+        in_specs=[SMEM, SMEM, SMEM] + [VMEM] * 5 + [ANY] * number,
         out_specs=(VMEM,) * 3,
         scratch_shapes=[
-            pltpu.VMEM((front_rows, D), BF16),
+            pltpu.VMEM((front_rows - out_base, D), BF16),
             pltpu.VMEM((short_len, short_len), F32),
             pltpu.VMEM((short_len, short_len), F32),
             pltpu.VMEM((rows, D), BF16),
             pltpu.VMEM((rows, D), BF16),
-            pltpu.VMEM((rows, 3 * D), BF16),
+            pltpu.SemaphoreType.DMA((jobs,)),
+        ],
+        compiler_params=params,
+        cost_estimate=pl.CostEstimate(flops=11_000_000_000, bytes_accessed=20_000_000, transcendentals=2_400_000),
+        name="attend_back",
+    )(coords, layouts, slopes, dresid, normed, qkv, lse, mixed, *pieces)
+    if paired:
+        recv_deep, recv_mid = swap_with(send_deep, core=1), swap_with(send_mid, core=1)
+        recv_deep, recv_mid = lax.optimization_barrier((recv_deep, recv_mid))
+        sent = core_sum(coords, keep_deep, recv_deep)
+        recv_att = swap_with(send_att, core=1)
+        sent, recv_att, dqkv = lax.optimization_barrier((sent, recv_att, dqkv))
+        sent = first_exchange(sent)
+    keep_front, send_front, small = pl.pallas_call(
+        partial(front_back_kernel, number),
+        out_shape=(shape((ROW_QKV, half), BF16), shape((ROW_QKV + 32, half), BF16), shape((8, D), F32)),
+        in_specs=[SMEM] + [VMEM] * 8 + [ANY] * number,
+        out_specs=(VMEM,) * 3,
+        scratch_shapes=[
+            pltpu.VMEM((front_rows, D), BF16),
             pltpu.VMEM((rows, D), BF16),
             pltpu.VMEM((2, 8, D), F32),
             pltpu.SemaphoreType.DMA((jobs,)),
         ],
         compiler_params=params,
-        cost_estimate=pl.CostEstimate(flops=13_000_000_000, bytes_accessed=20_000_000, transcendentals=2_400_000),
-        name="attend_back",
-    )(coords, layouts, slopes, lines, vecs, dresid, shifted, short, normed, qkv, lse, mixed, table, small_deep, *pieces)
-    recv_front = exchange(send_front)
-    return keep_front, recv_front, keep_deep, recv_deep, small
+        cost_estimate=pl.CostEstimate(flops=8_000_000_000, bytes_accessed=20_000_000, transcendentals=0),
+        name="front_back",
+    )(coords, lines, vecs, dresid, shifted, short, dqkv, table, small_deep, *pieces)
+    if not paired:
+        front = jnp.concatenate([keep_front, send_front[:ROW_QKV]], 1)
+        others = [
+            jnp.concatenate(pair, 1)
+            for pair in ((keep_att, send_att), (keep_mid, send_mid), (keep_deep, send_deep))
+        ]
+        return jnp.concatenate([front] + others, 0), small
+    late = 5
+    early = [array for k, array in enumerate(sent) if k != late]
+    early, keep_front, send_front, small = lax.optimization_barrier((early, keep_front, send_front, small))
+    sent = early[:late] + [sent[late]] + early[late:]
+    received = [swap_with(send_front, core=1), recv_att, recv_mid]
+    out_p, out_q = exchange_shapes(64)
+    parts = pl.pallas_call(
+        core_sum_front_kernel,
+        out_shape=(out_p,) * 4 + (out_q,) * 4,
+        in_specs=[SMEM] + [ANY] * 6 + [VMEM],
+        out_specs=(VMEM,) * 8,
+        scratch_shapes=[
+            pltpu.VMEM((ROW_HALF, half), BF16),
+            pltpu.VMEM((ROW_HALF + 32, half), BF16),
+            pltpu.SemaphoreType.DMA((7,)),
+        ],
+        compiler_params=params,
+        name="core_sum_front",
+    )(coords, keep_front, keep_att, keep_mid, *received, small)
+    return first_exchange(parts), sent
+
+
+def exchange_shapes(extra):
+    quarter = D // 4
+    return (
+        jax.ShapeDtypeStruct((4 * SCATTER_CUT + extra, quarter), BF16),
+        jax.ShapeDtypeStruct((4 * (2 * SHARD - SCATTER_CUT), quarter), BF16),
+    )
+
+
+def core_sum(coords, keep, received):
+    out_p, out_q = exchange_shapes(0)
+    return pl.pallas_call(
+        core_sum_kernel,
+        out_shape=(out_p,) * 4 + (out_q,) * 4,
+        in_specs=[SMEM] + [VMEM] * 2,
+        out_specs=(VMEM,) * 8,
+        compiler_params=pltpu.CompilerParams(vmem_limit_bytes=LIMIT),
+        name="core_sum",
+    )(coords, keep, received)
+
+
+def first_exchange(parts):
+    over = [parts[0]] + [swap_with(parts[k], line=k) for k in (1, 2, 3)]
+    return over + [parts[4]] + [swap_with(parts[4 + k], zed=k) for k in (1, 2, 3)]
 
 
 def swap_with(array, line=0, zed=0, core=0):
@@ -831,75 +960,35 @@
     return pieces + [swap_with(piece, core=1) for piece in pieces]
 
 
-def scatter_sum(coords, keep_front, recv_front, keep_deep, recv_deep, small):
+def scatter_sum(coords, front, deep):
     shape = jax.ShapeDtypeStruct
     params = pltpu.CompilerParams(vmem_limit_bytes=LIMIT)
     quarter = D // 4
-    line = 2 * SHARD
-    rest = line - SCATTER_CUT
-    parts = pl.pallas_call(
-        core_sum_kernel,
-        out_shape=(shape((8 * SCATTER_CUT + 64, quarter), BF16),) * 4 + (shape((8 * rest, quarter), BF16),) * 4,
-        in_specs=[SMEM] + [ANY] * 4 + [VMEM],
-        out_specs=(VMEM,) * 8,
-        scratch_shapes=[
-            pltpu.VMEM((ROW_END, D // 2), BF16),
-            pltpu.VMEM((ROW_END + 32, D // 2), BF16),
-            pltpu.SemaphoreType.DMA((5,)),
-        ],
-        compiler_params=params,
-        name="core_sum",
-    )(coords, keep_front, keep_deep, recv_front, recv_deep, small)
-    first = [parts[0]] + [swap_with(parts[k], line=k) for k in (1, 2, 3)]
-    first += [parts[4]] + [swap_with(parts[4 + k], zed=k) for k in (1, 2, 3)]
+    rest = 2 * SHARD - SCATTER_CUT
     parts = pl.pallas_call(
         first_sum_kernel,
         out_shape=(shape((2 * SCATTER_CUT + 64, quarter), BF16),) * 4 + (shape((2 * rest, quarter), BF16),) * 4,
-        in_specs=[SMEM] + [VMEM] * 8,
+        in_specs=[SMEM] + [VMEM] * 16,
         out_specs=(VMEM,) * 8,
         compiler_params=params,
         name="first_sum",
-    )(coords, *first)
+    )(coords, *front, *deep)
     second = [parts[0]] + [swap_with(parts[k], zed=k) for k in (1, 2, 3)]
     second += [parts[4]] + [swap_with(parts[4 + k], line=k) for k in (1, 2, 3)]
-    mine, other, small, squares = pl.pallas_call(
+    *outs, small, squares = pl.pallas_call(
         last_sum_kernel,
-        out_shape=(shape((line, quarter), F32),) * 2 + (shape((8, D), F32), shape((8, quarter), F32)),
+        out_shape=(shape((SHARD, quarter), F32),) * 4 + (shape((8, D), F32), shape((8, quarter), F32)),
         in_specs=[SMEM] + [VMEM] * 8,
-        out_specs=(VMEM,) * 4,
+        out_specs=(VMEM,) * 6,
+        scratch_shapes=[pltpu.VMEM((2 * SHARD, quarter), F32)],
         compiler_params=params,
         name="last_sum",
     )(coords, *second)
-    row, core = coords[0] // 2, coords[2]
-    theirs = swap_with(other, line=2)
-    half = jnp.concatenate(
-        [jnp.where(row == 0, mine, theirs), jnp.where(row == 0, theirs, mine)], 1
-    )
-    keep = jnp.where(core == 0, half[:SHARD], half[SHARD:])
-    send = jnp.where(core == 0, half[SHARD:], half[:SHARD])
-    back = swap_with(send, core=1)
-    owned = jnp.concatenate([jnp.where(core == 0, keep, back), jnp.where(core == 0, back, keep)], 1)
-    return owned, small, jnp.sum(squares)
-
-
-def sum_all(value):
-    value = jnp.broadcast_to(value, (8, 128))
-    value = value + swap_with(value, core=1)
-    for k in (1, 2):
-        value = value + swap_with(value, line=k)
-    for k in (1, 2):
-        value = value + swap_with(value, zed=k)
-    return value[0, 0]
-
-
-def adam(param, first_m, second_m, grad, decay):
-    first_new = BETA * first_m + (1.0 - BETA) * grad
-    second_new = BETA * second_m + (1.0 - BETA) * grad * grad
-    correct = 1.0 - BETA**STEP
-    update = -RATE * (
-        first_new / correct / (jnp.sqrt(second_new / correct) + EPS_ADAM) + decay * param
-    )
-    return (first_new, second_new, update)
+    squares = squares + swap_with(squares, core=1)
+    quarters = [outs[0], swap_with(outs[1], line=2), swap_with(outs[2], core=1), swap_with(outs[3], line=2, core=1)]
+    squares = (squares + swap_with(squares, line=1)) + (swap_with(squares, line=2) + swap_with(squares, line=3))
+    squares = [squares] + [swap_with(squares, zed=k) for k in (1, 2, 3)]
+    return quarters, small, squares
 
 
 def shards(byte_ids, layouts, weights, vectors, m_weights, v_weights, m_vectors, v_vectors):
@@ -908,7 +997,7 @@
     count = float(micro * layouts.shape[1] * devices * byte_ids.shape[2])
     lines, rest = lax.axis_size("dp"), lax.axis_size("fsdp")
     place = lax.axis_index("fsdp")
-    coords = jnp.stack([lax.axis_index("dp"), place // 2, place % 2, 0]).astype(jnp.int32)
+    coords = jnp.stack([lax.axis_index("dp"), place // 2, place % 2, lax.axis_index(AXES)]).astype(jnp.int32)
     paired = lines == 4 and rest == 8 and weights.shape[0] == SHARD
     weights_low = weights.astype(BF16)
     vectors_low = vectors.astype(BF16)
@@ -921,25 +1010,28 @@
         front, back = swap_halves(coords, weights_low)
         tail = lax.all_gather(back, AXES, axis=0, tiled=True)
         pieces = gather_pieces(front, vectors_low)
-        parts = device_grads(pieces, tail, None, coords, ids, flat_layouts, count, partial(swap_with, core=1))
-        owned, small, squares = scatter_sum(coords, *parts)
-        squares = sum_all(squares)
-    else:
-        coords = coords * 0
-        pieces = [lax.all_gather(weights_low, AXES, axis=0, tiled=True)]
-        vecs = lax.all_gather(vectors_low, AXES, axis=1, tiled=True)
-        vecs = jnp.pad(vecs.astype(F32), ((0, 2), (0, 0)))
-        parts = device_grads(pieces, None, vecs, coords, ids, flat_layouts, count, lambda array: array)
-        keep_front, send_front, keep_deep, send_deep, small = parts
-        local = jnp.concatenate(
-            [
-                jnp.concatenate([keep_front, send_front[:ROW_F1]], 1),
-                jnp.concatenate([keep_deep, send_deep], 1),
-            ],
-            0,
+        front, deep = device_grads(
+            pieces, tail, None, coords, ids, flat_layouts, count, True
         )
-        owned = lax.psum_scatter(local.astype(F32), AXES, scatter_dimension=0, tiled=True)
-        small, squares = lax.psum((small, jnp.sum(owned * owned)), AXES)
+        quarters, small, squares = scatter_sum(coords, front, deep)
+        like = [jax.ShapeDtypeStruct((1, 1), F32)] * 2
+        like += [jax.ShapeDtypeStruct(weights.shape, F32)] * 3 + [jax.ShapeDtypeStruct(vectors.shape, F32)] * 3
+        loss, grad_norm, *updated = pl.pallas_call(
+            partial(update_kernel, count),
+            out_shape=like,
+            in_specs=[SMEM] + [VMEM] * 15,
+            out_specs=[VMEM] * 8,
+            compiler_params=pltpu.CompilerParams(vmem_limit_bytes=LIMIT),
+            name="update",
+        )(coords, *quarters, *squares, small, weights, m_weights, v_weights, vectors, m_vectors, v_vectors)
+        return (loss[0, 0], grad_norm[0, 0], *updated)
+    coords = coords * 0
+    pieces = [lax.all_gather(weights_low, AXES, axis=0, tiled=True)]
+    vecs = lax.all_gather(vectors_low, AXES, axis=1, tiled=True)
+    vecs = jnp.pad(vecs.astype(F32), ((0, 2), (0, 0)))
+    local, small = device_grads(pieces, None, vecs, coords, ids, flat_layouts, count, False)
+    owned = lax.psum_scatter(local.astype(F32), AXES, scatter_dimension=0, tiled=True)
+    small, squares = lax.psum((small, jnp.sum(owned * owned)), AXES)
     loss = small[6, 0] / count
     vec_grads = small[:6]
     owned_vecs = lax.dynamic_slice(vec_grads, (0, mine), (6, width))

time: 300 us -> 294 us (0.980)
  Pallas kernels: 123 us -> 133 us
  waiting for transfers between devices: 82 us -> 72.7 us
  other arithmetic: 9.19 us -> 3.16 us
  starting transfers between devices: 58 us -> 62.5 us
  between operations: 18.9 us -> 14.7 us
    pallas_call x2 -> x5, Pallas kernels: 11.6 us -> 29.1 us  [the longest x1 13.4 us: device_grads(): pl.pallas_call(partial(front_back_kernel, number), out_shape=(shape((ROW_...]
    ppermute x42 -> x53, waiting for transfers between devices: 82 us -> 72.6 us  [swap_with(): return lax.ppermute(array, AXES, pairs)]
    pallas_call x1, Pallas kernels: 33.1 us -> 25.2 us  [device_grads(): pl.pallas_call(partial(attend_back_kernel, short_len, slots, number), out...]
    ppermute x42 -> x53, starting transfers between devices: 57.9 us -> 62.5 us  [swap_with(): return lax.ppermute(array, AXES, pairs)]
    unnamed x71 -> x93, local copies, waits for them, and re-layouts: 5.71 us -> 6.18 us
  transfers between devices with their start and end apart: 43 -> 54, of which waited for: 18 -> 20; matrix products, arithmetic and copies ran while one was open for 2% -> 1% of each run, Pallas kernels for 20% -> 25%
where the time goes in v4:
time: 294 us
  Pallas kernels  133 us (45%)
  waiting for transfers between devices  72.7 us (25%)
  starting transfers between devices  62.5 us (21%)
  between operations  14.7 us (5%)
  local copies, waits for them, and re-layouts  7.61 us (3%)
  other arithmetic  3.16 us (1%)
    ppermute x53, waiting for transfers between devices, swap_with(): return lax.ppermute(array, AXES, pairs)  72.6 us
    ppermute x53, starting transfers between devices, swap_with(): return lax.ppermute(array, AXES, pairs)  62.5 us
    pallas_call x1, Pallas kernels, device_grads(): pl.pallas_call(partial(deep_kernel, count, number), out_shape=(shape((ROW...  49 us
    pallas_call x1, Pallas kernels, device_grads(): pl.pallas_call(partial(attend_kernel, short_len, slots, number), out_shap...  25.8 us
    pallas_call x1, Pallas kernels, device_grads(): pl.pallas_call(partial(attend_back_kernel, short_len, slots, number), out...  25.2 us
    pallas_call x1, Pallas kernels, device_grads(): pl.pallas_call(partial(front_back_kernel, number), out_shape=(shape((ROW_...  13.4 us
    unnamed x93, local copies, waits for them, and re-layouts  6.18 us
  transfers between devices with their start and end apart: 54, of which 20 were waited for; matrix products, arithmetic and copies ran while one was open for 1% of the time, Pallas kernels for 25%

profile of v4, /device:TPU:0, one launch (start us, length us, event | category | flops | bytes accessed | tf_op | source)
XLA Modules:
  0.0 293.6 jit_solution(4220242391220662276)
XLA Ops:
  8.4 3.0 %collective-permute-start = (bf16[304,256]{1,0:T(8,128)(2,1)S(1)}, bf16[304,256]{1,0:T(8,128)(2,1)S(1)}, u32[]{:S(2)}, u32[]{:S(2)}) collective-permute-start(bf16[304,256]{1,0:T(8,128)(2,1)S(1)} %broadcast_select_fusion.3), channel_id=1, source_target_pairs={{0,16},{1,17},{2,18},{3,19},{4,20},{5,21},{6,22},{7,23},{8,24},{9,... | collective-permute-start | bytes 466952 | tf_op jit(solution)/shard_map/ppermute | solution.py:936
  11.4 4.0 %collective-permute-done = bf16[304,256]{1,0:T(8,128)(2,1)S(1)} collective-permute-done((bf16[304,256]{1,0:T(8,128)(2,1)S(1)}, bf16[304,256]{1,0:T(8,128)(2,1)S(1)}, u32[]{:S(2)}, u32[]{:S(2)}) %collective-permute-start) | collective-permute-done | bytes 155680 | tf_op jit(solution)/shard_map/ppermute | solution.py:936
  16.6 2.7 collective-permute-start.9
  20.2 4.1 %collective-permute-start.3 = (bf16[224,256]{1,0:T(8,128)(2,1)S(1)}, bf16[224,256]{1,0:T(8,128)(2,1)S(1)}, u32[]{:S(2)}, u32[]{:S(2)}) collective-permute-start(bf16[224,256]{1,0:T(8,128)(2,1)S(1)} %pad_maximum_fusion.1), channel_id=1, source_target_pairs={{0,6},{1,7},{2,4},{3,5},{4,2},{5,3},{6,0},{7,1},{8,14},{9,15},{10,... | collective-permute-start | bytes 344072 | tf_op jit(solution)/shard_map/ppermute | solution.py:936
  25.1 6.1 %collective-permute-done.1 = bf16[224,256]{1,0:T(8,128)(2,1)S(1)} collective-permute-done((bf16[224,256]{1,0:T(8,128)(2,1)S(1)}, bf16[224,256]{1,0:T(8,128)(2,1)S(1)}, u32[]{:S(2)}, u32[]{:S(2)}) %collective-permute-start.1) | collective-permute-done | bytes 114720 | tf_op jit(solution)/shard_map/ppermute | solution.py:936
  31.2 2.4 collective-permute-done.2
  33.6 2.5 collective-permute-start.6
  37.1 3.1 %collective-permute-start.12 = (bf16[384,256]{1,0:T(8,128)(2,1)S(1)}, bf16[384,256]{1,0:T(8,128)(2,1)S(1)}, u32[]{:S(2)}, u32[]{:S(2)}) collective-permute-start(bf16[384,256]{1,0:T(8,128)(2,1)S(1)} %pad_maximum_fusion.refs_4_), channel_id=1, source_target_pairs={{0,6},{1,7},{2,4},{3,5},{4,2},{5,3},{6,0},{7,1},{8,14},{9,15},{10,... | collective-permute-start | bytes 589832 | tf_op jit(solution)/shard_map/ppermute | solution.py:936
  40.2 5.6 %collective-permute-done.12.refs_7_ = bf16[384,256]{1,0:T(8,128)(2,1)S(1)} collective-permute-done((bf16[384,256]{1,0:T(8,128)(2,1)S(1)}, bf16[384,256]{1,0:T(8,128)(2,1)S(1)}, u32[]{:S(2)}, u32[]{:S(2)}) %collective-permute-start.12) | collective-permute-done | bytes 196640 | tf_op jit(solution)/shard_map/ppermute | solution.py:936
  45.8 7.5 %collective-permute-start.10 = (bf16[384,256]{1,0:T(8,128)(2,1)S(1)}, bf16[384,256]{1,0:T(8,128)(2,1)}, u32[]{:S(2)}, u32[]{:S(2)}) collective-permute-start(bf16[384,256]{1,0:T(8,128)(2,1)S(1)} %pad_maximum_fusion.refs_4_), channel_id=1, source_target_pairs={{0,2},{1,3},{2,0},{3,1},{4,6},{5,7},{6,4},{7,5},{8,10},{9,11},{10,... | collective-permute-start | bytes 589832 | tf_op jit(solution)/shard_map/ppermute | solution.py:936
  53.3 3.2 %collective-permute-done.11.refs_6_ = bf16[384,256]{1,0:T(8,128)(2,1)S(1)} collective-permute-done((bf16[384,256]{1,0:T(8,128)(2,1)S(1)}, bf16[384,256]{1,0:T(8,128)(2,1)S(1)}, u32[]{:S(2)}, u32[]{:S(2)}) %collective-permute-start.11) | collective-permute-done | bytes 196640 | tf_op jit(solution)/shard_map/ppermute | solution.py:936
  56.5 5.5 %collective-permute-done.10.refs_5_ = bf16[384,256]{1,0:T(8,128)(2,1)} collective-permute-done((bf16[384,256]{1,0:T(8,128)(2,1)S(1)}, bf16[384,256]{1,0:T(8,128)(2,1)}, u32[]{:S(2)}, u32[]{:S(2)}) %collective-permute-start.10) | collective-permute-done | bytes 196640 | tf_op jit(solution)/shard_map/ppermute | solution.py:936
  63.3 2.4 collective-permute-done.19.refs_14_
  69.2 25.8 %attend.1 = (bf16[768,1536]{1,0:T(8,128)(2,1)}, f32[768,512]{1,0:T(8,128)}, bf16[768,512]{1,0:T(8,128)(2,1)}, bf16[768,1536]{1,0:T(8,128)(2,1)}, f32[2,8,1,384]{...) custom-call(s32[4]{0:T(128)} %pad_add_fusion.coords_ref, ...), custom_call_target="tpu_custom_call" | custom-call | flops 8999999488 | bytes 20000000 | tf_op jit(solution)/shard_map/attend/pallas_call | solution.py:768
  95.0 49.0 %deep.1 = (bf16[1024,256]{1,0:T(8,128)(2,1)}, bf16[1024,256]{1,0:T(8,128)(2,1)}, bf16[4864,256]{1,0:T(8,128)(2,1)}, bf16[4864,256]{1,0:T(8,128)(2,1)}, f32[256,5...) custom-call(s32[4]{0:T(128)} %pad_add_fusion.coords_ref, s32[3,768,128]{2,1,0:T(8,128)} %get-tuple-element.91.cols_ref, ...), custom_call_target="tpu_custom_call" | custom-call | tf_op jit(solution)/shard_map/deep/pallas_call | solution.py:797
  144.6 25.2 %attend_back.1 = (bf16[2048,256]{1,0:T(8,128)(2,1)}, bf16[2048,256]{1,0:T(8,128)(2,1)}, bf16[768,1536]{1,0:T(8,128)(2,1)}) custom-call(s32[4]{0:T(128)} %pad_add_fusion.coords_ref, s32[2]{0:T(128)} %bitcast.12, f32[8]{0:T(128)} %constant.67.clone.slope_ref, f32[768,512]{1,0:T(8,128)} %get-tuple-element.107.dresid_ref, ...), custom_call_target="tpu_custom_call" | custom-call | flops 11000000512 | bytes 20000000 | tf_op jit(solution)/shard_map/attend_back/pallas_call | solution.py:832
  170.4 2.9 collective-permute-done.22.recv_mid
  173.3 1.4 copy-done
  174.8 4.4 %core_sum.1 = (bf16[1600,128]{1,0:T(8,128)(2,1)}, bf16[1600,128]{1,0:T(8,128)(2,1)}, bf16[1600,128]{1,0:T(8,128)(2,1)}, bf16[1600,128]{1,0:T(8,128)(2,1)}, bf16[...) custom-call(s32[4]{0:T(128)} %pad_add_fusion.coords_ref, ...), custom_call_target="tpu_custom_call" | custom-call | tf_op jit(solution)/shard_map/core_sum/pallas_call | solution.py:914
  179.6 2.1 collective-permute-start.28
  181.7 1.4 collective-permute-start.24
  183.1 1.4 collective-permute-start.25
  185.2 13.4 %front_back.1 = (bf16[1792,256]{1,0:T(8,128)(2,1)}, bf16[1824,256]{1,0:T(8,128)(2,1)}, f32[8,512]{1,0:T(8,128)}) custom-call(s32[4]{0:T(128)} %pad_add_fusion.coords_ref, s32[16,768]{1,0:T(8,128)} %get-tuple-element.92.lines_ref, f32[8,512]{1,0:T(8,128)} %get-tuple-element.93.vec_ref, f32[768,512]{1,0:T(8,128)} %get-tuple-element.107.dresid_ref, ...), custom_call_target="tpu_custom_call" | custom-call | flops 8000000000 | bytes 20000000 | tf_op jit(solution)/shard_map/front_back/pallas_call | solution.py:860
  198.7 4.4 %collective-permute-done.25.refs_10_ = bf16[1600,128]{1,0:T(8,128)(2,1)S(1)} collective-permute-done((bf16[1600,128]{1,0:T(8,128)(2,1)}, bf16[1600,128]{1,0:T(8,128)(2,1)S(1)}, u32[]{:S(2)}, u32[]{:S(2)}) %collective-permute-start.25) | collective-permute-done | bytes 409632 | tf_op jit(solution)/shard_map/ppermute | solution.py:936
  203.1 1.2 collective-permute-start.36
  204.3 1.5 collective-permute-done.29.recv_front
  206.8 5.1 %core_sum_front.1 = (bf16[1664,128]{1,0:T(8,128)(2,1)}, bf16[1664,128]{1,0:T(8,128)(2,1)}, bf16[1664,128]{1,0:T(8,128)(2,1)}, bf16[1664,128]{1,0:T(8,128)(2,1)},...) custom-call(s32[4]{0:T(128)} %pad_add_fusion.coords_ref, ...), custom_call_target="tpu_custom_call" | custom-call | tf_op jit(solution)/shard_map/core_sum_front/pallas_call | solution.py:888
  211.9 1.2 collective-permute-start.33
  214.7 1.8 collective-permute-start.32
  216.6 1.3 collective-permute-start.34
  217.8 2.4 collective-permute-done.33.refs_5_
  221.3 13.0 %collective-permute-done.34.refs_6_ = bf16[832,128]{1,0:T(8,128)(2,1)S(1)} collective-permute-done((bf16[832,128]{1,0:T(8,128)(2,1)}, bf16[832,128]{1,0:T(8,128)(2,1)S(1)}, u32[]{:S(2)}, u32[]{:S(2)}) %collective-permute-start.34) | collective-permute-done | bytes 213024 | tf_op jit(solution)/shard_map/ppermute | solution.py:936
  235.6 3.8 %first_sum.1 = (bf16[864,128]{1,0:T(8,128)(2,1)}, bf16[864,128]{1,0:T(8,128)(2,1)}, bf16[864,128]{1,0:T(8,128)(2,1)}, bf16[864,128]{1,0:T(8,128)(2,1)}, bf16[416...) custom-call(s32[4]{0:T(128)} %pad_add_fusion.coords_ref, ...), custom_call_target="tpu_custom_call" | custom-call | tf_op jit(solution)/shard_map/first_sum/pallas_call | solution.py:968
  239.4 3.7 %collective-permute-start.37 = (bf16[864,128]{1,0:T(8,128)(2,1)}, bf16[864,128]{1,0:T(8,128)(2,1)S(1)}, u32[]{:S(2)}, u32[]{:S(2)}) collective-permute-start(bf16[864,128]{1,0:T(8,128)(2,1)} %get-tuple-element.153), channel_id=1, source_target_pairs={{0,2},{1,3},{2,0},{3,1},{4,6},{5,7},{6,4},{7,5},{8,10},{9,11},{10,... | collective-permute-start | bytes 663560 | tf_op jit(solution)/shard_map/ppermute | solution.py:936
  243.7 1.8 collective-permute-start.39
  247.2 3.2 %collective-permute-done.40.refs_5_ = bf16[416,128]{1,0:T(8,128)(2,1)S(1)} collective-permute-done((bf16[416,128]{1,0:T(8,128)(2,1)}, bf16[416,128]{1,0:T(8,128)(2,1)S(1)}, u32[]{:S(2)}, u32[]{:S(2)}) %collective-permute-start.40) | collective-permute-done | bytes 106528 | tf_op jit(solution)/shard_map/ppermute | solution.py:936
  250.4 1.2 collective-permute-start.42
  251.6 4.7 %collective-permute-done.42.refs_7_ = bf16[416,128]{1,0:T(8,128)(2,1)S(1)} collective-permute-done((bf16[416,128]{1,0:T(8,128)(2,1)}, bf16[416,128]{1,0:T(8,128)(2,1)S(1)}, u32[]{:S(2)}, u32[]{:S(2)}) %collective-permute-start.42) | collective-permute-done | bytes 106528 | tf_op jit(solution)/shard_map/ppermute | solution.py:936
  256.3 5.6 %collective-permute-done.38.refs_2_ = bf16[864,128]{1,0:T(8,128)(2,1)S(1)} collective-permute-done((bf16[864,128]{1,0:T(8,128)(2,1)}, bf16[864,128]{1,0:T(8,128)(2,1)S(1)}, u32[]{:S(2)}, u32[]{:S(2)}) %collective-permute-start.38) | collective-permute-done | bytes 221216 | tf_op jit(solution)/shard_map/ppermute | solution.py:936
  262.6 2.5 last_sum.1
  265.1 1.4 collective-permute-done.46
  268.2 1.4 collective-permute-start.48
  270.6 1.4 collective-permute-start.43
  273.3 1.9 collective-permute-start.52
  275.1 2.6 collective-permute-start.51
  278.7 1.2 collective-permute-start.50
  279.9 2.4 collective-permute-done.50.q1
  283.1 3.7 %update.1 = (f32[1,1]{1,0:T(1,128)}, f32[1,1]{1,0:T(1,128)}, f32[304,512]{1,0:T(8,128)}, f32[304,512]{1,0:T(8,128)}, f32[304,512]{1,0:T(8,128)}, /*index=5*/f32[...) custom-call(s32[4]{0:T(128)} %pad_add_fusion.coords_ref, f32[304,128]{1,0:T(8,128)} %get-tuple-element.160.g0, ...), custom_call_target="tpu_custom_call" | custom-call | tf_op jit(solution)/shard_map/update/pallas_call | solution.py:1019
  (181 shorter events, 25.6 us)
Async XLA Ops:
  7.2 87.8 %all-gather.2.cloned.1.call-start = ((), (), s32[]{:S(2)}) async-start(), calls=%async_computation | async-start | bytes 5136384 | tf_op jit(solution)/shard_map/all_gather | solution.py:1011
  8.4 7.1 %collective-permute-start = (bf16[304,256]{1,0:T(8,128)(2,1)S(1)}, bf16[304,256]{1,0:T(8,128)(2,1)S(1)}, u32[]{:S(2)}, u32[]{:S(2)}) collective-permute-start(bf16[304,256]{1,0:T(8,128)(2,1)S(1)} %broadcast_select_fusion.3), channel_id=1, source_target_pairs={{0,16},{1,17},{2,18},{3,19},{4,20},{5,21},{6,22},{7,23},{8,24},{9,... | collective-permute-start | bytes 466952 | tf_op jit(solution)/shard_map/ppermute | solution.py:936
  16.6 7.7 %collective-permute-start.9 = (bf16[96,256]{1,0:T(8,128)(2,1)S(1)}, bf16[96,256]{1,0:T(8,128)(2,1)S(1)}, u32[]{:S(2)}, u32[]{:S(2)}) collective-permute-start(bf16[96,256]{1,0:T(8,128)(2,1)S(1)} %slice.19), channel_id=1, source_target_pairs={{0,24},{1,25},{2,26},{3,27},{4,28},{5,29},{6,30},{7,31},{8,16},{9,... | collective-permute-start | bytes 147464 | tf_op jit(solution)/shard_map/ppermute | solution.py:936
  19.3 5.7 %collective-permute-start.8 = (bf16[96,256]{1,0:T(8,128)(2,1)S(1)}, bf16[96,256]{1,0:T(8,128)(2,1)S(1)}, u32[]{:S(2)}, u32[]{:S(2)}) collective-permute-start(bf16[96,256]{1,0:T(8,128)(2,1)S(1)} %slice.19), channel_id=1, source_target_pairs={{0,16},{1,17},{2,18},{3,19},{4,20},{5,21},{6,22},{7,23},{8,24},{9,... | collective-permute-start | bytes 147464 | tf_op jit(solution)/shard_map/ppermute | solution.py:936
  19.8 5.2 %collective-permute-start.7 = (bf16[96,256]{1,0:T(8,128)(2,1)S(1)}, bf16[96,256]{1,0:T(8,128)(2,1)S(1)}, u32[]{:S(2)}, u32[]{:S(2)}) collective-permute-start(bf16[96,256]{1,0:T(8,128)(2,1)S(1)} %slice.19), channel_id=1, source_target_pairs={{0,8},{1,9},{2,10},{3,11},{4,12},{5,13},{6,14},{7,15},{8,0},{9,1},... | collective-permute-start | bytes 147464 | tf_op jit(solution)/shard_map/ppermute | solution.py:936
  20.2 13.3 %collective-permute-start.3 = (bf16[224,256]{1,0:T(8,128)(2,1)S(1)}, bf16[224,256]{1,0:T(8,128)(2,1)S(1)}, u32[]{:S(2)}, u32[]{:S(2)}) collective-permute-start(bf16[224,256]{1,0:T(8,128)(2,1)S(1)} %pad_maximum_fusion.1), channel_id=1, source_target_pairs={{0,6},{1,7},{2,4},{3,5},{4,2},{5,3},{6,0},{7,1},{8,14},{9,15},{10,... | collective-permute-start | bytes 344072 | tf_op jit(solution)/shard_map/ppermute | solution.py:936
  24.3 9.2 %collective-permute-start.2 = (bf16[224,256]{1,0:T(8,128)(2,1)S(1)}, bf16[224,256]{1,0:T(8,128)(2,1)S(1)}, u32[]{:S(2)}, u32[]{:S(2)}) collective-permute-start(bf16[224,256]{1,0:T(8,128)(2,1)S(1)} %pad_maximum_fusion.1), channel_id=1, source_target_pairs={{0,4},{1,5},{2,6},{3,7},{4,0},{5,1},{6,2},{7,3},{8,12},{9,13},{10,... | collective-permute-start | bytes 344072 | tf_op jit(solution)/shard_map/ppermute | solution.py:936
  24.3 6.8 %collective-permute-start.1 = (bf16[224,256]{1,0:T(8,128)(2,1)S(1)}, bf16[224,256]{1,0:T(8,128)(2,1)S(1)}, u32[]{:S(2)}, u32[]{:S(2)}) collective-permute-start(bf16[224,256]{1,0:T(8,128)(2,1)S(1)} %pad_maximum_fusion.1), channel_id=1, source_target_pairs={{0,2},{1,3},{2,0},{3,1},{4,6},{5,7},{6,4},{7,5},{8,10},{9,11},{10,... | collective-permute-start | bytes 344072 | tf_op jit(solution)/shard_map/ppermute | solution.py:936
  25.0 15.2 %collective-permute-start.17 = (bf16[384,256]{1,0:T(8,128)(2,1)S(1)}, bf16[384,256]{1,0:T(8,128)(2,1)S(1)}, u32[]{:S(2)}, u32[]{:S(2)}) collective-permute-start(bf16[384,256]{1,0:T(8,128)(2,1)S(1)} %pad_maximum_fusion.refs_4_), channel_id=1, source_target_pairs={{0,1},{1,0},{2,3},{3,2},{4,5},{5,4},{6,7},{7,6},{8,9},{9,8},{10,11... | collective-permute-start | bytes 589832 | tf_op jit(solution)/shard_map/ppermute | solution.py:936
  33.6 28.5 %collective-permute-start.6 = (bf16[896,256]{1,0:T(8,128)(2,1)S(1)}, bf16[896,256]{1,0:T(8,128)(2,1)S(1)}, u32[]{:S(2)}, u32[]{:S(2)}) collective-permute-start(bf16[896,256]{1,0:T(8,128)(2,1)S(1)} %constant_dynamic-update-slice_fusion.refs_0_), channel_id=1, source_target_pairs={{0,24},{1,25},{2,26},{3,27},{4,28},{5,29},{6,30},{7,31},{8,16},{9,... | collective-permute-start | bytes 1376264 | tf_op jit(solution)/shard_map/ppermute | solution.py:936
  36.0 26.5 %collective-permute-start.5 = (bf16[896,256]{1,0:T(8,128)(2,1)S(1)}, bf16[896,256]{1,0:T(8,128)(2,1)S(1)}, u32[]{:S(2)}, u32[]{:S(2)}) collective-permute-start(bf16[896,256]{1,0:T(8,128)(2,1)S(1)} %constant_dynamic-update-slice_fusion.refs_0_), channel_id=1, source_target_pairs={{0,16},{1,17},{2,18},{3,19},{4,20},{5,21},{6,22},{7,23},{8,24},{9,... | collective-permute-start | bytes 1376264 | tf_op jit(solution)/shard_map/ppermute | solution.py:936
  36.5 26.1 %collective-permute-start.4 = (bf16[896,256]{1,0:T(8,128)(2,1)S(1)}, bf16[896,256]{1,0:T(8,128)(2,1)S(1)}, u32[]{:S(2)}, u32[]{:S(2)}) collective-permute-start(bf16[896,256]{1,0:T(8,128)(2,1)S(1)} %constant_dynamic-update-slice_fusion.refs_0_), channel_id=1, source_target_pairs={{0,8},{1,9},{2,10},{3,11},{4,12},{5,13},{6,14},{7,15},{8,0},{9,1},... | collective-permute-start | bytes 1376264 | tf_op jit(solution)/shard_map/ppermute | solution.py:936
  37.1 8.7 %collective-permute-start.12 = (bf16[384,256]{1,0:T(8,128)(2,1)S(1)}, bf16[384,256]{1,0:T(8,128)(2,1)S(1)}, u32[]{:S(2)}, u32[]{:S(2)}) collective-permute-start(bf16[384,256]{1,0:T(8,128)(2,1)S(1)} %pad_maximum_fusion.refs_4_), channel_id=1, source_target_pairs={{0,6},{1,7},{2,4},{3,5},{4,2},{5,3},{6,0},{7,1},{8,14},{9,15},{10,... | collective-permute-start | bytes 589832 | tf_op jit(solution)/shard_map/ppermute | solution.py:936
  40.2 16.3 %collective-permute-start.11 = (bf16[384,256]{1,0:T(8,128)(2,1)S(1)}, bf16[384,256]{1,0:T(8,128)(2,1)S(1)}, u32[]{:S(2)}, u32[]{:S(2)}) collective-permute-start(bf16[384,256]{1,0:T(8,128)(2,1)S(1)} %pad_maximum_fusion.refs_4_), channel_id=1, source_target_pairs={{0,4},{1,5},{2,6},{3,7},{4,0},{5,1},{6,2},{7,3},{8,12},{9,13},{10,... | collective-permute-start | bytes 589832 | tf_op jit(solution)/shard_map/ppermute | solution.py:936
  45.8 16.3 %collective-permute-start.10 = (bf16[384,256]{1,0:T(8,128)(2,1)S(1)}, bf16[384,256]{1,0:T(8,128)(2,1)}, u32[]{:S(2)}, u32[]{:S(2)}) collective-permute-start(bf16[384,256]{1,0:T(8,128)(2,1)S(1)} %pad_maximum_fusion.refs_4_), channel_id=1, source_target_pairs={{0,2},{1,3},{2,0},{3,1},{4,6},{5,7},{6,4},{7,5},{8,10},{9,11},{10,... | collective-permute-start | bytes 589832 | tf_op jit(solution)/shard_map/ppermute | solution.py:936
  56.5 6.6 %collective-permute-start.20 = (bf16[384,256]{1,0:T(8,128)(2,1)S(1)}, bf16[384,256]{1,0:T(8,128)(2,1)S(1)}, u32[]{:S(2)}, u32[]{:S(2)}) collective-permute-start(bf16[384,256]{1,0:T(8,128)(2,1)S(1)} %collective-permute-done.12.refs_7_), channel_id=1, source_target_pairs={{0,1},{1,0},{2,3},{3,2},{4,5},{5,4},{6,7},{7,6},{8,9},{9,8},{10,11... | collective-permute-start | bytes 589832 | tf_op jit(solution)/shard_map/ppermute | solution.py:936
  62.1 6.2 %collective-permute-start.13 = (bf16[896,256]{1,0:T(8,128)(2,1)S(1)}, bf16[896,256]{1,0:T(8,128)(2,1)S(1)}, u32[]{:S(2)}, u32[]{:S(2)}) collective-permute-start(bf16[896,256]{1,0:T(8,128)(2,1)S(1)} %constant_dynamic-update-slice_fusion.refs_0_), channel_id=1, source_target_pairs={{0,1},{1,0},{2,3},{3,2},{4,5},{5,4},{6,7},{7,6},{8,9},{9,8},{10,11... | collective-permute-start | bytes 1376264 | tf_op jit(solution)/shard_map/ppermute | solution.py:936
  62.1 6.2 %collective-permute-start.16 = (bf16[896,256]{1,0:T(8,128)(2,1)S(1)}, bf16[896,256]{1,0:T(8,128)(2,1)S(1)}, u32[]{:S(2)}, u32[]{:S(2)}) collective-permute-start(bf16[896,256]{1,0:T(8,128)(2,1)S(1)} %collective-permute-done.6.refs_3_), channel_id=1, source_target_pairs={{0,1},{1,0},{2,3},{3,2},{4,5},{5,4},{6,7},{7,6},{8,9},{9,8},{10,11... | collective-permute-start | bytes 1376264 | tf_op jit(solution)/shard_map/ppermute | solution.py:936
  62.6 5.7 %collective-permute-start.15 = (bf16[896,256]{1,0:T(8,128)(2,1)S(1)}, bf16[896,256]{1,0:T(8,128)(2,1)}, u32[]{:S(2)}, u32[]{:S(2)}) collective-permute-start(bf16[896,256]{1,0:T(8,128)(2,1)S(1)} %collective-permute-done.5.refs_2_), channel_id=1, source_target_pairs={{0,1},{1,0},{2,3},{3,2},{4,5},{5,4},{6,7},{7,6},{8,9},{9,8},{10,11... | collective-permute-start | bytes 1376264 | tf_op jit(solution)/shard_map/ppermute | solution.py:936
  62.7 5.6 %collective-permute-start.14 = (bf16[896,256]{1,0:T(8,128)(2,1)S(1)}, bf16[896,256]{1,0:T(8,128)(2,1)}, u32[]{:S(2)}, u32[]{:S(2)}) collective-permute-start(bf16[896,256]{1,0:T(8,128)(2,1)S(1)} %collective-permute-done.4.refs_1_), channel_id=1, source_target_pairs={{0,1},{1,0},{2,3},{3,2},{4,5},{5,4},{6,7},{7,6},{8,9},{9,8},{10,11... | collective-permute-start | bytes 1376264 | tf_op jit(solution)/shard_map/ppermute | solution.py:936
  144.1 29.3 %collective-permute-start.21 = (bf16[4864,256]{1,0:T(8,128)(2,1)}, bf16[4864,256]{1,0:T(8,128)(2,1)S(1)}, u32[]{:S(2)}, u32[]{:S(2)}) collective-permute-start(bf16[4864,256]{1,0:T(8,128)(2,1)} %get-tuple-element.96), channel_id=1, source_target_pairs={{0,1},{1,0},{2,3},{3,2},{4,5},{5,4},{6,7},{7,6},{8,9},{9,8},{10,11... | collective-permute-start | bytes 7471112 | tf_op jit(solution)/shard_map/ppermute | solution.py:936
  169.8 9.4 %collective-permute-start.23 = (bf16[2048,256]{1,0:T(8,128)(2,1)}, bf16[2048,256]{1,0:T(8,128)(2,1)S(1)}, u32[]{:S(2)}, u32[]{:S(2)}) collective-permute-start(bf16[2048,256]{1,0:T(8,128)(2,1)} %get-tuple-element.112), channel_id=1, source_target_pairs={{0,1},{1,0},{2,3},{3,2},{4,5},{5,4},{6,7},{7,6},{8,9},{9,8},{10,11... | collective-permute-start | bytes 3145736 | tf_op jit(solution)/shard_map/ppermute | solution.py:936
  179.2 19.4 %collective-permute-start.27 = (bf16[832,128]{1,0:T(8,128)(2,1)}, bf16[832,128]{1,0:T(8,128)(2,1)S(1)}, u32[]{:S(2)}, u32[]{:S(2)}) collective-permute-start(bf16[832,128]{1,0:T(8,128)(2,1)} %get-tuple-element.119), channel_id=1, source_target_pairs={{0,4},{1,5},{2,6},{3,7},{4,0},{5,1},{6,2},{7,3},{8,12},{9,13},{10,... | collective-permute-start | bytes 638984 | tf_op jit(solution)/shard_map/ppermute | solution.py:936
  179.6 19.0 %collective-permute-start.28 = (bf16[832,128]{1,0:T(8,128)(2,1)}, bf16[832,128]{1,0:T(8,128)(2,1)S(1)}, u32[]{:S(2)}, u32[]{:S(2)}) collective-permute-start(bf16[832,128]{1,0:T(8,128)(2,1)} %get-tuple-element.120), channel_id=1, source_target_pairs={{0,6},{1,7},{2,4},{3,5},{4,2},{5,3},{6,0},{7,1},{8,14},{9,15},{10,... | collective-permute-start | bytes 638984 | tf_op jit(solution)/shard_map/ppermute | solution.py:936
  181.7 16.9 %collective-permute-start.24 = (bf16[1600,128]{1,0:T(8,128)(2,1)}, bf16[1600,128]{1,0:T(8,128)(2,1)S(1)}, u32[]{:S(2)}, u32[]{:S(2)}) collective-permute-start(bf16[1600,128]{1,0:T(8,128)(2,1)} %get-tuple-element.115), channel_id=1, source_target_pairs={{0,8},{1,9},{2,10},{3,11},{4,12},{5,13},{6,14},{7,15},{8,0},{9,1},... | collective-permute-start | bytes 1228808 | tf_op jit(solution)/shard_map/ppermute | solution.py:936
  183.1 19.9 %collective-permute-start.25 = (bf16[1600,128]{1,0:T(8,128)(2,1)}, bf16[1600,128]{1,0:T(8,128)(2,1)S(1)}, u32[]{:S(2)}, u32[]{:S(2)}) collective-permute-start(bf16[1600,128]{1,0:T(8,128)(2,1)} %get-tuple-element.116), channel_id=1, source_target_pairs={{0,16},{1,17},{2,18},{3,19},{4,20},{5,21},{6,22},{7,23},{8,24},{9,... | collective-permute-start | bytes 1228808 | tf_op jit(solution)/shard_map/ppermute | solution.py:936
  184.5 18.5 %collective-permute-start.26 = (bf16[1600,128]{1,0:T(8,128)(2,1)}, bf16[1600,128]{1,0:T(8,128)(2,1)S(1)}, u32[]{:S(2)}, u32[]{:S(2)}) collective-permute-start(bf16[1600,128]{1,0:T(8,128)(2,1)} %get-tuple-element.117), channel_id=1, source_target_pairs={{0,24},{1,25},{2,26},{3,27},{4,28},{5,29},{6,30},{7,31},{8,16},{9,... | collective-permute-start | bytes 1228808 | tf_op jit(solution)/shard_map/ppermute | solution.py:936
  203.1 13.4 %collective-permute-start.36 = (bf16[832,128]{1,0:T(8,128)(2,1)S(1)}, bf16[832,128]{1,0:T(8,128)(2,1)S(1)}, u32[]{:S(2)}, u32[]{:S(2)}) collective-permute-start(bf16[832,128]{1,0:T(8,128)(2,1)S(1)} %copy-done.44), channel_id=1, source_target_pairs={{0,2},{1,3},{2,0},{3,1},{4,6},{5,7},{6,4},{7,5},{8,10},{9,11},{10,... | collective-permute-start | bytes 638984 | tf_op jit(solution)/shard_map/ppermute | solution.py:936
  211.9 8.3 %collective-permute-start.33 = (bf16[832,128]{1,0:T(8,128)(2,1)}, bf16[832,128]{1,0:T(8,128)(2,1)S(1)}, u32[]{:S(2)}, u32[]{:S(2)}) collective-permute-start(bf16[832,128]{1,0:T(8,128)(2,1)} %get-tuple-element.141), channel_id=1, source_target_pairs={{0,2},{1,3},{2,0},{3,1},{4,6},{5,7},{6,4},{7,5},{8,10},{9,11},{10,... | collective-permute-start | bytes 638984 | tf_op jit(solution)/shard_map/ppermute | solution.py:936
  213.1 21.2 %collective-permute-start.30 = (bf16[1664,128]{1,0:T(8,128)(2,1)}, bf16[1664,128]{1,0:T(8,128)(2,1)S(1)}, u32[]{:S(2)}, u32[]{:S(2)}) collective-permute-start(bf16[1664,128]{1,0:T(8,128)(2,1)} %get-tuple-element.137), channel_id=1, source_target_pairs={{0,8},{1,9},{2,10},{3,11},{4,12},{5,13},{6,14},{7,15},{8,0},{9,1},... | collective-permute-start | bytes 1277960 | tf_op jit(solution)/shard_map/ppermute | solution.py:936
  214.2 20.1 %collective-permute-start.31 = (bf16[1664,128]{1,0:T(8,128)(2,1)}, bf16[1664,128]{1,0:T(8,128)(2,1)S(1)}, u32[]{:S(2)}, u32[]{:S(2)}) collective-permute-start(bf16[1664,128]{1,0:T(8,128)(2,1)} %get-tuple-element.138), channel_id=1, source_target_pairs={{0,16},{1,17},{2,18},{3,19},{4,20},{5,21},{6,22},{7,23},{8,24},{9,... | collective-permute-start | bytes 1277960 | tf_op jit(solution)/shard_map/ppermute | solution.py:936
  214.7 20.1 %collective-permute-start.32 = (bf16[1664,128]{1,0:T(8,128)(2,1)}, bf16[1664,128]{1,0:T(8,128)(2,1)S(1)}, u32[]{:S(2)}, u32[]{:S(2)}) collective-permute-start(bf16[1664,128]{1,0:T(8,128)(2,1)} %get-tuple-element.139), channel_id=1, source_target_pairs={{0,24},{1,25},{2,26},{3,27},{4,28},{5,29},{6,30},{7,31},{8,16},{9,... | collective-permute-start | bytes 1277960 | tf_op jit(solution)/shard_map/ppermute | solution.py:936
  216.6 17.7 %collective-permute-start.34 = (bf16[832,128]{1,0:T(8,128)(2,1)}, bf16[832,128]{1,0:T(8,128)(2,1)S(1)}, u32[]{:S(2)}, u32[]{:S(2)}) collective-permute-start(bf16[832,128]{1,0:T(8,128)(2,1)} %get-tuple-element.142), channel_id=1, source_target_pairs={{0,4},{1,5},{2,6},{3,7},{4,0},{5,1},{6,2},{7,3},{8,12},{9,13},{10,... | collective-permute-start | bytes 638984 | tf_op jit(solution)/shard_map/ppermute | solution.py:936
  220.2 14.1 %collective-permute-start.35 = (bf16[832,128]{1,0:T(8,128)(2,1)}, bf16[832,128]{1,0:T(8,128)(2,1)S(1)}, u32[]{:S(2)}, u32[]{:S(2)}) collective-permute-start(bf16[832,128]{1,0:T(8,128)(2,1)} %get-tuple-element.143), channel_id=1, source_target_pairs={{0,6},{1,7},{2,4},{3,5},{4,2},{5,3},{6,0},{7,1},{8,14},{9,15},{10,... | collective-permute-start | bytes 638984 | tf_op jit(solution)/shard_map/ppermute | solution.py:936
  239.4 16.8 %collective-permute-start.37 = (bf16[864,128]{1,0:T(8,128)(2,1)}, bf16[864,128]{1,0:T(8,128)(2,1)S(1)}, u32[]{:S(2)}, u32[]{:S(2)}) collective-permute-start(bf16[864,128]{1,0:T(8,128)(2,1)} %get-tuple-element.153), channel_id=1, source_target_pairs={{0,2},{1,3},{2,0},{3,1},{4,6},{5,7},{6,4},{7,5},{8,10},{9,11},{10,... | collective-permute-start | bytes 663560 | tf_op jit(solution)/shard_map/ppermute | solution.py:936
  243.1 18.8 %collective-permute-start.38 = (bf16[864,128]{1,0:T(8,128)(2,1)}, bf16[864,128]{1,0:T(8,128)(2,1)S(1)}, u32[]{:S(2)}, u32[]{:S(2)}) collective-permute-start(bf16[864,128]{1,0:T(8,128)(2,1)} %get-tuple-element.154), channel_id=1, source_target_pairs={{0,4},{1,5},{2,6},{3,7},{4,0},{5,1},{6,2},{7,3},{8,12},{9,13},{10,... | collective-permute-start | bytes 663560 | tf_op jit(solution)/shard_map/ppermute | solution.py:936
  243.7 18.1 %collective-permute-start.39 = (bf16[864,128]{1,0:T(8,128)(2,1)}, bf16[864,128]{1,0:T(8,128)(2,1)S(1)}, u32[]{:S(2)}, u32[]{:S(2)}) collective-permute-start(bf16[864,128]{1,0:T(8,128)(2,1)} %get-tuple-element.155), channel_id=1, source_target_pairs={{0,6},{1,7},{2,4},{3,5},{4,2},{5,3},{6,0},{7,1},{8,14},{9,15},{10,... | collective-permute-start | bytes 663560 | tf_op jit(solution)/shard_map/ppermute | solution.py:936
  245.5 4.9 %collective-permute-start.40 = (bf16[416,128]{1,0:T(8,128)(2,1)}, bf16[416,128]{1,0:T(8,128)(2,1)S(1)}, u32[]{:S(2)}, u32[]{:S(2)}) collective-permute-start(bf16[416,128]{1,0:T(8,128)(2,1)} %get-tuple-element.157), channel_id=1, source_target_pairs={{0,8},{1,9},{2,10},{3,11},{4,12},{5,13},{6,14},{7,15},{8,0},{9,1},... | collective-permute-start | bytes 319496 | tf_op jit(solution)/shard_map/ppermute | solution.py:936
  246.6 5.0 %collective-permute-start.41 = (bf16[416,128]{1,0:T(8,128)(2,1)}, bf16[416,128]{1,0:T(8,128)(2,1)S(1)}, u32[]{:S(2)}, u32[]{:S(2)}) collective-permute-start(bf16[416,128]{1,0:T(8,128)(2,1)} %get-tuple-element.158), channel_id=1, source_target_pairs={{0,16},{1,17},{2,18},{3,19},{4,20},{5,21},{6,22},{7,23},{8,24},{9,... | collective-permute-start | bytes 319496 | tf_op jit(solution)/shard_map/ppermute | solution.py:936
  250.4 5.8 %collective-permute-start.42 = (bf16[416,128]{1,0:T(8,128)(2,1)}, bf16[416,128]{1,0:T(8,128)(2,1)S(1)}, u32[]{:S(2)}, u32[]{:S(2)}) collective-permute-start(bf16[416,128]{1,0:T(8,128)(2,1)} %get-tuple-element.159), channel_id=1, source_target_pairs={{0,24},{1,25},{2,26},{3,27},{4,28},{5,29},{6,30},{7,31},{8,16},{9,... | collective-permute-start | bytes 319496 | tf_op jit(solution)/shard_map/ppermute | solution.py:936
  267.2 4.9 %collective-permute-start.49 = (f32[8,128]{1,0:T(8,128)S(1)}, f32[8,128]{1,0:T(8,128)S(1)}, u32[]{:S(2)}, u32[]{:S(2)}) collective-permute-start(f32[8,128]{1,0:T(8,128)S(1)} %add.39), channel_id=1, source_target_pairs={{0,24},{1,25},{2,26},{3,27},{4,28},{5,29},{6,30},{7,31},{8,16},{9,... | collective-permute-start | bytes 12296 | tf_op jit(solution)/shard_map/ppermute | solution.py:936
  268.2 4.5 %collective-permute-start.48 = (f32[8,128]{1,0:T(8,128)S(1)}, f32[8,128]{1,0:T(8,128)S(1)}, u32[]{:S(2)}, u32[]{:S(2)}) collective-permute-start(f32[8,128]{1,0:T(8,128)S(1)} %add.39), channel_id=1, source_target_pairs={{0,16},{1,17},{2,18},{3,19},{4,20},{5,21},{6,22},{7,23},{8,24},{9,... | collective-permute-start | bytes 12296 | tf_op jit(solution)/shard_map/ppermute | solution.py:936
  269.7 3.6 %collective-permute-start.47 = (f32[8,128]{1,0:T(8,128)S(1)}, f32[8,128]{1,0:T(8,128)S(1)}, u32[]{:S(2)}, u32[]{:S(2)}) collective-permute-start(f32[8,128]{1,0:T(8,128)S(1)} %add.39), channel_id=1, source_target_pairs={{0,8},{1,9},{2,10},{3,11},{4,12},{5,13},{6,14},{7,15},{8,0},{9,1},... | collective-permute-start | bytes 12296 | tf_op jit(solution)/shard_map/ppermute | solution.py:936
  270.6 11.7 %collective-permute-start.43 = (f32[304,128]{1,0:T(8,128)}, f32[304,128]{1,0:T(8,128)S(1)}, u32[]{:S(2)}, u32[]{:S(2)}) collective-permute-start(f32[304,128]{1,0:T(8,128)} %get-tuple-element.161), channel_id=1, source_target_pairs={{0,16},{1,17},{2,18},{3,19},{4,20},{5,21},{6,22},{7,23},{8,24},{9,... | collective-permute-start | bytes 466952 | tf_op jit(solution)/shard_map/ppermute | solution.py:936
  272.1 10.3 %collective-permute-start.44 = (f32[304,128]{1,0:T(8,128)}, f32[304,128]{1,0:T(8,128)S(1)}, u32[]{:S(2)}, u32[]{:S(2)}) collective-permute-start(f32[304,128]{1,0:T(8,128)} %get-tuple-element.162), channel_id=1, source_target_pairs={{0,1},{1,0},{2,3},{3,2},{4,5},{5,4},{6,7},{7,6},{8,9},{9,8},{10,11... | collective-permute-start | bytes 466952 | tf_op jit(solution)/shard_map/ppermute | solution.py:936
  272.1 10.3 %collective-permute-start.45 = (f32[304,128]{1,0:T(8,128)}, f32[304,128]{1,0:T(8,128)S(1)}, u32[]{:S(2)}, u32[]{:S(2)}) collective-permute-start(f32[304,128]{1,0:T(8,128)} %get-tuple-element.163), channel_id=1, source_target_pairs={{0,17},{1,16},{2,19},{3,18},{4,21},{5,20},{6,23},{7,22},{8,25},{9,... | collective-permute-start | bytes 466952 | tf_op jit(solution)/shard_map/ppermute | solution.py:936
  273.3 5.4 %collective-permute-start.52 = (f32[8,128]{1,0:T(8,128)S(1)}, f32[8,128]{1,0:T(8,128)S(1)}, u32[]{:S(2)}, u32[]{:S(2)}) collective-permute-start(f32[8,128]{1,0:T(8,128)S(1)} %add_add_fusion.q0), channel_id=1, source_target_pairs={{0,6},{1,7},{2,4},{3,5},{4,2},{5,3},{6,0},{7,1},{8,14},{9,15},{10,... | collective-permute-start | bytes 12296 | tf_op jit(solution)/shard_map/ppermute | solution.py:936
  275.1 4.8 %collective-permute-start.51 = (f32[8,128]{1,0:T(8,128)S(1)}, f32[8,128]{1,0:T(8,128)S(1)}, u32[]{:S(2)}, u32[]{:S(2)}) collective-permute-start(f32[8,128]{1,0:T(8,128)S(1)} %add_add_fusion.q0), channel_id=1, source_target_pairs={{0,4},{1,5},{2,6},{3,7},{4,0},{5,1},{6,2},{7,3},{8,12},{9,13},{10,... | collective-permute-start | bytes 12296 | tf_op jit(solution)/shard_map/ppermute | solution.py:936
  (51 other events, 588.5 us)
Sparse Core Ops, SparseCore 0:
  16.3 72.2 all-gather.1
